TPU v7x, 32 devices: a whole 2x2x4 slice. The times are simulated.
32 devices in a mesh: dp: 16 (over z, y, core), expert: 2 (over x).
Axes of the slice: x: 2, y: 2, z: 4, core: 2. Of those that a mesh axis runs over, the one named last changes fastest.
Arguments:
- tokens: bfloat16 [2048, 2048], P(('dp', 'expert')), may hold values from -16 to 16
- cotangent: bfloat16 [2048, 2048], P(('dp', 'expert')), may hold values from -8 to 8
- route: int32 [4096], P(('dp', 'expert')), may hold values from 0 to 63, as said below
- counts: int32 [32, 2], P(('dp', 'expert')), may hold values from 32 to 64, as said below
- gate_master: float32 [2, 2048, 768], P('expert', 'dp'), may hold values from -0.125 to 0.125
- up_master: float32 [2, 2048, 768], P('expert', 'dp'), may hold values from -0.125 to 0.125
- down_master: float32 [2, 2048, 768], P('expert', 'dp'), may hold values from -0.21875 to 0.21875
- first_moment: float32 [2, 3, 2048, 768], P('expert', None, 'dp'), may hold values from -2 to 2
- second_moment: float32 [2, 3, 2048, 768], P('expert', None, 'dp'), may hold values from 0.01 to 1
Outputs:
- combined: float32 [2, 3, 2048, 768], P('expert', None, 'dp')
- new_weights: float32 [2, 3, 2048, 768], P('expert', None, 'dp')
- new_first: float32 [2, 3, 2048, 768], P('expert', None, 'dp')
- new_second: float32 [2, 3, 2048, 768], P('expert', None, 'dp')
- forward: bfloat16 [2048, 2048], P(('dp', 'expert'))
Inputs may be any that keep to these rules, and one draw needn't show every extreme that they name: `route`: for each device and each expert, the 64 slots name distinct local token rows. `counts`: in every draw, for some data index and some expert, every source device of that data index sends exactly 64 live slots.
All inputs are finite; a program needn't handle non-finite values.
Results may differ from a plain program's by a relative error of at most 0.011.
The roundings to bfloat16 on the way count: a program that leaves them out, or rounds other values in their place, can miss the bound.
Values may be sent and summed in bfloat16 or wider, within the bound.
No kernel may reach another device: no remote copies, remote signals or barrier semaphores. Data moves between devices by JAX's collectives and lax.ppermute only.
A program may use at most 128 MiB of HBM per device.

v0:
```python
import jax
import jax.numpy as jnp
from jax import lax
from jax.sharding import PartitionSpec as P

first_decay = 0.9
second_decay = 0.95
learn_rate = 0.01
adam_eps = 1e-08
weight_decay = 0.1
adam_count = 100.0
norm_eps = 1e-06
contract_rows = (((0,), (0,)), ((), ()))
contract_last = (((1,), (1,)), ((), ()))


def swapped(array, axis, apart):
    return lax.ppermute(array, axis, [(i, i ^ 1 << apart) for i in range(lax.axis_size(axis))])


def weight_grads(token_cols, grad_cols, d_gate, d_up, hidden_act):
    return jnp.stack(
        [
            lax.dot_general(token_cols, d_gate, contract_rows, preferred_element_type=jnp.float32),
            lax.dot_general(token_cols, d_up, contract_rows, preferred_element_type=jnp.float32),
            lax.dot_general(
                grad_cols, hidden_act, contract_rows, preferred_element_type=jnp.float32
            ),
        ]
    )


def half_columns(matrix, dp_parts, selected):
    shaped = matrix.reshape(matrix.shape[0], dp_parts // 2, 2, matrix.shape[1] // dp_parts)
    chosen = lax.dynamic_index_in_dim(shaped, selected, 2, keepdims=False)
    return chosen.reshape(matrix.shape[0], matrix.shape[1] // 2)


def group_sum(partial_value, level_index):
    total = partial_value
    for bit_index in range(level_index + 1):
        total = total + swapped(total, "dp", bit_index)
    return total


def combine_level(kept_half, received_half, own_bit, level_index):
    mine_wide = kept_half.astype(jnp.float32)
    theirs_wide = received_half.astype(jnp.float32)
    cross = jnp.sum(mine_wide * theirs_wide, axis=(1, 2, 3))
    own_square = jnp.sum(mine_wide * mine_wide, axis=(1, 2, 3))
    their_square = jnp.sum(theirs_wide * theirs_wide, axis=(1, 2, 3))
    is_lower = own_bit == 0
    lower_square = jnp.where(is_lower, own_square, their_square)
    upper_square = jnp.where(is_lower, their_square, own_square)
    totals = group_sum(jnp.stack([cross, lower_square, upper_square]), level_index)
    lower_coef = 1.0 - totals[0] / (2.0 * (totals[1] + norm_eps))
    upper_coef = 1.0 - totals[0] / (2.0 * (totals[2] + norm_eps))
    own_coef = jnp.where(is_lower, lower_coef, upper_coef)
    their_coef = jnp.where(is_lower, upper_coef, lower_coef)
    return own_coef[:, None, None, None] * mine_wide + their_coef[:, None, None, None] * theirs_wide


def shards(
    tokens,
    cotangent,
    route,
    counts,
    gate_master,
    up_master,
    down_master,
    first_moment,
    second_moment,
):
    experts = lax.axis_size("expert")
    dp_parts = lax.axis_size("dp")
    levels = dp_parts.bit_length() - 1
    my_index = lax.axis_index("dp")
    slot_count = route.shape[0]
    capacity = slot_count // experts
    slot_ids = jnp.arange(slot_count, dtype=jnp.int32)
    live_slots = slot_ids % capacity < jnp.repeat(counts[0], capacity)
    sent_tokens = jnp.where(live_slots[:, None], jnp.take(tokens, route, axis=0), 0)
    sent_grads = jnp.where(live_slots[:, None], jnp.take(cotangent, route, axis=0), 0)
    token_rows, grad_rows = (
        lax.all_to_all(sent_tokens, "expert", split_axis=0, concat_axis=0, tiled=True),
        lax.all_to_all(sent_grads, "expert", split_axis=0, concat_axis=0, tiled=True),
    )
    masters = jnp.stack([gate_master[0], up_master[0], down_master[0]])
    compute_weights = masters.astype(jnp.bfloat16)
    block_rows = masters.shape[1]
    hidden_width = masters.shape[2]
    full_weights = lax.all_gather(compute_weights, "dp", axis=1, tiled=True)
    gate_pre = jnp.dot(token_rows, full_weights[0], preferred_element_type=jnp.float32)
    up_pre = jnp.dot(token_rows, full_weights[1], preferred_element_type=jnp.float32)
    back_hidden = jnp.dot(grad_rows, full_weights[2], preferred_element_type=jnp.float32)
    sigmoid_gate = jax.nn.sigmoid(gate_pre)
    active_gate = gate_pre * sigmoid_gate
    hidden_act = (active_gate * up_pre).astype(jnp.bfloat16)
    d_gate = (back_hidden * up_pre * sigmoid_gate * (1.0 + gate_pre * (1.0 - sigmoid_gate))).astype(
        jnp.bfloat16
    )
    d_up = (back_hidden * active_gate).astype(jnp.bfloat16)
    low_bit = my_index & 1
    shape_half = (3, dp_parts // 2, block_rows, hidden_width)
    held_blocks = None
    give_tokens = half_columns(token_rows, dp_parts, 1 - low_bit)
    give_grads = half_columns(grad_rows, dp_parts, 1 - low_bit)
    got_tokens, got_grads, got_dgate, got_dup, got_hidden = swapped(
        (give_tokens, give_grads, d_gate, d_up, hidden_act), "dp", 0
    )
    part_grads = weight_grads(
        half_columns(token_rows, dp_parts, low_bit),
        half_columns(grad_rows, dp_parts, low_bit),
        d_gate,
        d_up,
        hidden_act,
    )
    own_part = part_grads.astype(jnp.bfloat16).reshape(shape_half)
    their_part = (
        weight_grads(got_tokens, got_grads, got_dgate, got_dup, got_hidden)
        .astype(jnp.bfloat16)
        .reshape(shape_half)
    )
    wide_blocks = combine_level(own_part, their_part, low_bit, 0)
    held_blocks = wide_blocks.astype(jnp.bfloat16)
    first_level = 1
    for level_index in range(first_level, levels):
        own_bit = my_index >> level_index & 1
        grouped = held_blocks.reshape(3, held_blocks.shape[1] // 2, 2, block_rows, hidden_width)
        kept_half = lax.dynamic_index_in_dim(grouped, own_bit, 2, keepdims=False)
        given_half = lax.dynamic_index_in_dim(grouped, 1 - own_bit, 2, keepdims=False)
        received_half = swapped(given_half, "dp", level_index)
        wide_blocks = combine_level(kept_half, received_half, own_bit, level_index)
        held_blocks = wide_blocks if level_index + 1 == levels else wide_blocks.astype(jnp.bfloat16)
    combined = held_blocks[:, 0]
    new_first = first_decay * first_moment[0] + (1.0 - first_decay) * combined
    new_second = second_decay * second_moment[0] + (1.0 - second_decay) * combined * combined
    first_hat = new_first / (1.0 - first_decay**adam_count)
    second_hat = new_second / (1.0 - second_decay**adam_count)
    new_masters = masters - learn_rate * (
        first_hat / (jnp.sqrt(second_hat) + adam_eps) + weight_decay * masters
    )
    new_down = new_masters[2].astype(jnp.bfloat16)
    full_down = lax.all_gather(new_down, "dp", axis=0, tiled=True)
    slot_outputs = lax.dot_general(
        hidden_act, full_down, contract_last, preferred_element_type=jnp.float32
    ).astype(jnp.bfloat16)
    returned = lax.all_to_all(slot_outputs, "expert", split_axis=0, concat_axis=0, tiled=True)
    pool_ids = jnp.arange(tokens.shape[0], dtype=jnp.int32)
    selector = ((route[None, :] == pool_ids[:, None]) & live_slots[None, :]).astype(jnp.bfloat16)
    forward = jnp.dot(selector, returned, preferred_element_type=jnp.float32).astype(jnp.bfloat16)
    return (combined[None], new_masters[None], new_first[None], new_second[None], forward)


def solution(mesh):
    in_specs = (
        P(("dp", "expert"), None),
        P(("dp", "expert"), None),
        P(("dp", "expert")),
        P(("dp", "expert"), None),
        P("expert", "dp", None),
        P("expert", "dp", None),
        P("expert", "dp", None),
        P("expert", None, "dp", None),
        P("expert", None, "dp", None),
    )
    out_specs = (
        P("expert", None, "dp", None),
        P("expert", None, "dp", None),
        P("expert", None, "dp", None),
        P("expert", None, "dp", None),
        P(("dp", "expert"), None),
    )
    return jax.shard_map(shards, mesh=mesh, in_specs=in_specs, out_specs=out_specs, check_vma=False)
```

profile of v0, /device:TPU:0, one launch (start us, length us, event | category | flops | bytes accessed | tf_op | source)
XLA Modules:
  0.0 340.4 jit_solution(12004289634935276718)
XLA Ops:
  14.5 12.0 %all_to_all.36 = bf16[2,64,2048]{2,1,0:T(8,128)(2,1)S(1)} all-to-all(bf16[2,64,2048]{2,1,0:T(8,128)(2,1)S(1)} %bitcast.142), channel_id=1, replica_groups=mesh['dp'=16,'expert'=2] {'expert'}, dimensions={0} | all-to-all | bytes 1048576 | tf_op jit(solution)/shard_map/all_to_all | solution.py:85
  26.4 3.5 %all-to-all-start.1 = ((bf16[2,64,2048]{2,1,0:T(8,128)(2,1)}), bf16[2,64,2048]{2,1,0:T(8,128)(2,1)S(1)}, u32[]{:S(2)}, u32[]{:S(2)}) async-start(bf16[2,64,2048]{2,1,0:T(8,128)(2,1)} %bitcast.3), calls=%async_computation.1 | async-start | bytes 1048576 | tf_op jit(solution)/shard_map/all_to_all | solution.py:86
  33.0 4.0 %all-to-all-done.1 = bf16[2,64,2048]{2,1,0:T(8,128)(2,1)S(1)} async-done(((bf16[2,64,2048]{2,1,0:T(8,128)(2,1)}), bf16[2,64,2048]{2,1,0:T(8,128)(2,1)S(1)}, u32[]{:S(2)}, u32[]{:S(2)}) %all-to-all-start.1) | async-done | bytes 524320 | tf_op jit(solution)/shard_map/all_to_all | solution.py:86
  39.4 56.2 %all-gather.4.cloned.1.call-done = bf16[3,2048,768]{2,1,0:T(8,128)(2,1)} async-done(((bf16[3,128,768]{2,1,0:T(8,128)(2,1)}), bf16[3,2048,768]{2,1,0:T(8,128)(2,1)}) %all-gather.4.cloned.1.call-update) | async-done | bytes 9437200 | tf_op jit(solution)/shard_map/all_gather | solution.py:92
  95.7 2.5 fusion.9
  98.2 2.5 fusion.10
  100.6 2.7 multiply_convert_fusion.2
  107.6 3.7 %fusion.1 = (f32[3]{0:T(128)S(1)}, f32[3]{0:T(128)S(1)}, f32[3]{0:T(128)S(1)}) fusion(bf16[1,8,128,768]{3,2,1,0:T(8,128)(2,1)S(1)} %bitcast.135, bf16[1,8,128,768]{3,2,1,0:T(8,128)(2,1)S(1)} %bitcast.133, bf16[1,8,128,768]{3,2,1,0:T(8,128)(2,1)S(1)} %bitcast.131, bf16[1,8,128,768]{3,2,1,0:T(8,128)(2,1)S(1)} %bitcast.129, ...), kind=kLoop, calls=%fused_computation.6 | loop fusion | flops 28311540 | bytes 9437220 | tf_op jit(solution)/shard_map/reduce_sum | solution.py:49
  118.4 53.1 %collective-permute-done.6 = bf16[3,4,128,768]{3,2,1,0:T(8,128)(2,1)S(1)} collective-permute-done((bf16[3,4,128,768]{3,2,1,0:T(8,128)(2,1)}, bf16[3,4,128,768]{3,2,1,0:T(8,128)(2,1)S(1)}, u32[]{:S(2)}, u32[]{:S(2)}) %collective-permute-start.6) | collective-permute-done | bytes 2359328 | tf_op jit(solution)/shard_map/ppermute | solution.py:18
  171.4 4.2 %fusion.6 = (f32[3]{0:T(128)S(1)}, f32[3]{0:T(128)S(1)}, f32[3]{0:T(128)S(1)}) fusion(bf16[3,4,128,768]{3,2,1,0:T(8,128)(2,1)S(1)} %collective-permute-done.6, bf16[3,4,2,128,768]{4,3,1,0,2:T(8,128)(2,1)} %copy-done.2, s32[]{:T(128)S(6)} %select_n.260), kind=kLoop, calls=%fused_computation.17 | loop fusion | flops 9437175 | bytes 4718632 | tf_op jit(solution)/shard_map/reduce_sum | solution.py:49
  177.5 3.0 collective-permute-done.8
  180.6 2.6 fusion.5
  184.9 26.6 %collective-permute-done.9 = bf16[3,2,128,768]{3,2,1,0:T(8,128)(2,1)} collective-permute-done((bf16[3,2,128,768]{3,2,1,0:T(8,128)(2,1)}, bf16[3,2,128,768]{3,2,1,0:T(8,128)(2,1)}, u32[]{:S(2)}, u32[]{:S(2)}) %collective-permute-start.9) | collective-permute-done | bytes 1179680 | tf_op jit(solution)/shard_map/ppermute | solution.py:18
  215.5 3.0 collective-permute-done.11
  219.2 3.0 collective-permute-done.12
  227.3 25.4 %collective-permute-done.13 = bf16[3,1,128,768]{3,2,1,0:T(8,128)(2,1)S(1)} collective-permute-done((bf16[3,1,128,768]{3,2,1,0:T(8,128)(2,1)}, bf16[3,1,128,768]{3,2,1,0:T(8,128)(2,1)S(1)}, u32[]{:S(2)}, u32[]{:S(2)}) %collective-permute-start.13) | collective-permute-done | bytes 589856 | tf_op jit(solution)/shard_map/ppermute | solution.py:18
  256.1 3.0 collective-permute-done.15
  259.3 3.6 %collective-permute-done.16 = f32[3,3]{1,0:T(4,128)S(1)} collective-permute-done((f32[3,3]{1,0:T(4,128)S(1)}, f32[3,3]{1,0:T(4,128)S(1)}, u32[]{:S(2)}, u32[]{:S(2)}) %collective-permute-start.16) | collective-permute-done | bytes 68 | tf_op jit(solution)/shard_map/ppermute | solution.py:18
  262.9 4.5 %collective-permute-done.17 = f32[3,3]{1,0:T(4,128)S(1)} collective-permute-done((f32[3,3]{1,0:T(4,128)S(1)}, f32[3,3]{1,0:T(4,128)S(1)}, u32[]{:S(2)}, u32[]{:S(2)}) %collective-permute-start.17) | collective-permute-done | bytes 68 | tf_op jit(solution)/shard_map/ppermute | solution.py:18
  271.4 43.4 %all-gather.6.cloned.1.call-done = bf16[1,2048,768]{2,1,0:T(8,128)(2,1)} async-done(((bf16[1,128,768]{2,1,0:T(8,128)(2,1)}), bf16[1,2048,768]{2,1,0:T(8,128)(2,1)}) %all-gather.6.cloned.1.call-update) | async-done | bytes 3145744 | tf_op jit(solution)/shard_map/all_gather | solution.py:144
  314.8 3.8 %fusion.13 = bf16[128,2048]{1,0:T(8,128)(2,1)} fusion(bf16[128,768]{1,0:T(8,128)(2,1)S(1)} %copy-done.11, bf16[1,2048,768]{2,1,0:T(8,128)(2,1)} %all-gather.6.cloned.1.call-done), kind=kOutput, calls=%fused_computation.36 | convolution fusion | flops 402915328 | bytes 3866624 | tf_op jit(solution)/shard_map/dot_general | solution.py:145
  318.7 4.2 %all-to-all-start.2 = ((bf16[2,64,2048]{2,1,0:T(8,128)(2,1)}), bf16[2,64,2048]{2,1,0:T(8,128)(2,1)}, u32[]{:S(2)}, u32[]{:S(2)}) async-start(bf16[2,64,2048]{2,1,0:T(8,128)(2,1)} %bitcast.143), calls=%async_computation.2 | async-start | bytes 1048576 | tf_op jit(solution)/shard_map/all_to_all | solution.py:148
  322.9 4.2 %multiply_subtract_fusion = (f32[1,3,128,768]{3,2,1,0:T(8,128)}, f32[1,3,128,768]{3,2,1,0:T(8,128)}, f32[1,3,128,768]{3,2,1,0:T(8,128)}, f32[1,3,128,768]{3,2,1,0:T(8,128)}) fusion(f32[1,1,128,768]{3,2,1,0:T(8,128)} %bitcast.144, f32[1,1,128,768]{3,2,1,0:T(8,128)} %bitcast.145, f32[1,1,128,768]{3,2,1,0:T(8,128)} %bitcast.146, ...), kind=kLoop, calls=%fused_computation.68 | loop fusion | flops 6488064 | bytes 9437212 | tf_op jit(solution)/shard_map/sub | solution.py:140
  327.1 4.5 %all-to-all-done.2 = bf16[2,64,2048]{2,1,0:T(8,128)(2,1)} async-done(((bf16[2,64,2048]{2,1,0:T(8,128)(2,1)}), bf16[2,64,2048]{2,1,0:T(8,128)(2,1)}, u32[]{:S(2)}, u32[]{:S(2)}) %all-to-all-start.2) | async-done | bytes 524320 | tf_op jit(solution)/shard_map/all_to_all | solution.py:148
  (121 shorter events, 46.7 us)
Async XLA Ops:
  7.2 88.5 %all-gather.4.cloned.1.call-start = ((), (), s32[]{:S(2)}) async-start(), calls=%async_computation.3 | async-start | bytes 10027008 | tf_op jit(solution)/shard_map/all_gather | solution.py:92
  26.4 10.5 %all-to-all-start.1 = ((bf16[2,64,2048]{2,1,0:T(8,128)(2,1)}), bf16[2,64,2048]{2,1,0:T(8,128)(2,1)S(1)}, u32[]{:S(2)}, u32[]{:S(2)}) async-start(bf16[2,64,2048]{2,1,0:T(8,128)(2,1)} %bitcast.3), calls=%async_computation.1 | async-start | bytes 1048576 | tf_op jit(solution)/shard_map/all_to_all | solution.py:86
  29.9 284.9 %all-gather.6.cloned.1.call-start = ((), (), s32[]{:S(2)}) async-start(), calls=%async_computation.4 | async-start | bytes 3342336 | tf_op jit(solution)/shard_map/all_gather | solution.py:144
  32.5 73.4 %collective-permute-start = (bf16[128,1024]{0,1:T(8,128)(2,1)}, bf16[128,1024]{0,1:T(8,128)(2,1)S(1)}, u32[]{:S(2)}, u32[]{:S(2)}) collective-permute-start(bf16[128,1024]{0,1:T(8,128)(2,1)} %bitcast.13), channel_id=1, source_target_pairs={{0,2},{2,0},{4,6},{6,4},{8,10},{10,8},{12,14},{14,12},{16,18},{18,... | collective-permute-start | bytes 786440 | tf_op jit(solution)/shard_map/ppermute | solution.py:18
  39.4 67.7 %collective-permute-start.3 = (bf16[128,1024]{0,1:T(8,128)(2,1)S(1)}, bf16[128,1024]{0,1:T(8,128)(2,1)S(1)}, u32[]{:S(2)}, u32[]{:S(2)}) collective-permute-start(bf16[128,1024]{0,1:T(8,128)(2,1)S(1)} %bitcast.148), channel_id=1, source_target_pairs={{0,2},{2,0},{4,6},{6,4},{8,10},{10,8},{12,14},{14,12},{16,18},{18,... | collective-permute-start | bytes 786440 | tf_op jit(solution)/shard_map/ppermute | solution.py:18
  103.3 2.6 collective-permute-start.1
  103.6 2.8 collective-permute-start.2
  105.0 2.0 collective-permute-start.4
  111.4 1.2 collective-permute-start.5
  117.8 53.6 %collective-permute-start.6 = (bf16[3,4,128,768]{3,2,1,0:T(8,128)(2,1)}, bf16[3,4,128,768]{3,2,1,0:T(8,128)(2,1)S(1)}, u32[]{:S(2)}, u32[]{:S(2)}) collective-permute-start(bf16[3,4,128,768]{3,2,1,0:T(8,128)(2,1)} %dynamic-slice_bitcast_fusion), channel_id=1, source_target_pairs={{0,4},{2,6},{4,0},{6,2},{8,12},{10,14},{12,8},{14,10},{16,20},{18,... | collective-permute-start | bytes 7077896 | tf_op jit(solution)/shard_map/ppermute | solution.py:18
  118.4 62.2 %copy-start.3 = (bf16[3,4,2,128,768]{4,3,1,0,2:T(8,128)(2,1)S(1)}, bf16[3,4,2,128,768]{4,3,1,0,2:T(8,128)(2,1)}, u32[]{:S(2)}) copy-start(bf16[3,4,2,128,768]{4,3,1,0,2:T(8,128)(2,1)} %copy-done.2) | copy-start | bytes 14155780
  175.6 1.2 collective-permute-start.7
  176.9 3.7 %collective-permute-start.8 = (f32[3,3]{1,0:T(4,128)S(1)}, f32[3,3]{1,0:T(4,128)S(1)}, u32[]{:S(2)}, u32[]{:S(2)}) collective-permute-start(f32[3,3]{1,0:T(4,128)S(1)} %fusion.68), channel_id=1, source_target_pairs={{0,4},{2,6},{4,0},{6,2},{8,12},{10,14},{12,8},{14,10},{16,20},{18,... | collective-permute-start | bytes 116 | tf_op jit(solution)/shard_map/ppermute | solution.py:18
  184.3 27.2 %collective-permute-start.9 = (bf16[3,2,128,768]{3,2,1,0:T(8,128)(2,1)}, bf16[3,2,128,768]{3,2,1,0:T(8,128)(2,1)}, u32[]{:S(2)}, u32[]{:S(2)}) collective-permute-start(bf16[3,2,128,768]{3,2,1,0:T(8,128)(2,1)} %dynamic-slice_bitcast_fusion.1), channel_id=1, source_target_pairs={{0,8},{2,10},{4,12},{6,14},{8,0},{10,2},{12,4},{14,6},{16,24},{18,... | collective-permute-start | bytes 3538952 | tf_op jit(solution)/shard_map/ppermute | solution.py:18
  213.6 1.2 collective-permute-start.10
  214.9 3.7 %collective-permute-start.11 = (f32[3,3]{1,0:T(4,128)S(1)}, f32[3,3]{1,0:T(4,128)S(1)}, u32[]{:S(2)}, u32[]{:S(2)}) collective-permute-start(f32[3,3]{1,0:T(4,128)S(1)} %fusion.67), channel_id=1, source_target_pairs={{0,4},{2,6},{4,0},{6,2},{8,12},{10,14},{12,8},{14,10},{16,20},{18,... | collective-permute-start | bytes 116 | tf_op jit(solution)/shard_map/ppermute | solution.py:18
  218.5 3.7 %collective-permute-start.12 = (f32[3,3]{1,0:T(4,128)S(1)}, f32[3,3]{1,0:T(4,128)S(1)}, u32[]{:S(2)}, u32[]{:S(2)}) collective-permute-start(f32[3,3]{1,0:T(4,128)S(1)} %fusion.98), channel_id=1, source_target_pairs={{0,8},{2,10},{4,12},{6,14},{8,0},{10,2},{12,4},{14,6},{16,24},{18,... | collective-permute-start | bytes 116 | tf_op jit(solution)/shard_map/ppermute | solution.py:18
  225.9 26.9 %collective-permute-start.13 = (bf16[3,1,128,768]{3,2,1,0:T(8,128)(2,1)}, bf16[3,1,128,768]{3,2,1,0:T(8,128)(2,1)S(1)}, u32[]{:S(2)}, u32[]{:S(2)}) collective-permute-start(bf16[3,1,128,768]{3,2,1,0:T(8,128)(2,1)} %constant_dynamic-slice_fusion), channel_id=1, source_target_pairs={{0,16},{2,18},{4,20},{6,22},{8,24},{10,26},{12,28},{14,30},{16,0},... | collective-permute-start | bytes 1769480 | tf_op jit(solution)/shard_map/ppermute | solution.py:18
  254.3 1.2 collective-permute-start.14
  255.5 3.7 %collective-permute-start.15 = (f32[3,3]{1,0:T(4,128)S(1)}, f32[3,3]{1,0:T(4,128)S(1)}, u32[]{:S(2)}, u32[]{:S(2)}) collective-permute-start(f32[3,3]{1,0:T(4,128)S(1)} %fusion.66), channel_id=1, source_target_pairs={{0,4},{2,6},{4,0},{6,2},{8,12},{10,14},{12,8},{14,10},{16,20},{18,... | collective-permute-start | bytes 116 | tf_op jit(solution)/shard_map/ppermute | solution.py:18
  259.2 3.7 %collective-permute-start.16 = (f32[3,3]{1,0:T(4,128)S(1)}, f32[3,3]{1,0:T(4,128)S(1)}, u32[]{:S(2)}, u32[]{:S(2)}) collective-permute-start(f32[3,3]{1,0:T(4,128)S(1)} %fusion.97), channel_id=1, source_target_pairs={{0,8},{2,10},{4,12},{6,14},{8,0},{10,2},{12,4},{14,6},{16,24},{18,... | collective-permute-start | bytes 116 | tf_op jit(solution)/shard_map/ppermute | solution.py:18
  262.9 4.5 %collective-permute-start.17 = (f32[3,3]{1,0:T(4,128)S(1)}, f32[3,3]{1,0:T(4,128)S(1)}, u32[]{:S(2)}, u32[]{:S(2)}) collective-permute-start(f32[3,3]{1,0:T(4,128)S(1)} %add.250), channel_id=1, source_target_pairs={{0,16},{2,18},{4,20},{6,22},{8,24},{10,26},{12,28},{14,30},{16,0},... | collective-permute-start | bytes 116 | tf_op jit(solution)/shard_map/ppermute | solution.py:18
  269.5 45.3 %copy-start.11 = (bf16[128,768]{1,0:T(8,128)(2,1)S(1)}, bf16[128,768]{1,0:T(8,128)(2,1)}, u32[]{:S(2)}) copy-start(bf16[128,768]{1,0:T(8,128)(2,1)} %copy-done.10) | copy-start | bytes 589828
  318.7 13.0 %all-to-all-start.2 = ((bf16[2,64,2048]{2,1,0:T(8,128)(2,1)}), bf16[2,64,2048]{2,1,0:T(8,128)(2,1)}, u32[]{:S(2)}, u32[]{:S(2)}) async-start(bf16[2,64,2048]{2,1,0:T(8,128)(2,1)} %bitcast.143), calls=%async_computation.2 | async-start | bytes 1048576 | tf_op jit(solution)/shard_map/all_to_all | solution.py:148
  (12 other events, 106.5 us)
Sparse Core Ops, SparseCore 0:
  11.5 84.1 all-gather.3
  271.5 43.2 all-gather.5
where the time goes:
time: 341 us; the launch traced here: 340 us
  waiting for transfers between devices  238 us (70%)
  other arithmetic  28.6 us (8%)
  matrix products  16.7 us (5%)
  local copies, waits for them, and re-layouts  16.4 us (5%)
  starting transfers between devices  14.5 us (4%)
  between operations  14.5 us (4%)
  blocking collectives  12 us (4%)
    ppermute x18, waiting for transfers between devices, swapped(): lax.ppermute(array, axis, [(i, i ^ 1 << apart) for i in range(lax.axis_si...  130 us
    all_gather x1, waiting for transfers between devices, shards(): full_weights = lax.all_gather(compute_weights, 'dp', axis=1, tiled=True)  56.2 us
    all_gather x1, waiting for transfers between devices, shards(): full_down = lax.all_gather(new_down, 'dp', axis=0, tiled=True)  43.4 us
    all_to_all x1, blocking collectives, shards(): lax.all_to_all(sent_tokens, 'expert', split_axis=0, concat_axis=0, tiled=...  12 us
    reduce_sum x4, other arithmetic, combine_level(): cross = jnp.sum(mine_wide * theirs_wide, axis=(1, 2, 3))  11.6 us
  transfers between devices with their start and end apart: 22, of which 17 were waited for; matrix products, arithmetic and copies ran while one was open for 7% of the time, Pallas kernels for 0%

commit v1 on v0

v1 whole, which is shorter than its diff:
```python
import functools

import jax
import jax.numpy as jnp
from jax import lax
from jax.experimental import pallas as pl
from jax.experimental.pallas import tpu as pltpu
from jax.sharding import PartitionSpec as P

first_decay = 0.9
second_decay = 0.95
learn_rate = 0.01
adam_eps = 1e-08
weight_decay = 0.1
adam_count = 100.0
norm_eps = 1e-06
gathered_limit = 16
mask_lanes = 128
vmem_bytes = 56 * 1024 * 1024
f32 = jnp.float32
bf16 = jnp.bfloat16
any_space = pl.BlockSpec(memory_space=pl.ANY)
smem_space = pl.BlockSpec(memory_space=pltpu.SMEM)
vmem_space = pl.BlockSpec(memory_space=pltpu.VMEM)
params = pltpu.CompilerParams(vmem_limit_bytes=vmem_bytes)


def swapped(array, axis, bit):
    return lax.ppermute(array, axis, [(i, i ^ 1 << bit) for i in range(lax.axis_size(axis))])


def bits_of(size):
    return size.bit_length() - 1


def cube_gather(array, steps):
    pieces = {(0, 0): array}
    for axis, bit in steps:
        for (e, k), piece in list(pieces.items()):
            key = (e ^ (1 << bit), k) if axis == "expert" else (e, k ^ (1 << bit))
            pieces[key] = swapped(piece, axis, bit)
    return pieces


def tree_sum(value, bits):
    for bit in range(bits):
        value = value + swapped(value, "dp", bit)
    return value


def nt(a, b):
    return lax.dot_general(a, b, (((1,), (1,)), ((), ())), preferred_element_type=f32)


def tn(a, b):
    return lax.dot_general(a, b, (((0,), (0,)), ((), ())), preferred_element_type=f32)


def tree_weights(entry, count):
    gram = {(i, j): entry(i, j) for i in range(count) for j in range(i, count)}
    weights = [None] * count
    size = count
    while size > 1:
        scale = []
        for j in range(0, size, 2):
            cross = gram[j, j + 1]
            scale.append(1.0 - cross / (2.0 * (gram[j, j] + norm_eps)))
            scale.append(1.0 - cross / (2.0 * (gram[j + 1, j + 1] + norm_eps)))
        span = count // size
        for leaf in range(count):
            factor = scale[leaf // span]
            weights[leaf] = factor if weights[leaf] is None else weights[leaf] * factor
        full = lambda i, j: gram[min(i, j), max(i, j)] * (scale[i] * scale[j])
        size //= 2
        if size > 1:
            gram = {
                (i, j): full(2 * i, 2 * j)
                + full(2 * i, 2 * j + 1)
                + full(2 * i + 1, 2 * j)
                + full(2 * i + 1, 2 * j + 1)
                for i in range(size)
                for j in range(i, size)
            }
    return weights


def prepare_kernel(route_ref, counts_ref, cot_ref, gate_ref, up_ref, down_ref, sent_ref, ext_ref):
    group, mats = sent_ref.shape[0], 3
    part = sent_ref.shape[1] // mats
    pool, width = cot_ref.shape
    experts, capacity = route_ref.shape
    for index, ref in enumerate((gate_ref, up_ref, down_ref)):
        turned = ref[...].T.astype(bf16)
        for k in range(group):
            sent_ref[k, index * part : (index + 1) * part, :] = turned[k * part : (k + 1) * part, :]
    ext_ref[:, :width] = cot_ref[...]
    ids = lax.broadcasted_iota(jnp.int32, (pool, capacity), 0)
    slots = lax.broadcasted_iota(jnp.int32, (pool, capacity), 1)
    lanes = lax.broadcasted_iota(jnp.int32, (pool, mask_lanes), 1)
    flags = jnp.zeros((pool, mask_lanes), f32)
    for e in range(experts):
        named = (ids == route_ref[e : e + 1, :]) & (slots < counts_ref[0, e])
        found = jnp.sum(named.astype(f32), axis=1, keepdims=True)
        flags = jnp.where(lanes == e, found, flags)
    ext_ref[:, width:] = flags.astype(bf16)


def gather_kernel(group, experts, idx_ref, *refs):
    count = group * experts
    tok, cot = refs[:count], refs[count : 2 * count]
    held = refs[2 * count : -11]
    hid_ref, dgate_ref, dup_ref, gram_ref, x_out, y_out = refs[-11:-5]
    x_ref, y_ref, w_ref, sems, out_sems = refs[-5:]
    slot, expert, outer_index = idx_ref[0], idx_ref[1], idx_ref[2]
    pool = tok[0].shape[0]
    rows = experts * pool
    part, total = hid_ref.shape
    width = x_ref.shape[1]
    loads = []
    for which, (pieces, into) in enumerate(((tok, x_ref), (cot, y_ref))):
        made = []
        for e in range(experts):
            for k in range(group):
                n = e * group + k
                at = ((slot ^ k) * experts + (expert ^ e)) * pool
                made.append(
                    pltpu.make_async_copy(
                        pieces[n], into.at[pl.ds(pl.multiple_of(at, pool), pool), :], sems.at[which, n]
                    )
                )
        for copy in made:
            copy.start()
        loads.append(made)
    per = held[0].shape[0]
    outer = per * len(held)
    block_rows = held[0].shape[3]
    for o in range(outer):
        for h, ref in enumerate(held):
            @pl.when(((outer_index ^ o) // per) == h)
            def _(ref=ref, o=o):
                source = ref.at[(outer_index ^ o) % per]
                for b in range(group):
                    at = (o * group + b) * block_rows
                    w_ref[:, at : at + block_rows] = source[b]
    for copy in loads[0]:
        copy.wait()
    x_save = pltpu.make_async_copy(x_ref, x_out, out_sems.at[0])
    x_save.start()
    pre = nt(w_ref[: 2 * part, :], x_ref[...])
    for copy in loads[1]:
        copy.wait()
    y_save = pltpu.make_async_copy(y_ref, y_out, out_sems.at[1])
    y_save.start()
    back_hidden = nt(w_ref[2 * part :, :], y_ref[:, :width])
    pick = lax.broadcasted_iota(jnp.int32, (8, mask_lanes), 1) == expert
    mask = nt(pick.astype(bf16), y_ref[:, width:])[0:1] > 0.5
    gate_pre, up_pre = pre[:part], pre[part:]
    sigmoid_gate = jax.nn.sigmoid(gate_pre)
    active_gate = gate_pre * sigmoid_gate
    kept = lambda value: jnp.where(mask, value, 0.0).astype(bf16)
    hid_ref[...] = kept(active_gate * up_pre)
    dgate_ref[...] = kept(
        back_hidden * up_pre * sigmoid_gate * (1.0 + gate_pre * (1.0 - sigmoid_gate))
    )
    dup_ref[...] = kept(back_hidden * active_gate)
    shape = gram_ref.shape
    row_ids = lax.broadcasted_iota(jnp.int32, shape, 0)
    lane_ids = lax.broadcasted_iota(jnp.int32, shape, 1)
    gram = jnp.zeros(shape, f32)
    for a in range(group):
        low = a * rows
        mine = slice(low, low + rows)
        outer_x = nt(x_ref[mine, :], x_ref[low:, :])
        outer_y = nt(y_ref[mine, :width], y_ref[low:, :width])
        for m, (ref, prod) in enumerate(
            ((dgate_ref, outer_x), (dup_ref, outer_x), (hid_ref, outer_y))
        ):
            both = prod * tn(ref[:, mine], ref[:, low:])
            for b in range(a, group):
                value = jnp.sum(both[:, (b - a) * rows : (b - a + 1) * rows], keepdims=True)
                gram = jnp.where((row_ids == m * group + a) & (lane_ids == b), value, gram)
    gram_ref[...] = gram
    x_save.wait()
    y_save.wait()


def vector_kernel(group, mats, gram_ref, in_ref, *refs):
    factors, out_ref = refs[:-1], refs[-1]
    part, total = factors[0].shape
    rows = total // group
    count, _, block_rows = out_ref.shape
    width = count * block_rows
    scaled = []
    for m, ref in zip(mats, factors):
        entry = lambda i, j: jnp.full((1, rows), gram_ref[m * group + i, j], f32)
        weights = tree_weights(entry, group)
        scaled.append(
            jnp.concatenate(
                [
                    (ref[:, d * rows : (d + 1) * rows].astype(f32) * weights[d]).astype(bf16)
                    for d in range(group)
                ],
                axis=1,
            )
        )
    left = jnp.concatenate(scaled, axis=0)
    vector = jnp.dot(left, in_ref[:, :width], preferred_element_type=f32).astype(bf16)
    for i in range(count):
        out_ref[i] = vector[:, i * block_rows : (i + 1) * block_rows]


def call(kernel, outs, args, in_specs, scratch=(), out_specs=None, aliases=None, name=None):
    return pl.pallas_call(
        kernel,
        out_shape=outs,
        in_specs=in_specs,
        out_specs=out_specs if out_specs is not None else jax.tree.map(lambda _: vmem_space, outs),
        scratch_shapes=list(scratch),
        compiler_params=params,
        input_output_aliases=aliases or {},
        name=name,
    )(*args)


def coefficients(gram):
    mats, count = gram.shape[0], gram.shape[1]
    weights = jnp.ones((mats, count), f32)
    while gram.shape[1] > 1:
        pairs = gram.shape[1] // 2
        blocks = gram.reshape(mats, pairs, 2, pairs, 2)
        diag = jnp.stack([blocks[:, j, :, j, :] for j in range(pairs)], axis=1)
        cross = diag[:, :, 0, 1]
        lower = 1.0 - cross / (2.0 * (diag[:, :, 0, 0] + norm_eps))
        upper = 1.0 - cross / (2.0 * (diag[:, :, 1, 1] + norm_eps))
        scale = jnp.stack([lower, upper], axis=2).reshape(mats, 2 * pairs)
        weights = weights * jnp.repeat(scale, count // (2 * pairs), axis=1)
        gram = gram * scale[:, :, None] * scale[:, None, :]
        gram = gram.reshape(mats, pairs, 2, pairs, 2).sum((2, 4))
    return weights


def shards(
    tokens,
    cotangent,
    route,
    counts,
    gate_master,
    up_master,
    down_master,
    first_moment,
    second_moment,
):
    experts = lax.axis_size("expert")
    dp = lax.axis_size("dp")
    group = max(1, min(gathered_limit // experts, dp))
    inner_bits = bits_of(group)
    outer_bits = bits_of(dp // group)
    outer = dp // group
    pool, width = tokens.shape
    rows = experts * pool
    block_rows, hidden_width = gate_master.shape[1:]
    part = hidden_width // group
    my_dp = lax.axis_index("dp")
    slot_index = my_dp % group
    outer_index = my_dp // group
    expert_index = lax.axis_index("expert")
    groups = [[o * group + s for s in range(group)] for o in range(outer)]
    capacity = route.shape[0] // experts

    my_ids = jnp.stack([slot_index, expert_index, outer_index]).astype(jnp.int32)
    sds = jax.ShapeDtypeStruct
    sent, grads_ext = call(
        prepare_kernel,
        (sds((group, 3 * part, block_rows), bf16), sds((pool, width + mask_lanes), bf16)),
        (route.reshape(experts, capacity), counts, cotangent, gate_master[0], up_master[0], down_master[0]),
        [vmem_space, smem_space] + [vmem_space] * 4,
        name="prepare",
    )
    own_group = lax.all_to_all(sent, "dp", 0, 0, axis_index_groups=groups, tiled=True)
    held = [own_group[None]]
    for bit in range(outer_bits):
        held = [jnp.concatenate(held)] if len(held) > 1 else held
        held = [held[0], swapped(held[0], "dp", inner_bits + bit)]
    dp_steps = [("dp", b) for b in reversed(range(inner_bits))]
    ex_steps = [("expert", b) for b in range(bits_of(experts))]
    core_step = dp_steps[-1:]
    steps_t = dp_steps[:-1] + ex_steps + core_step
    steps_c = dp_steps[:-1][:1] + ex_steps + dp_steps[:-1][1:] + core_step
    keys = [(e, k) for e in range(experts) for k in range(group)]
    token_pieces = cube_gather(tokens, steps_t)
    grad_pieces = cube_gather(grads_ext, steps_c)
    total = group * rows
    factor = sds((part, total), bf16)
    hidden, d_gate, d_up, gram, token_all, grad_all = call(
        functools.partial(gather_kernel, group, experts),
        (
            factor,
            factor,
            factor,
            sds((-(-3 * group // 8) * 8, 128), f32),
            sds((total, width), bf16),
            sds((total, width + mask_lanes), bf16),
        ),
        (my_ids, *[token_pieces[k] for k in keys], *[grad_pieces[k] for k in keys], *held),
        [smem_space] + [any_space] * (2 * len(keys)) + [vmem_space] * len(held),
        scratch=(
            pltpu.VMEM((total, width), bf16),
            pltpu.VMEM((total, width + mask_lanes), bf16),
            pltpu.VMEM((3 * part, width), bf16),
            pltpu.SemaphoreType.DMA((2, len(keys))),
            pltpu.SemaphoreType.DMA((2,)),
        ),
        out_specs=(vmem_space,) * 4 + (any_space,) * 2,
        name="forward_and_gram",
    )
    gram = tree_sum(gram, inner_bits)

    def local_tree(left, mats, factors):
        vector = call(
            functools.partial(vector_kernel, group, mats),
            sds((dp, len(mats) * part, block_rows), bf16),
            (gram, left, *factors),
            [smem_space] + [vmem_space] * (1 + len(factors)),
            name="local_tree",
        )
        got = lax.all_to_all(vector, "dp", 0, 0, tiled=True)
        got = got.reshape(outer, group, len(mats), part, block_rows).transpose(2, 0, 1, 3, 4)
        got = got.reshape(len(mats), outer, hidden_width, block_rows).astype(f32)
        if outer > 2:
            last = jnp.einsum("miab,mjab->mij", got, got, precision=lax.Precision.HIGHEST)
        else:
            last = (got[:, :, None] * got[:, None]).sum((3, 4))
        coef = coefficients(tree_sum(last, inner_bits + outer_bits))
        total = (coef[:, :, None, None] * got).sum(1)
        return total.transpose(0, 2, 1)

    masters = jnp.stack([gate_master[0], up_master[0], down_master[0]])
    down_sum = local_tree(grad_all, (2,), [hidden])
    pair_sum = local_tree(token_all, (0, 1), [d_gate, d_up])

    def adam(total, pick):
        first = first_decay * first_moment[0, pick] + (1.0 - first_decay) * total
        second = second_decay * second_moment[0, pick] + (1.0 - second_decay) * total * total
        first_hat = first / (1.0 - first_decay**adam_count)
        second_hat = second / (1.0 - second_decay**adam_count)
        old = masters[pick]
        new = old - learn_rate * (first_hat / (jnp.sqrt(second_hat) + adam_eps) + weight_decay * old)
        return total, new, first, second

    down_out = adam(down_sum, slice(2, 3))
    pair_out = adam(pair_sum, slice(0, 2))
    combined, new_masters, new_first, new_second = (
        jnp.concatenate([a, b])[None] for a, b in zip(pair_out, down_out)
    )

    new_down = down_out[1][0].astype(bf16)[None]
    for bit in range(outer_bits):
        other = swapped(new_down, "dp", inner_bits + bit)
        is_lower = (outer_index >> bit) & 1 == 0
        new_down = jnp.concatenate(
            [jnp.where(is_lower, new_down, other), jnp.where(is_lower, other, new_down)]
        )
    new_down = new_down.reshape(outer * block_rows, hidden_width)
    hidden_all = lax.all_gather(hidden, "dp", axis=0, axis_index_groups=groups, tiled=True)
    slot_outputs = lax.dot_general(
        hidden_all, new_down, (((0,), (1,)), ((), ())), preferred_element_type=f32
    ).astype(bf16)
    slot_outputs = slot_outputs.reshape(group, experts, pool, outer * block_rows)
    returned = lax.all_to_all(slot_outputs, "expert", 1, 1, tiled=True)
    summed = returned.astype(f32).sum(1).astype(bf16)
    columns = lax.all_to_all(summed, "dp", 0, 0, axis_index_groups=groups, tiled=True)
    columns = columns.reshape(group, pool, outer, block_rows).transpose(1, 2, 0, 3)
    forward = columns.reshape(pool, width)
    return (combined, new_masters, new_first, new_second, forward)


def solution(mesh):
    in_specs = (
        P(("dp", "expert"), None),
        P(("dp", "expert"), None),
        P(("dp", "expert")),
        P(("dp", "expert"), None),
        P("expert", "dp", None),
        P("expert", "dp", None),
        P("expert", "dp", None),
        P("expert", None, "dp", None),
        P("expert", None, "dp", None),
    )
    out_specs = (
        P("expert", None, "dp", None),
        P("expert", None, "dp", None),
        P("expert", None, "dp", None),
        P("expert", None, "dp", None),
        P(("dp", "expert"), None),
    )
    return jax.shard_map(shards, mesh=mesh, in_specs=in_specs, out_specs=out_specs, check_vma=False)
```

time: 341 us -> 239 us (0.70)
  waiting for transfers between devices: 238 us -> 97.5 us
  starting transfers between devices: 14.5 us -> 55.8 us
  Pallas kernels: 0 us -> 33.5 us
  other arithmetic: 28.6 us -> 12.6 us
  matrix products: 16.7 us -> 2.09 us
  blocking collectives: 12 us -> 0 us
    all_gather x2 -> x1, waiting for transfers between devices: 99.7 us -> 0.01 us  [shards(): lax.all_gather(hidden, 'dp', axis=0, axis_index_groups=groups, tiled=True)]
    ppermute x18 -> x43, waiting for transfers between devices: 130 us -> 84.8 us  [swapped(): lax.ppermute(array, axis, [(i, i ^ 1 << bit) for i in range(lax.axis_size...]
    pallas_call x0 -> x4, Pallas kernels: none -> 33.5 us  [call(): pl.pallas_call(kernel, out_shape=outs, in_specs=in_specs, out_specs=out_s...]
    ppermute x18 -> x43, starting transfers between devices: 6.69 us -> 34.9 us  [swapped(): lax.ppermute(array, axis, [(i, i ^ 1 << bit) for i in range(lax.axis_size...]
    dot_general x11 -> x1, matrix products: 16.7 us -> 2.09 us  [shards(): lax.dot_general(hidden_all, new_down, (((0,), (1,)), ((), ())), preferred...]
    all_to_all x2 -> x5, starting transfers between devices: 7.7 us -> 20.5 us  [the longest x2 8.61 us: local_tree(): got = lax.all_to_all(vector, 'dp', 0, 0, tiled=True)]
    all_to_all x1 -> x0, blocking collectives: 12 us -> none  [shards(): lax.all_to_all(sent_tokens, 'expert', split_axis=0, concat_axis=0, tiled=...]
    reduce_sum x4 -> x5, other arithmetic: 11.6 us -> 2.85 us  [the longest x1 1.9 us: shards(): summed = returned.astype(f32).sum(1).astype(bf16)]
  transfers between devices with their start and end apart: 22 -> 49, of which waited for: 17 -> 23; matrix products, arithmetic and copies ran while one was open for 7% -> 9% of each run, Pallas kernels for 0% -> 3%
where the time goes in v1:
time: 239 us; the launch traced here: 238 us
  waiting for transfers between devices  97.5 us (41%)
  starting transfers between devices  55.8 us (23%)
  Pallas kernels  33.5 us (14%)
  local copies, waits for them, and re-layouts  19.2 us (8%)
  between operations  17.1 us (7%)
  other arithmetic  12.6 us (5%)
    ppermute x43, waiting for transfers between devices, swapped(): lax.ppermute(array, axis, [(i, i ^ 1 << bit) for i in range(lax.axis_size...  84.8 us
    ppermute x43, starting transfers between devices, swapped(): lax.ppermute(array, axis, [(i, i ^ 1 << bit) for i in range(lax.axis_size...  34.9 us
    pallas_call x4, Pallas kernels, call(): pl.pallas_call(kernel, out_shape=outs, in_specs=in_specs, out_specs=out_s...  33.5 us
    unnamed x64, local copies, waits for them, and re-layouts  13 us
    all_to_all x2, starting transfers between devices, local_tree(): got = lax.all_to_all(vector, 'dp', 0, 0, tiled=True)  8.61 us
    all_to_all x1, waiting for transfers between devices, shards(): returned = lax.all_to_all(slot_outputs, 'expert', 1, 1, tiled=True)  6.32 us
    all_to_all x2, waiting for transfers between devices, local_tree(): got = lax.all_to_all(vector, 'dp', 0, 0, tiled=True)  5.86 us
  transfers between devices with their start and end apart: 49, of which 23 were waited for; matrix products, arithmetic and copies ran while one was open for 9% of the time, Pallas kernels for 3%

profile of v1, /device:TPU:0, one launch (start us, length us, event | category | flops | bytes accessed | tf_op | source)
XLA Modules:
  0.0 237.8 jit_solution(16404223662119657442)
XLA Ops:
  7.2 3.1 %collective-permute-start.3 = (bf16[64,2048]{1,0:T(8,128)(2,1)}, bf16[64,2048]{1,0:T(8,128)(2,1)S(1)}, u32[]{:S(2)}, u32[]{:S(2)}) collective-permute-start(bf16[64,2048]{1,0:T(8,128)(2,1)} %refs_0_.1), channel_id=1, source_target_pairs={{0,8},{2,10},{4,12},{6,14},{8,0},{10,2},{12,4},{14,6},{16,24},{18,... | collective-permute-start | bytes 786440 | tf_op jit(solution)/shard_map/ppermute | solution.py:29
  20.3 3.7 %all-to-all-start = ((bf16[8,288,128]{2,1,0:T(8,128)(2,1)}), bf16[8,288,128]{2,1,0:T(8,128)(2,1)S(1)}, u32[]{:S(2)}, u32[]{:S(2)}) async-start(bf16[8,288,128]{2,1,0:T(8,128)(2,1)} %get-tuple-element.14), calls=%async_computation | async-start | bytes 1179648 | tf_op jit(solution)/shard_map/all_to_all | solution.py:279
  28.8 10.4 %collective-permute-done.5.refs_6_ = bf16[64,2048]{1,0:T(8,128)(2,1)} collective-permute-done((bf16[64,2048]{1,0:T(8,128)(2,1)S(1)}, bf16[64,2048]{1,0:T(8,128)(2,1)}, u32[]{:S(2)}, u32[]{:S(2)}) %collective-permute-start.5) | collective-permute-done | bytes 262176 | tf_op jit(solution)/shard_map/ppermute | solution.py:29
  43.3 4.1 %collective-permute-done.26.refs_28_ = bf16[64,2176]{1,0:T(8,128)(2,1)S(1)} collective-permute-done((bf16[64,2176]{1,0:T(8,128)(2,1)S(1)}, bf16[64,2176]{1,0:T(8,128)(2,1)S(1)}, u32[]{:S(2)}, u32[]{:S(2)}) %collective-permute-start.26) | collective-permute-done | bytes 278560 | tf_op jit(solution)/shard_map/ppermute | solution.py:29
  50.8 4.9 %collective-permute-done.24.refs_26_ = bf16[64,2176]{1,0:T(8,128)(2,1)S(1)} collective-permute-done((bf16[64,2176]{1,0:T(8,128)(2,1)S(1)}, bf16[64,2176]{1,0:T(8,128)(2,1)S(1)}, u32[]{:S(2)}, u32[]{:S(2)}) %collective-permute-start.24) | collective-permute-done | bytes 278560 | tf_op jit(solution)/shard_map/ppermute | solution.py:29
  61.2 6.1 %collective-permute-done.28.refs_30_ = bf16[64,2176]{1,0:T(8,128)(2,1)} collective-permute-done((bf16[64,2176]{1,0:T(8,128)(2,1)S(1)}, bf16[64,2176]{1,0:T(8,128)(2,1)}, u32[]{:S(2)}, u32[]{:S(2)}) %collective-permute-start.28) | collective-permute-done | bytes 278560 | tf_op jit(solution)/shard_map/ppermute | solution.py:29
  70.0 15.1 %collective-permute-done.30.refs_33_ = bf16[1,8,288,128]{3,2,1,0:T(8,128)(2,1)S(1)} collective-permute-done((bf16[1,8,288,128]{3,2,1,0:T(8,128)(2,1)S(1)}, bf16[1,8,288,128]{3,2,1,0:T(8,128)(2,1)S(1)}, u32[]{:S(2)}, u32[]{:S(2)}) %collective-permute-start.30) | collective-permute-done | bytes 589856 | tf_op jit(solution)/shard_map/ppermute | solution.py:29
  86.0 23.0 %forward_and_gram.1 = (bf16[96,1024]{1,0:T(8,128)(2,1)}, bf16[96,1024]{1,0:T(8,128)(2,1)}, bf16[96,1024]{1,0:T(8,128)(2,1)}, f32[24,128]{1,0:T(8,128)}, bf16[102...) custom-call(s32[3]{0:T(128)} %pad_add_fusion.idx_ref, bf16[64,2048]{1,0:T(8,128)(2,1)} %refs_0_.1, ...), custom_call_target="tpu_custom_call" | custom-call | tf_op jit(solution)/shard_map/forward_and_gram/pallas_call | solution.py:213
  111.6 3.2 %collective-permute-done.32 = f32[24,128]{1,0:T(8,128)S(1)} collective-permute-done((f32[24,128]{1,0:T(8,128)S(1)}, f32[24,128]{1,0:T(8,128)S(1)}, u32[]{:S(2)}, u32[]{:S(2)}) %collective-permute-start.32) | collective-permute-done | bytes 12320 | tf_op jit(solution)/shard_map/ppermute | solution.py:29
  115.5 3.0 %collective-permute-done.33 = f32[24,128]{1,0:T(8,128)S(1)} collective-permute-done((f32[24,128]{1,0:T(8,128)S(1)}, f32[24,128]{1,0:T(8,128)S(1)}, u32[]{:S(2)}, u32[]{:S(2)}) %collective-permute-start.33) | collective-permute-done | bytes 12320 | tf_op jit(solution)/shard_map/ppermute | solution.py:29
  119.1 3.8 %local_tree.3 = bf16[16,96,128]{2,1,0:T(8,128)(2,1)} custom-call(f32[24,128]{1,0:T(8,128)} %add.105.gram_ref, bf16[1024,2176]{1,0:T(8,128)(2,1)} %get-tuple-element.19.in_ref, bf16[96,1024]{1,0:T(8,128)(2,1)} %get-tuple-element.20.refs_0_), custom_call_target="tpu_custom_call" | custom-call | tf_op jit(solution)/shard_map/local_tree/pallas_call | solution.py:213
  123.0 5.0 %all-to-all-start.2 = ((bf16[16,96,128]{2,1,0:T(8,128)(2,1)}), bf16[16,96,128]{2,1,0:T(8,128)(2,1)S(1)}, u32[]{:S(2)}, u32[]{:S(2)}) async-start(bf16[16,96,128]{2,1,0:T(8,128)(2,1)} %local_tree.3), calls=%async_computation.2 | async-start | bytes 786432 | tf_op jit(solution)/shard_map/all_to_all | solution.py:326
  130.0 4.3 %local_tree.2 = bf16[16,192,128]{2,1,0:T(8,128)(2,1)} custom-call(f32[24,128]{1,0:T(8,128)} %add.105.gram_ref, bf16[1024,2048]{1,0:T(8,128)(2,1)} %get-tuple-element.16.in_ref, bf16[96,1024]{1,0:T(8,128)(2,1)} %get-tuple-element.17.refs_0_, bf16[96,1024]{1,0:T(8,128)(2,1)} %get-tuple-element.18.refs_1_), custom_call_target="tpu_custom_call" | custom-call | tf_op jit(solution)/shard_map/local_tree/pallas_call | solution.py:213
  134.3 5.9 %all-to-all-done.2 = bf16[16,96,128]{2,1,0:T(8,128)(2,1)S(1)} async-done(((bf16[16,96,128]{2,1,0:T(8,128)(2,1)}), bf16[16,96,128]{2,1,0:T(8,128)(2,1)S(1)}, u32[]{:S(2)}, u32[]{:S(2)}) %all-to-all-start.2) | async-done | bytes 393248 | tf_op jit(solution)/shard_map/all_to_all | solution.py:326
  140.2 3.6 %all-to-all-start.1 = ((bf16[16,192,128]{2,1,0:T(8,128)(2,1)}), bf16[16,192,128]{2,1,0:T(8,128)(2,1)S(1)}, u32[]{:S(2)}, u32[]{:S(2)}) async-start(bf16[16,192,128]{2,1,0:T(8,128)(2,1)} %local_tree.2), calls=%async_computation.1 | async-start | bytes 1572864 | tf_op jit(solution)/shard_map/all_to_all | solution.py:326
  147.1 5.8 %collective-permute-done.39 = f32[1,2,2]{2,1,0:T(2,128)S(1)} collective-permute-done((f32[1,2,2]{2,1,0:T(2,128)S(1)}, f32[1,2,2]{2,1,0:T(2,128)S(1)}, u32[]{:S(2)}, u32[]{:S(2)}) %collective-permute-start.39) | collective-permute-done | bytes 48 | tf_op jit(solution)/shard_map/ppermute | solution.py:29
  152.9 7.5 %collective-permute-done.40 = f32[1,2,2]{2,1,0:T(2,128)S(1)} collective-permute-done((f32[1,2,2]{2,1,0:T(2,128)S(1)}, f32[1,2,2]{2,1,0:T(2,128)S(1)}, u32[]{:S(2)}, u32[]{:S(2)}) %collective-permute-start.40) | collective-permute-done | bytes 48 | tf_op jit(solution)/shard_map/ppermute | solution.py:29
  160.4 3.7 %collective-permute-start.41 = (f32[1,2,2]{2,1,0:T(2,128)S(1)}, f32[1,2,2]{2,1,0:T(2,128)S(1)}, u32[]{:S(2)}, u32[]{:S(2)}) collective-permute-start(f32[1,2,2]{2,1,0:T(2,128)S(1)} %add.114), channel_id=1, source_target_pairs={{0,16},{2,18},{4,20},{6,22},{8,24},{10,26},{12,28},{14,30},{16,0},... | collective-permute-start | bytes 56 | tf_op jit(solution)/shard_map/ppermute | solution.py:29
  176.7 4.8 %collective-permute-done.42 = bf16[1,128,768]{1,2,0:T(8,128)(2,1)} collective-permute-done((bf16[1,128,768]{1,2,0:T(8,128)(2,1)}, bf16[1,128,768]{1,2,0:T(8,128)(2,1)}, u32[]{:S(2)}, u32[]{:S(2)}) %collective-permute-start.42) | collective-permute-done | bytes 196640 | tf_op jit(solution)/shard_map/ppermute | solution.py:29
  188.7 3.6 %collective-permute-done.36 = f32[2,2,2]{2,1,0:T(2,128)S(1)} collective-permute-done((f32[2,2,2]{2,1,0:T(2,128)S(1)}, f32[2,2,2]{2,1,0:T(2,128)S(1)}, u32[]{:S(2)}, u32[]{:S(2)}) %collective-permute-start.36) | collective-permute-done | bytes 64 | tf_op jit(solution)/shard_map/ppermute | solution.py:29
  192.8 4.0 %collective-permute-done.37 = f32[2,2,2]{2,1,0:T(2,128)S(1)} collective-permute-done((f32[2,2,2]{2,1,0:T(2,128)S(1)}, f32[2,2,2]{2,1,0:T(2,128)S(1)}, u32[]{:S(2)}, u32[]{:S(2)}) %collective-permute-start.37) | collective-permute-done | bytes 64 | tf_op jit(solution)/shard_map/ppermute | solution.py:29
  199.9 4.2 %all-to-all-start.3 = ((bf16[8,2,64,256]{3,2,0,1:T(8,128)(2,1)}), bf16[8,2,64,256]{3,2,0,1:T(8,128)(2,1)}, u32[]{:S(2)}, u32[]{:S(2)}) async-start(bf16[8,2,64,256]{3,2,0,1:T(8,128)(2,1)} %copy.74), calls=%async_computation.3 | async-start | bytes 1048576 | tf_op jit(solution)/shard_map/all_to_all | solution.py:369
  204.5 6.3 %all-to-all-done.3 = bf16[8,2,64,256]{3,2,0,1:T(8,128)(2,1)} async-done(((bf16[8,2,64,256]{3,2,0,1:T(8,128)(2,1)}), bf16[8,2,64,256]{3,2,0,1:T(8,128)(2,1)}, u32[]{:S(2)}, u32[]{:S(2)}) %all-to-all-start.3) | async-done | bytes 524320 | tf_op jit(solution)/shard_map/all_to_all | solution.py:369
  212.8 4.0 %all-to-all-start.4 = ((bf16[8,64,256]{2,1,0:T(8,128)(2,1)}), bf16[8,64,256]{2,1,0:T(8,128)(2,1)}, u32[]{:S(2)}, u32[]{:S(2)}) async-start(bf16[8,64,256]{2,1,0:T(8,128)(2,1)} %reduce_sum.61), calls=%async_computation.4 | async-start | bytes 524288 | tf_op jit(solution)/shard_map/all_to_all | solution.py:371
  (188 shorter events, 77.7 us)
Async XLA Ops:
  7.2 10.3 %collective-permute-start.3 = (bf16[64,2048]{1,0:T(8,128)(2,1)}, bf16[64,2048]{1,0:T(8,128)(2,1)S(1)}, u32[]{:S(2)}, u32[]{:S(2)}) collective-permute-start(bf16[64,2048]{1,0:T(8,128)(2,1)} %refs_0_.1), channel_id=1, source_target_pairs={{0,8},{2,10},{4,12},{6,14},{8,0},{10,2},{12,4},{14,6},{16,24},{18,... | collective-permute-start | bytes 786440 | tf_op jit(solution)/shard_map/ppermute | solution.py:29
  11.8 12.2 %collective-permute-start.7 = (bf16[64,2048]{1,0:T(8,128)(2,1)}, bf16[64,2048]{1,0:T(8,128)(2,1)}, u32[]{:S(2)}, u32[]{:S(2)}) collective-permute-start(bf16[64,2048]{1,0:T(8,128)(2,1)} %refs_0_.1), channel_id=1, source_target_pairs={{0,1},{1,0},{2,3},{3,2},{4,5},{5,4},{6,7},{7,6},{8,9},{9,8},{10,11... | collective-permute-start | bytes 786440 | tf_op jit(solution)/shard_map/ppermute | solution.py:29
  17.1 9.2 %collective-permute-start.18 = (bf16[64,2176]{1,0:T(8,128)(2,1)}, bf16[64,2176]{1,0:T(8,128)(2,1)S(1)}, u32[]{:S(2)}, u32[]{:S(2)}) collective-permute-start(bf16[64,2176]{1,0:T(8,128)(2,1)} %get-tuple-element.13.refs_16_), channel_id=1, source_target_pairs={{0,8},{2,10},{4,12},{6,14},{8,0},{10,2},{12,4},{14,6},{16,24},{18,... | collective-permute-start | bytes 835592 | tf_op jit(solution)/shard_map/ppermute | solution.py:29
  17.5 9.5 %collective-permute-start.22 = (bf16[64,2176]{1,0:T(8,128)(2,1)}, bf16[64,2176]{1,0:T(8,128)(2,1)S(1)}, u32[]{:S(2)}, u32[]{:S(2)}) collective-permute-start(bf16[64,2176]{1,0:T(8,128)(2,1)} %get-tuple-element.13.refs_16_), channel_id=1, source_target_pairs={{0,1},{1,0},{2,3},{3,2},{4,5},{5,4},{6,7},{7,6},{8,9},{9,8},{10,11... | collective-permute-start | bytes 835592 | tf_op jit(solution)/shard_map/ppermute | solution.py:29
  18.4 9.8 %collective-permute-start.16 = (bf16[64,2176]{1,0:T(8,128)(2,1)}, bf16[64,2176]{1,0:T(8,128)(2,1)S(1)}, u32[]{:S(2)}, u32[]{:S(2)}) collective-permute-start(bf16[64,2176]{1,0:T(8,128)(2,1)} %get-tuple-element.13.refs_16_), channel_id=1, source_target_pairs={{0,4},{2,6},{4,0},{6,2},{8,12},{10,14},{12,8},{14,10},{16,20},{18,... | collective-permute-start | bytes 835592 | tf_op jit(solution)/shard_map/ppermute | solution.py:29
  20.3 35.4 %all-to-all-start = ((bf16[8,288,128]{2,1,0:T(8,128)(2,1)}), bf16[8,288,128]{2,1,0:T(8,128)(2,1)S(1)}, u32[]{:S(2)}, u32[]{:S(2)}) async-start(bf16[8,288,128]{2,1,0:T(8,128)(2,1)} %get-tuple-element.14), calls=%async_computation | async-start | bytes 1179648 | tf_op jit(solution)/shard_map/all_to_all | solution.py:279
  24.6 14.7 %collective-permute-start.5 = (bf16[64,2048]{1,0:T(8,128)(2,1)S(1)}, bf16[64,2048]{1,0:T(8,128)(2,1)}, u32[]{:S(2)}, u32[]{:S(2)}) collective-permute-start(bf16[64,2048]{1,0:T(8,128)(2,1)S(1)} %collective-permute-done.3.refs_4_), channel_id=1, source_target_pairs={{0,4},{2,6},{4,0},{6,2},{8,12},{10,14},{12,8},{14,10},{16,20},{18,... | collective-permute-start | bytes 786440 | tf_op jit(solution)/shard_map/ppermute | solution.py:29
  26.2 14.4 %collective-permute-start.11 = (bf16[64,2048]{1,0:T(8,128)(2,1)S(1)}, bf16[64,2048]{1,0:T(8,128)(2,1)S(1)}, u32[]{:S(2)}, u32[]{:S(2)}) collective-permute-start(bf16[64,2048]{1,0:T(8,128)(2,1)S(1)} %collective-permute-done.3.refs_4_), channel_id=1, source_target_pairs={{0,1},{1,0},{2,3},{3,2},{4,5},{5,4},{6,7},{7,6},{8,9},{9,8},{10,11... | collective-permute-start | bytes 786440 | tf_op jit(solution)/shard_map/ppermute | solution.py:29
  27.0 13.6 %collective-permute-start.9 = (bf16[64,2048]{1,0:T(8,128)(2,1)S(1)}, bf16[64,2048]{1,0:T(8,128)(2,1)}, u32[]{:S(2)}, u32[]{:S(2)}) collective-permute-start(bf16[64,2048]{1,0:T(8,128)(2,1)S(1)} %collective-permute-done.1.refs_2_), channel_id=1, source_target_pairs={{0,1},{1,0},{2,3},{3,2},{4,5},{5,4},{6,7},{7,6},{8,9},{9,8},{10,11... | collective-permute-start | bytes 786440 | tf_op jit(solution)/shard_map/ppermute | solution.py:29
  28.3 12.9 %collective-permute-start.4 = (bf16[64,2048]{1,0:T(8,128)(2,1)S(1)}, bf16[64,2048]{1,0:T(8,128)(2,1)}, u32[]{:S(2)}, u32[]{:S(2)}) collective-permute-start(bf16[64,2048]{1,0:T(8,128)(2,1)S(1)} %collective-permute-done.3.refs_4_), channel_id=1, source_target_pairs={{0,2},{2,0},{4,6},{6,4},{8,10},{10,8},{12,14},{14,12},{16,18},{18,... | collective-permute-start | bytes 786440 | tf_op jit(solution)/shard_map/ppermute | solution.py:29
  28.3 14.4 %collective-permute-start.2 = (bf16[64,2048]{1,0:T(8,128)(2,1)S(1)}, bf16[64,2048]{1,0:T(8,128)(2,1)S(1)}, u32[]{:S(2)}, u32[]{:S(2)}) collective-permute-start(bf16[64,2048]{1,0:T(8,128)(2,1)S(1)} %collective-permute-done.1.refs_2_), channel_id=1, source_target_pairs={{0,2},{2,0},{4,6},{6,4},{8,10},{10,8},{12,14},{14,12},{16,18},{18,... | collective-permute-start | bytes 786440 | tf_op jit(solution)/shard_map/ppermute | solution.py:29
  40.6 9.5 %collective-permute-start.20 = (bf16[64,2176]{1,0:T(8,128)(2,1)S(1)}, bf16[64,2176]{1,0:T(8,128)(2,1)S(1)}, u32[]{:S(2)}, u32[]{:S(2)}) collective-permute-start(bf16[64,2176]{1,0:T(8,128)(2,1)S(1)} %collective-permute-done.18.refs_20_), channel_id=1, source_target_pairs={{0,4},{2,6},{4,0},{6,2},{8,12},{10,14},{12,8},{14,10},{16,20},{18,... | collective-permute-start | bytes 835592 | tf_op jit(solution)/shard_map/ppermute | solution.py:29
  41.2 14.5 %collective-permute-start.24 = (bf16[64,2176]{1,0:T(8,128)(2,1)S(1)}, bf16[64,2176]{1,0:T(8,128)(2,1)S(1)}, u32[]{:S(2)}, u32[]{:S(2)}) collective-permute-start(bf16[64,2176]{1,0:T(8,128)(2,1)S(1)} %collective-permute-done.22.refs_24_), channel_id=1, source_target_pairs={{0,4},{2,6},{4,0},{6,2},{8,12},{10,14},{12,8},{14,10},{16,20},{18,... | collective-permute-start | bytes 835592 | tf_op jit(solution)/shard_map/ppermute | solution.py:29
  42.7 13.0 %collective-permute-start.19 = (bf16[64,2176]{1,0:T(8,128)(2,1)S(1)}, bf16[64,2176]{1,0:T(8,128)(2,1)S(1)}, u32[]{:S(2)}, u32[]{:S(2)}) collective-permute-start(bf16[64,2176]{1,0:T(8,128)(2,1)S(1)} %collective-permute-done.18.refs_20_), channel_id=1, source_target_pairs={{0,2},{2,0},{4,6},{6,4},{8,10},{10,8},{12,14},{14,12},{16,18},{18,... | collective-permute-start | bytes 835592 | tf_op jit(solution)/shard_map/ppermute | solution.py:29
  42.8 15.6 %collective-permute-start.23 = (bf16[64,2176]{1,0:T(8,128)(2,1)S(1)}, bf16[64,2176]{1,0:T(8,128)(2,1)}, u32[]{:S(2)}, u32[]{:S(2)}) collective-permute-start(bf16[64,2176]{1,0:T(8,128)(2,1)S(1)} %collective-permute-done.22.refs_24_), channel_id=1, source_target_pairs={{0,2},{2,0},{4,6},{6,4},{8,10},{10,8},{12,14},{14,12},{16,18},{18,... | collective-permute-start | bytes 835592 | tf_op jit(solution)/shard_map/ppermute | solution.py:29
  47.4 11.5 %collective-permute-start.17 = (bf16[64,2176]{1,0:T(8,128)(2,1)S(1)}, bf16[64,2176]{1,0:T(8,128)(2,1)}, u32[]{:S(2)}, u32[]{:S(2)}) collective-permute-start(bf16[64,2176]{1,0:T(8,128)(2,1)S(1)} %collective-permute-done.16.refs_18_), channel_id=1, source_target_pairs={{0,2},{2,0},{4,6},{6,4},{8,10},{10,8},{12,14},{14,12},{16,18},{18,... | collective-permute-start | bytes 835592 | tf_op jit(solution)/shard_map/ppermute | solution.py:29
  55.8 29.3 %collective-permute-start.30 = (bf16[1,8,288,128]{3,2,1,0:T(8,128)(2,1)S(1)}, bf16[1,8,288,128]{3,2,1,0:T(8,128)(2,1)S(1)}, u32[]{:S(2)}, u32[]{:S(2)}) collective-permute-start(bf16[1,8,288,128]{3,2,1,0:T(8,128)(2,1)S(1)} %bitcast.81), channel_id=1, source_target_pairs={{0,16},{2,18},{4,20},{6,22},{8,24},{10,26},{12,28},{14,30},{16,0},... | collective-permute-start | bytes 1769480 | tf_op jit(solution)/shard_map/ppermute | solution.py:29
  58.4 8.9 %collective-permute-start.28 = (bf16[64,2176]{1,0:T(8,128)(2,1)S(1)}, bf16[64,2176]{1,0:T(8,128)(2,1)}, u32[]{:S(2)}, u32[]{:S(2)}) collective-permute-start(bf16[64,2176]{1,0:T(8,128)(2,1)S(1)} %collective-permute-done.26.refs_28_), channel_id=1, source_target_pairs={{0,4},{2,6},{4,0},{6,2},{8,12},{10,14},{12,8},{14,10},{16,20},{18,... | collective-permute-start | bytes 835592 | tf_op jit(solution)/shard_map/ppermute | solution.py:29
  123.0 17.2 %all-to-all-start.2 = ((bf16[16,96,128]{2,1,0:T(8,128)(2,1)}), bf16[16,96,128]{2,1,0:T(8,128)(2,1)S(1)}, u32[]{:S(2)}, u32[]{:S(2)}) async-start(bf16[16,96,128]{2,1,0:T(8,128)(2,1)} %local_tree.3), calls=%async_computation.2 | async-start | bytes 786432 | tf_op jit(solution)/shard_map/all_to_all | solution.py:326
  128.0 69.1 %all-gather.2.cloned.1.call-start = ((), (), s32[]{:S(2)}) async-start(), calls=%async_computation.5 | async-start | bytes 1769472 | tf_op jit(solution)/shard_map/all_gather | solution.py:364
  140.2 43.3 %all-to-all-start.1 = ((bf16[16,192,128]{2,1,0:T(8,128)(2,1)}), bf16[16,192,128]{2,1,0:T(8,128)(2,1)S(1)}, u32[]{:S(2)}, u32[]{:S(2)}) async-start(bf16[16,192,128]{2,1,0:T(8,128)(2,1)} %local_tree.2), calls=%async_computation.1 | async-start | bytes 1572864 | tf_op jit(solution)/shard_map/all_to_all | solution.py:326
  170.3 11.1 %collective-permute-start.42 = (bf16[1,128,768]{1,2,0:T(8,128)(2,1)}, bf16[1,128,768]{1,2,0:T(8,128)(2,1)}, u32[]{:S(2)}, u32[]{:S(2)}) collective-permute-start(bf16[1,128,768]{1,2,0:T(8,128)(2,1)} %get-tuple-element.43), channel_id=1, source_target_pairs={{0,16},{2,18},{4,20},{6,22},{8,24},{10,26},{12,28},{14,30},{16,0},... | collective-permute-start | bytes 589832 | tf_op jit(solution)/shard_map/ppermute | solution.py:29
  199.9 10.9 %all-to-all-start.3 = ((bf16[8,2,64,256]{3,2,0,1:T(8,128)(2,1)}), bf16[8,2,64,256]{3,2,0,1:T(8,128)(2,1)}, u32[]{:S(2)}, u32[]{:S(2)}) async-start(bf16[8,2,64,256]{3,2,0,1:T(8,128)(2,1)} %copy.74), calls=%async_computation.3 | async-start | bytes 1048576 | tf_op jit(solution)/shard_map/all_to_all | solution.py:369
  212.8 16.1 %all-to-all-start.4 = ((bf16[8,64,256]{2,1,0:T(8,128)(2,1)}), bf16[8,64,256]{2,1,0:T(8,128)(2,1)}, u32[]{:S(2)}, u32[]{:S(2)}) async-start(bf16[8,64,256]{2,1,0:T(8,128)(2,1)} %reduce_sum.61), calls=%async_computation.4 | async-start | bytes 524288 | tf_op jit(solution)/shard_map/all_to_all | solution.py:371
  (55 other events, 686.6 us)
Sparse Core Ops, SparseCore 0:
  130.4 26.9 all-gather.1

commit v2 on v1

v2 whole, which is shorter than its diff:
```python
import functools

import jax
import jax.numpy as jnp
from jax import lax
from jax.experimental import pallas as pl
from jax.experimental.pallas import tpu as pltpu
from jax.sharding import PartitionSpec as P

first_decay = 0.9
second_decay = 0.95
learn_rate = 0.01
adam_eps = 1e-08
weight_decay = 0.1
adam_count = 100.0
norm_eps = 1e-06
gathered_limit = 16
mask_lanes = 128
mebi = 1024 * 1024
vmem_bytes = 14 * mebi
vmem_most = 56 * mebi
f32 = jnp.float32
bf16 = jnp.bfloat16
any_space = pl.BlockSpec(memory_space=pl.ANY)
smem_space = pl.BlockSpec(memory_space=pltpu.SMEM)
vmem_space = pl.BlockSpec(memory_space=pltpu.VMEM)


def swapped(array, axis, bit):
    return lax.ppermute(array, axis, [(i, i ^ 1 << bit) for i in range(lax.axis_size(axis))])


def bits_of(size):
    return size.bit_length() - 1


def cube_gather(array, steps):
    pieces = {(0, 0): array}
    for axis, bit in steps:
        for (e, k), piece in list(pieces.items()):
            key = (e ^ (1 << bit), k) if axis == "expert" else (e, k ^ (1 << bit))
            pieces[key] = swapped(piece, axis, bit)
    return pieces


def waved_gather(mine, x_rows, sent, exchange, ids):
    z = lambda value: swapped(value, "dp", 2)
    y = lambda value: swapped(value, "dp", 1)
    x = lambda value: swapped(value, "expert", 0)
    from_z, from_y, from_x = z(mine), y(mine), x(mine)
    weights = exchange(sent)
    from_z, from_y, from_x, weights = lax.optimization_barrier((from_z, from_y, from_x, weights))
    from_zy, from_zx = y(from_z), x(from_z)
    from_yx = [x(from_y[:x_rows]), y(from_x[x_rows:])]
    from_zyx = [x(from_zy[:x_rows]), y(from_zx[x_rows:])]
    from_z, from_y, from_x, mine, ids, *_ = lax.optimization_barrier(
        (from_z, from_y, from_x, mine, ids, from_zy, from_zx)
    )
    pieces = {
        (0, 0): [mine],
        (0, 4): [from_z],
        (0, 2): [from_y],
        (1, 0): [from_x],
        (0, 6): [from_zy],
        (1, 4): [from_zx],
        (1, 2): from_yx,
        (1, 6): from_zyx,
    }
    for (e, k), held in list(pieces.items()):
        pieces[e, k | 1] = [swapped(piece, "dp", 0) for piece in held]
    return pieces, weights, ids


def tree_sum(value, bits, first=0):
    for bit in range(first, bits):
        value = value + swapped(value, "dp", bit)
    return value


def nt(a, b):
    return lax.dot_general(a, b, (((1,), (1,)), ((), ())), preferred_element_type=f32)


def tn(a, b):
    return lax.dot_general(a, b, (((0,), (0,)), ((), ())), preferred_element_type=f32)


def tree_weights(entry, count):
    gram = {(i, j): entry(i, j) for i in range(count) for j in range(i, count)}
    weights = [None] * count
    size = count
    while size > 1:
        scale = []
        for j in range(0, size, 2):
            cross = gram[j, j + 1]
            scale.append(1.0 - cross / (2.0 * (gram[j, j] + norm_eps)))
            scale.append(1.0 - cross / (2.0 * (gram[j + 1, j + 1] + norm_eps)))
        span = count // size
        for leaf in range(count):
            factor = scale[leaf // span]
            weights[leaf] = factor if weights[leaf] is None else weights[leaf] * factor
        full = lambda i, j: gram[min(i, j), max(i, j)] * (scale[i] * scale[j])
        size //= 2
        if size > 1:
            gram = {
                (i, j): full(2 * i, 2 * j)
                + full(2 * i, 2 * j + 1)
                + full(2 * i + 1, 2 * j)
                + full(2 * i + 1, 2 * j + 1)
                for i in range(size)
                for j in range(i, size)
            }
    return weights


def prepare_kernel(
    route_ref, counts_ref, tok_ref, cot_ref, gate_ref, up_ref, down_ref, out_ref, sent_ref
):
    group, part = sent_ref.shape[0], sent_ref.shape[1] // 3
    for index, ref in enumerate((gate_ref, up_ref, down_ref)):
        turned = ref[...].T.astype(bf16)
        for k in range(group):
            sent_ref[k, index * part : (index + 1) * part, :] = turned[k * part : (k + 1) * part, :]
    pool, width = cot_ref.shape
    experts, capacity = route_ref.shape
    out_ref[:pool, :width] = tok_ref[...]
    out_ref[:pool, width:] = jnp.zeros((pool, mask_lanes), bf16)
    out_ref[pool:, :width] = cot_ref[...]
    ids = lax.broadcasted_iota(jnp.int32, (pool, capacity), 0)
    slots = lax.broadcasted_iota(jnp.int32, (pool, capacity), 1)
    lanes = lax.broadcasted_iota(jnp.int32, (pool, mask_lanes), 1)
    flags = jnp.zeros((pool, mask_lanes), f32)
    for e in range(experts):
        named = (ids == route_ref[e : e + 1, :]) & (slots < counts_ref[0, e])
        found = jnp.sum(named.astype(f32), axis=1, keepdims=True)
        flags = jnp.where(lanes == e, found, flags)
    out_ref[pool:, width:] = flags.astype(bf16)


def place_rows(layout, refs, into, first, lanes, rows, pool, members):
    for (e, k), held in layout.items():
        low, at = 0, k * rows + e * pool
        for index, count in held:
            begin, end = max(low, first), min(low + count, first + pool)
            if begin < end and k in members:
                source = refs[index][begin - low : end - low, :lanes]
                into[at + begin - first : at + end - first, :] = source
            low += count


def gather_kernel(layout, experts, group, pool, pieces, idx_ref, *refs):
    shared, held, refs = refs[:pieces], refs[pieces:-9], refs[-9:]
    hid_ref, hid_abs_ref, dgate_ref, dup_ref, gram_ref, x_ref, y_ref, w_ref, row_ref = refs
    slot, expert, outer_index = idx_ref[0], idx_ref[1], idx_ref[2]
    part, total = hid_ref.shape
    rows = total // group
    width = x_ref.shape[1]
    per, _, _, block_rows = held[0].shape
    for o in range(per * len(held)):
        for h, ref in enumerate(held):

            @pl.when(((outer_index ^ o) // per) == h)
            def _(ref=ref, o=o):
                source = ref.at[(outer_index ^ o) % per]
                for b in range(group):
                    at = (o * group + b) * block_rows
                    w_ref[:, at : at + block_rows] = source[b]

    row_ref[...] = jnp.zeros_like(row_ref)
    pick = lax.broadcasted_iota(jnp.int32, (8, mask_lanes), 1) == expert
    both_members = max(1, min(group, 256 // rows))
    for first in range(0, group, both_members):
        members = range(first, first + both_members)
        mine, end = slice(first * rows, (first + both_members) * rows), (first + both_members) * rows
        place_rows(layout, shared, x_ref, 0, width, rows, pool, members)
        place_rows(layout, shared, y_ref, pool, width + mask_lanes, rows, pool, members)
        pre = nt(w_ref[: 2 * part, :], x_ref[mine, :])
        outer_x = nt(x_ref[mine, :], x_ref[:end, :])
        back_hidden = nt(w_ref[2 * part :, :], y_ref[mine, :width])
        outer_y = nt(y_ref[mine, :width], y_ref[:end, :width])
        mask = nt(pick.astype(bf16), y_ref[mine, width:])[0:1] > 0.5
        gate_pre, up_pre = pre[:part], pre[part:]
        sigmoid_gate = jax.nn.sigmoid(gate_pre)
        active_gate = gate_pre * sigmoid_gate
        kept = lambda value: jnp.where(mask, value, 0.0).astype(bf16)
        hidden = kept(active_gate * up_pre)
        hid_ref[:, mine] = hidden
        for n, k in enumerate(members):
            at = pl.multiple_of((slot ^ k) * rows, rows)
            hid_abs_ref[:, pl.ds(at, rows)] = hidden[:, n * rows : (n + 1) * rows]
        dgate_ref[:, mine] = kept(
            back_hidden * up_pre * sigmoid_gate * (1.0 + gate_pre * (1.0 - sigmoid_gate))
        )
        dup_ref[:, mine] = kept(back_hidden * active_gate)
        for m, (ref, prod) in enumerate(
            ((dgate_ref, outer_x), (dup_ref, outer_x), (hid_ref, outer_y))
        ):
            both = prod * tn(ref[:, mine], ref[:, :end])
            for n, k in enumerate(members):
                sums = both[n * rows : (n + 1) * rows, : (k + 1) * rows].sum(0, keepdims=True)
                row_ref[m * group + k : m * group + k + 1, : (k + 1) * rows] = sums
    lanes = lax.broadcasted_iota(jnp.int32, gram_ref.shape, 1)
    relative = jnp.zeros(gram_ref.shape, f32)
    for k in range(group):
        sums = row_ref[:, k * rows : (k + 1) * rows].sum(1, keepdims=True)
        relative = jnp.where(lanes == (slot ^ k), sums, relative)
    row_ids = lax.broadcasted_iota(jnp.int32, gram_ref.shape, 0)
    gram = jnp.zeros(gram_ref.shape, f32)
    for m in range(3):
        for k in range(group):
            row = relative[m * group + k : m * group + k + 1]
            gram = jnp.where(row_ids == m * group + (slot ^ k), row, gram)
    gram_ref[...] = gram


def vector_kernel(group, mats, idx_ref, gram_ref, in_ref, *refs):
    factors, out_ref = refs[:-1], refs[-1]
    part, total = factors[0].shape
    rows = total // group
    count, _, block_rows = out_ref.shape
    width = count * block_rows
    slot = idx_ref[0]
    scaled = []
    for m, ref in zip(mats, factors):

        def entry(i, j):
            a, b = slot ^ i, slot ^ j
            value = gram_ref[m * group + a, b]
            if i != j:
                value = value + gram_ref[m * group + b, a]
            return jnp.full((1, rows), value, f32)

        weights = tree_weights(entry, group)
        scaled.append(
            jnp.concatenate(
                [
                    (ref[:, d * rows : (d + 1) * rows].astype(f32) * weights[d]).astype(bf16)
                    for d in range(group)
                ],
                axis=1,
            )
        )
    left = jnp.concatenate(scaled, axis=0)
    vector = jnp.dot(left, in_ref[:, :width], preferred_element_type=f32).astype(bf16)
    for i in range(count):
        out_ref[i] = vector[:, i * block_rows : (i + 1) * block_rows]


def update_kernel(group, mats, gram_ref, got_ref, *refs):
    masters = refs[:mats]
    first_ref, second_ref = refs[mats : mats + 2]
    outs = refs[-5:] if mats == 1 else refs[-4:]
    sum_ref, new_ref, new_first_ref, new_second_ref = outs[:4]
    outer = got_ref.shape[0] // group
    block_rows = got_ref.shape[2]
    part = got_ref.shape[1] // mats
    for m in range(mats):
        entry = lambda i, j: jnp.full((1, block_rows), gram_ref[m * outer + i, j], f32)
        weights = tree_weights(entry, outer)
        total = 0.0
        for o in range(outer):
            held = [
                got_ref[o * group + s, m * part : (m + 1) * part, :].astype(f32)
                for s in range(group)
            ]
            total = total + weights[o] * jnp.concatenate(held, axis=0)
        total = total.T
        first = first_decay * first_ref[m] + (1.0 - first_decay) * total
        second = second_decay * second_ref[m] + (1.0 - second_decay) * total * total
        first_hat = first / (1.0 - first_decay**adam_count)
        second_hat = second / (1.0 - second_decay**adam_count)
        old = masters[m][...]
        new = old - learn_rate * (first_hat / (jnp.sqrt(second_hat) + adam_eps) + weight_decay * old)
        sum_ref[m] = total
        new_ref[m] = new
        new_first_ref[m] = first
        new_second_ref[m] = second
        if mats == 1:
            outs[-1][...] = new.astype(bf16)


def project_kernel(group, idx_ref, *refs):
    parts, downs, (out_ref, hidden_ref, all_ref) = refs[:group], refs[group:-3], refs[-3:]
    slot, expert, outer_index = idx_ref[0], idx_ref[1], idx_ref[2]
    bits, part = bits_of(group), parts[0].shape[0]
    for n, ref in enumerate(parts):
        relative = sum((n >> b & 1) << (bits - 1 - b) for b in range(bits))
        at = pl.multiple_of((slot ^ relative) * part, 16)
        hidden_ref[pl.ds(at, part), :] = ref[...]
    per, block_rows = downs[0].shape[:2]
    for o in range(per * len(downs)):
        for h, ref in enumerate(downs):

            @pl.when(((outer_index ^ o) // per) == h)
            def _(ref=ref, o=o):
                all_ref[o * block_rows : (o + 1) * block_rows, :] = ref[(outer_index ^ o) % per]

    made = lax.dot_general(
        hidden_ref[...], all_ref[...], (((0,), (1,)), ((), ())), preferred_element_type=f32
    )
    experts, pool = out_ref.shape[1], out_ref.shape[2]
    for d in range(out_ref.shape[0]):
        for e in range(experts):
            at = (d * experts + e) * pool
            out_ref[d, expert ^ e] = made[at : at + pool].astype(bf16)


def finish_kernel(experts, block_rows, got_ref, out_ref):
    group = got_ref.shape[0] // experts
    for o in range(got_ref.shape[2] // block_rows):
        for s in range(group):
            lanes = slice(o * block_rows, (o + 1) * block_rows)
            total = got_ref[s * experts, :, lanes].astype(f32)
            for e in range(1, experts):
                total = total + got_ref[s * experts + e, :, lanes].astype(f32)
            at = (o * group + s) * block_rows
            out_ref[:, at : at + block_rows] = total.astype(bf16)


def call(kernel, outs, args, in_specs, scratch=(), out_specs=None, aliases=None, name=None, grid=(), vmem=vmem_bytes):
    return pl.pallas_call(
        kernel,
        out_shape=outs,
        grid=grid,
        in_specs=in_specs,
        out_specs=out_specs if out_specs is not None else jax.tree.map(lambda _: vmem_space, outs),
        scratch_shapes=list(scratch),
        compiler_params=pltpu.CompilerParams(vmem_limit_bytes=min(vmem, vmem_most)),
        input_output_aliases=aliases or {},
        name=name,
    )(*args)


def after(value, *others):
    return lax.optimization_barrier((value, *others))[0]


def shards(
    tokens,
    cotangent,
    route,
    counts,
    gate_master,
    up_master,
    down_master,
    first_moment,
    second_moment,
):
    experts = lax.axis_size("expert")
    dp = lax.axis_size("dp")
    group = max(1, min(gathered_limit // experts, dp))
    inner_bits = bits_of(group)
    outer_bits = bits_of(dp // group)
    outer = dp // group
    dp_bits = inner_bits + outer_bits
    pool, width = tokens.shape
    rows = experts * pool
    total = group * rows
    block_rows, hidden_width = gate_master.shape[1:]
    part = hidden_width // group
    my_dp = lax.axis_index("dp")
    expert_index = lax.axis_index("expert")
    my_ids = jnp.stack([my_dp % group, expert_index, my_dp // group]).astype(jnp.int32)
    groups = [[o * group + s for s in range(group)] for o in range(outer)]
    cubes = [[o * group * experts + s for s in range(group * experts)] for o in range(outer)]
    capacity = route.shape[0] // experts
    sds = jax.ShapeDtypeStruct
    masters = [gate_master[0], up_master[0], down_master[0]]

    mine, sent = call(
        prepare_kernel,
        (
            sds((2 * pool, width + mask_lanes), bf16),
            sds((group, 3 * part, block_rows), bf16),
        ),
        (route.reshape(experts, capacity), counts, tokens, cotangent, *masters),
        [vmem_space, smem_space] + [vmem_space] * 5,
        name="prepare",
        vmem=vmem_most,
    )
    exchange = lambda sent: lax.all_to_all(
        sent, "dp", 0, 0, axis_index_groups=groups, tiled=True
    )
    if inner_bits == 3 and experts == 2:
        pieces, own_group, my_ids = waved_gather(
            mine, -(-5 * pool // 64) * 16, sent, exchange, my_ids
        )
    else:
        steps = [("expert", b) for b in range(bits_of(experts))]
        steps += [("dp", b) for b in reversed(range(inner_bits))]
        pieces = {key: [value] for key, value in cube_gather(mine, steps).items()}
        own_group = exchange(sent)
    shared, layout = [], {}
    for key, parts in pieces.items():
        layout[key] = [(len(shared) + n, piece.shape[0]) for n, piece in enumerate(parts)]
        shared += parts
    held = [own_group[None]]
    for bit in range(outer_bits):
        held = [jnp.concatenate(held)] if len(held) > 1 else held
        held = [held[0], swapped(held[0], "dp", inner_bits + bit)]
    wide = width + mask_lanes
    factor = sds((part, total), bf16)
    gram_rows = -(-3 * group // 8) * 8
    rows_bytes, weight_bytes = 4 * total * wide, 6 * part * width
    hidden, hidden_own, d_gate, d_up, gram, token_all, grad_all = call(
        functools.partial(gather_kernel, layout, experts, group, pool, len(shared)),
        (
            *(factor,) * 4,
            sds((gram_rows, 128), f32),
            sds((total, width), bf16),
            sds((total, wide), bf16),
        ),
        (my_ids, *shared, *held),
        [smem_space] + [vmem_space] * (len(shared) + len(held)),
        scratch=(
            pltpu.VMEM((3 * part, width), bf16),
            pltpu.VMEM((gram_rows, total), f32),
        ),
        name="forward_and_gram",
        vmem=5 * rows_bytes // 2 + 3 * weight_bytes + 4 * total * total * (outer // 4),
    )
    gram = tree_sum(gram, inner_bits)

    def local_vector(left, mats, factors):
        return call(
            functools.partial(vector_kernel, group, mats),
            sds((dp, len(mats) * part, block_rows), bf16),
            (my_ids, gram, left, *factors),
            [smem_space] * 2 + [vmem_space] * (1 + len(factors)),
            vmem=rows_bytes + 3 * len(mats) * 4 * part * width + 4 * mebi,
            name="local_tree",
        )

    def last_gram(got, mats):
        wide = got.reshape(outer, group, mats, part, block_rows).transpose(2, 0, 1, 3, 4)
        wide = wide.reshape(mats, outer, hidden_width, block_rows).astype(f32)
        if outer > 2:
            products = jnp.einsum("miab,mjab->mij", wide, wide, precision=lax.Precision.HIGHEST)
        else:
            products = (wide[:, :, None] * wide[:, None]).sum((3, 4))
        return tree_sum(products.reshape(mats * outer, outer), half)

    def update(got, products, mats, start, olds, previous):
        block = pl.BlockSpec((mats, block_rows, hidden_width), lambda i: (start, 0, 0))
        whole = sds((3, block_rows, hidden_width), f32)
        kernel = functools.partial(update_kernel, group, mats)
        outs, out_specs = (whole,) * 4, (block,) * 4
        if mats == 1:
            outs += (sds((block_rows, hidden_width), bf16),)
            out_specs += (vmem_space,)
        return call(
            kernel,
            outs,
            (products, got, *olds, first_moment[0], second_moment[0], *previous),
            [smem_space] + [vmem_space] * (1 + mats) + [block] * 2 + [any_space] * len(previous),
            out_specs=out_specs,
            aliases={4 + mats + i: i for i in range(len(previous))},
            grid=(1,),
            name="update",
            vmem=4 * got.shape[0] * got.shape[1] * 256 + 10 * mebi,
        )

    down_vector = local_vector(grad_all, (2,), [hidden])
    pair_vector = local_vector(token_all, (0, 1), [d_gate, d_up])
    exchange_rows = lambda vector: lax.all_to_all(vector, "dp", 0, 0, tiled=True)
    down_got = exchange_rows(after(down_vector, pair_vector))
    hidden_parts = [after(hidden_own, pair_vector)]
    for bit in reversed(range(inner_bits)):
        hidden_parts += [swapped(piece, "dp", bit) for piece in hidden_parts]
    half = inner_bits - 1
    down_gram = tree_sum(last_gram(down_got, 1), dp_bits, half)
    pair_got = exchange_rows(after(pair_vector, down_got, *hidden_parts[: group // 2]))
    *partial_out, new_down = update(down_got, down_gram, 1, 2, masters[2:], ())
    pair_gram = last_gram(after(pair_got, new_down), 2)
    downs = [new_down[None]]
    for bit in range(outer_bits):
        downs = [jnp.concatenate(downs)] if len(downs) > 1 else downs
        downs = [downs[0], swapped(downs[0], "dp", inner_bits + bit)]
    downs[-1] = after(downs[-1], pair_gram)
    pair_gram = tree_sum(pair_gram, dp_bits, half)
    slot_outputs = call(
        functools.partial(project_kernel, group),
        sds((group, experts, pool, outer * block_rows), bf16),
        (my_ids, *hidden_parts, *downs),
        [smem_space] + [vmem_space] * (group + len(downs)),
        scratch=(
            pltpu.VMEM((hidden_width, total), bf16),
            pltpu.VMEM((outer * block_rows, hidden_width), bf16),
        ),
        name="project",
        vmem=12 * total * outer * block_rows + 12 * mebi,
    )
    slot_outputs = slot_outputs.reshape(group * experts, pool, outer * block_rows)
    columns = lax.all_to_all(
        slot_outputs, ("dp", "expert"), 0, 0, axis_index_groups=cubes, tiled=True
    )
    outs = update(pair_got, pair_gram, 2, 0, masters[:2], partial_out)
    forward = call(
        functools.partial(finish_kernel, experts, block_rows),
        sds((pool, width), bf16),
        (columns,),
        [vmem_space],
        name="finish",
    )
    return (*[out[None] for out in outs], forward)


def solution(mesh):
    in_specs = (
        P(("dp", "expert"), None),
        P(("dp", "expert"), None),
        P(("dp", "expert")),
        P(("dp", "expert"), None),
        P("expert", "dp", None),
        P("expert", "dp", None),
        P("expert", "dp", None),
        P("expert", None, "dp", None),
        P("expert", None, "dp", None),
    )
    out_specs = (
        P("expert", None, "dp", None),
        P("expert", None, "dp", None),
        P("expert", None, "dp", None),
        P("expert", None, "dp", None),
        P(("dp", "expert"), None),
    )
    return jax.shard_map(shards, mesh=mesh, in_specs=in_specs, out_specs=out_specs, check_vma=False)
```

time: 239 us -> 187 us (0.78)
  between operations: 17.1 us -> 0.92 us
  local copies, waits for them, and re-layouts: 19.2 us -> 5.85 us
  other arithmetic: 12.6 us -> 0.75 us
  waiting for transfers between devices: 97.5 us -> 91.8 us
  Pallas kernels: 33.5 us -> 28.7 us
    all_to_all x4 -> x3, waiting for transfers between devices: 12.2 us -> 0.01 us  [the longest x2 0.01 us: shards(): lax.all_to_all(vector, 'dp', 0, 0, tiled=True)]
    unnamed x64 -> x32, local copies, waits for them, and re-layouts: 13 us -> 3.56 us
    ppermute x43 -> x39, waiting for transfers between devices: 84.8 us -> 91.8 us  [swapped(): lax.ppermute(array, axis, [(i, i ^ 1 << bit) for i in range(lax.axis_size...]
    pallas_call x4 -> x8, Pallas kernels: 33.5 us -> 28.7 us  [call(): pl.pallas_call(kernel, out_shape=outs, grid=grid, in_specs=in_specs, out_...]
    ppermute x43 -> x39, starting transfers between devices: 34.9 us -> 39 us  [swapped(): lax.ppermute(array, axis, [(i, i ^ 1 << bit) for i in range(lax.axis_size...]
    all_to_all x4 -> x3, starting transfers between devices: 16.9 us -> 13.8 us  [the longest x2 9.52 us: shards(): lax.all_to_all(vector, 'dp', 0, 0, tiled=True)]
    sub x2 -> x0, other arithmetic: 2.81 us -> none  [the longest x1 2.63 us: adam(): old - learn_rate * (first_hat / (jnp.sqrt(second_hat) + adam_eps) + weigh...]
    broadcast_in_dim x3 -> x0, other arithmetic: 2.57 us -> none  [shards(): jnp.concatenate([a, b])[None]]
  transfers between devices with their start and end apart: 49 -> 43, of which waited for: 23 -> 25; matrix products, arithmetic and copies ran while one was open for 9% -> 1% of each run, Pallas kernels for 3% -> 3%
where the time goes in v2:
time: 187 us; the launch traced here: 186 us
  waiting for transfers between devices  91.8 us (49%)
  starting transfers between devices  58.1 us (31%)
  Pallas kernels  28.7 us (15%)
  local copies, waits for them, and re-layouts  5.85 us (3%)
    ppermute x39, waiting for transfers between devices, swapped(): lax.ppermute(array, axis, [(i, i ^ 1 << bit) for i in range(lax.axis_size...  91.8 us
    ppermute x39, starting transfers between devices, swapped(): lax.ppermute(array, axis, [(i, i ^ 1 << bit) for i in range(lax.axis_size...  39 us
    pallas_call x8, Pallas kernels, call(): pl.pallas_call(kernel, out_shape=outs, grid=grid, in_specs=in_specs, out_...  28.7 us
    all_to_all x2, starting transfers between devices, shards(): lax.all_to_all(vector, 'dp', 0, 0, tiled=True)  9.52 us
    all_to_all x1, starting transfers between devices, shards(): lax.all_to_all(sent, 'dp', 0, 0, axis_index_groups=groups, tiled=True)  5.26 us
    all_to_all x1, starting transfers between devices, shards(): lax.all_to_all(slot_outputs, ('dp', 'expert'), 0, 0, axis_index_groups=cu...  4.24 us
  transfers between devices with their start and end apart: 43, of which 25 were waited for; matrix products, arithmetic and copies ran while one was open for 1% of the time, Pallas kernels for 3%

profile of v2, /device:TPU:0, one launch (start us, length us, event | category | flops | bytes accessed | tf_op | source)
XLA Modules:
  0.0 186.1 jit_solution(1706182786175657319)
XLA Ops:
  1.9 2.7 %prepare.1 = (bf16[128,2176]{1,0:T(8,128)(2,1)}, bf16[8,288,128]{2,1,0:T(8,128)(2,1)}) custom-call(s32[2,64]{1,0:T(2,128)} %reshape.61.route_ref, s32[1,2]{1,0:T(1,128)} %counts_ref.1, bf16[64,2048]{1,0:T(8,128)(2,1)} %tok_ref.1, bf16[64,2048]{1,0:T(8,128)(2,1)} %cot_ref.1, f32[128,768]{1,0:T(8,128)} %bitcast.34, f32[128,768]{1,0:T(8,128)} %bitcast.36, ...), custom_call_target="tpu_custom_call" | custom-call | tf_op jit(solution)/shard_map/prepare/pallas_call | solution.py:321
  4.6 5.3 %all-to-all-start = ((bf16[8,288,128]{2,1,0:T(8,128)(2,1)}), bf16[8,288,128]{2,1,0:T(8,128)(2,1)S(1)}, u32[]{:S(2)}, u32[]{:S(2)}) async-start(bf16[8,288,128]{2,1,0:T(8,128)(2,1)} %get-tuple-element.38), calls=%async_computation | async-start | bytes 1179648 | tf_op jit(solution)/shard_map/all_to_all | solution.py:381
  14.8 10.3 %collective-permute-done.2.refs_3_ = bf16[128,2176]{1,0:T(8,128)(2,1)S(1)} collective-permute-done((bf16[128,2176]{1,0:T(8,128)(2,1)}, bf16[128,2176]{1,0:T(8,128)(2,1)S(1)}, u32[]{:S(2)}, u32[]{:S(2)}) %collective-permute-start.2) | collective-permute-done | bytes 557088 | tf_op jit(solution)/shard_map/ppermute | solution.py:30
  25.1 6.2 %collective-permute-done.1.refs_2_ = bf16[128,2176]{1,0:T(8,128)(2,1)S(1)} collective-permute-done((bf16[128,2176]{1,0:T(8,128)(2,1)}, bf16[128,2176]{1,0:T(8,128)(2,1)S(1)}, u32[]{:S(2)}, u32[]{:S(2)}) %collective-permute-start.1) | collective-permute-done | bytes 557088 | tf_op jit(solution)/shard_map/ppermute | solution.py:30
  34.4 2.6 %collective-permute-start.19 = (bf16[1,8,288,128]{3,2,1,0:T(8,128)(2,1)S(1)}, bf16[1,8,288,128]{3,2,1,0:T(8,128)(2,1)S(1)}, u32[]{:S(2)}, u32[]{:S(2)}) collective-permute-start(bf16[1,8,288,128]{3,2,1,0:T(8,128)(2,1)S(1)} %bitcast.31), channel_id=1, source_target_pairs={{0,16},{2,18},{4,20},{6,22},{8,24},{10,26},{12,28},{14,30},{16,0},... | collective-permute-start | bytes 1769480 | tf_op jit(solution)/shard_map/ppermute | solution.py:30
  38.9 12.7 %collective-permute-done.6.refs_7_ = bf16[48,2176]{1,0:T(8,128)(2,1)} collective-permute-done((bf16[48,2176]{1,0:T(8,128)(2,1)S(1)}, bf16[48,2176]{1,0:T(8,128)(2,1)}, u32[]{:S(2)}, u32[]{:S(2)}) %collective-permute-start.6) | collective-permute-done | bytes 208928 | tf_op jit(solution)/shard_map/ppermute | solution.py:30
  56.6 5.6 %collective-permute-done.19.refs_21_ = bf16[1,8,288,128]{3,2,1,0:T(8,128)(2,1)S(1)} collective-permute-done((bf16[1,8,288,128]{3,2,1,0:T(8,128)(2,1)S(1)}, bf16[1,8,288,128]{3,2,1,0:T(8,128)(2,1)S(1)}, u32[]{:S(2)}, u32[]{:S(2)}) %collective-permute-start.19) | collective-permute-done | bytes 589856 | tf_op jit(solution)/shard_map/ppermute | solution.py:30
  70.4 12.0 %forward_and_gram.1 = (bf16[96,1024]{1,0:T(8,128)(2,1)S(1)}, bf16[96,1024]{1,0:T(8,128)(2,1)S(1)}, bf16[96,1024]{1,0:T(8,128)(2,1)S(1)}, bf16[96,1024]{1,0:T(8,1...) custom-call(s32[3]{0:T(128)S(1)} %pad_add_fusion.idx_ref, ...), custom_call_target="tpu_custom_call" | custom-call | tf_op jit(solution)/shard_map/forward_and_gram/pallas_call | solution.py:321
  84.2 3.1 %collective-permute-done.21 = f32[24,128]{1,0:T(8,128)S(1)} collective-permute-done((f32[24,128]{1,0:T(8,128)S(1)}, f32[24,128]{1,0:T(8,128)S(1)}, u32[]{:S(2)}, u32[]{:S(2)}) %collective-permute-start.21) | collective-permute-done | bytes 12320 | tf_op jit(solution)/shard_map/ppermute | solution.py:30
  88.1 2.9 %collective-permute-done.22 = f32[24,128]{1,0:T(8,128)S(1)} collective-permute-done((f32[24,128]{1,0:T(8,128)S(1)}, f32[24,128]{1,0:T(8,128)S(1)}, u32[]{:S(2)}, u32[]{:S(2)}) %collective-permute-start.22) | collective-permute-done | bytes 12320 | tf_op jit(solution)/shard_map/ppermute | solution.py:30
  93.5 2.9 %local_tree.2 = bf16[16,192,128]{2,1,0:T(8,128)(2,1)} custom-call(s32[3]{0:T(128)S(1)} %pad_add_fusion.idx_ref, f32[24,128]{1,0:T(8,128)S(1)} %add.41.gram_ref, bf16[1024,2048]{1,0:T(8,128)(2,1)S(1)} %get-tuple-element.49.in_ref, bf16[96,1024]{1,0:T(8,128)(2,1)S(1)} %get-tuple-element.50.refs_0_, bf16[96,1024]{1,0:T(8,128)(2,1)S(1)} %get-tuple-element.51.refs_1_), custom_call_target="tpu_custom_call" | custom-call | tf_op jit(solution)/shard_map/local_tree/pallas_call | solution.py:321
  96.3 4.8 %all-to-all-start.1 = ((bf16[16,96,128]{2,1,0:T(8,128)(2,1)}), bf16[16,96,128]{2,1,0:T(8,128)(2,1)S(1)}, u32[]{:S(2)}, u32[]{:S(2)}) async-start(bf16[16,96,128]{2,1,0:T(8,128)(2,1)} %local_tree.3), calls=%async_computation.1 | async-start | bytes 786432 | tf_op jit(solution)/shard_map/all_to_all | solution.py:465
  104.6 10.2 %collective-permute-done.23.refs_1_ = bf16[96,1024]{1,0:T(8,128)(2,1)S(1)} collective-permute-done((bf16[96,1024]{1,0:T(8,128)(2,1)S(1)}, bf16[96,1024]{1,0:T(8,128)(2,1)S(1)}, u32[]{:S(2)}, u32[]{:S(2)}) %collective-permute-start.23) | collective-permute-done | bytes 196640 | tf_op jit(solution)/shard_map/ppermute | solution.py:30
  116.2 5.0 %collective-permute-done.25.refs_3_ = bf16[96,1024]{1,0:T(8,128)(2,1)S(1)} collective-permute-done((bf16[96,1024]{1,0:T(8,128)(2,1)S(1)}, bf16[96,1024]{1,0:T(8,128)(2,1)S(1)}, u32[]{:S(2)}, u32[]{:S(2)}) %collective-permute-start.25) | collective-permute-done | bytes 196640 | tf_op jit(solution)/shard_map/ppermute | solution.py:30
  121.9 4.7 %all-to-all-start.2 = ((bf16[16,192,128]{2,1,0:T(8,128)(2,1)}), bf16[16,192,128]{2,1,0:T(8,128)(2,1)S(1)}, u32[]{:S(2)}, u32[]{:S(2)}) async-start(bf16[16,192,128]{2,1,0:T(8,128)(2,1)} %local_tree.2), calls=%async_computation.2 | async-start | bytes 1572864 | tf_op jit(solution)/shard_map/all_to_all | solution.py:465
  130.8 2.7 %collective-permute-done.27 = f32[2,2]{1,0:T(2,128)S(1)} collective-permute-done((f32[2,2]{1,0:T(2,128)S(1)}, f32[2,2]{1,0:T(2,128)S(1)}, u32[]{:S(2)}, u32[]{:S(2)}) %collective-permute-start.27) | collective-permute-done | bytes 48 | tf_op jit(solution)/shard_map/ppermute | solution.py:30
  134.4 6.1 %collective-permute-done.28 = f32[2,2]{1,0:T(2,128)S(1)} collective-permute-done((f32[2,2]{1,0:T(2,128)S(1)}, f32[2,2]{1,0:T(2,128)S(1)}, u32[]{:S(2)}, u32[]{:S(2)}) %collective-permute-start.28) | collective-permute-done | bytes 48 | tf_op jit(solution)/shard_map/ppermute | solution.py:30
  140.5 4.4 %collective-permute-start.29 = (f32[2,2]{1,0:T(2,128)S(1)}, f32[2,2]{1,0:T(2,128)S(1)}, u32[]{:S(2)}, u32[]{:S(2)}) collective-permute-start(f32[2,2]{1,0:T(2,128)S(1)} %add.44), channel_id=1, source_target_pairs={{0,16},{2,18},{4,20},{6,22},{8,24},{10,26},{12,28},{14,30},{16,0},... | collective-permute-start | bytes 56 | tf_op jit(solution)/shard_map/ppermute | solution.py:30
  144.9 2.7 %collective-permute-done.29 = f32[2,2]{1,0:T(2,128)S(1)} collective-permute-done((f32[2,2]{1,0:T(2,128)S(1)}, f32[2,2]{1,0:T(2,128)S(1)}, u32[]{:S(2)}, u32[]{:S(2)}) %collective-permute-start.29) | collective-permute-done | bytes 48 | tf_op jit(solution)/shard_map/ppermute | solution.py:30
  156.8 3.2 %collective-permute-done.38.refs_9_ = bf16[1,128,768]{2,1,0:T(8,128)(2,1)} collective-permute-done((bf16[1,128,768]{2,1,0:T(8,128)(2,1)}, bf16[1,128,768]{2,1,0:T(8,128)(2,1)}, u32[]{:S(2)}, u32[]{:S(2)}) %collective-permute-start.38) | collective-permute-done | bytes 196640 | tf_op jit(solution)/shard_map/ppermute | solution.py:30
  163.0 4.2 %all-to-all-start.3 = ((bf16[16,64,256]{2,1,0:T(8,128)(2,1)}), bf16[16,64,256]{2,1,0:T(8,128)(2,1)}, u32[]{:S(2)}, u32[]{:S(2)}) async-start(bf16[16,64,256]{2,1,0:T(8,128)(2,1)} %bitcast.33), calls=%async_computation.3 | async-start | bytes 1048576 | tf_op jit(solution)/shard_map/all_to_all | solution.py:494
  169.0 6.9 %collective-permute-done.32 = f32[4,2]{1,0:T(4,128)S(1)} collective-permute-done((f32[4,2]{1,0:T(4,128)S(1)}, f32[4,2]{1,0:T(4,128)S(1)}, u32[]{:S(2)}, u32[]{:S(2)}) %collective-permute-start.32) | collective-permute-done | bytes 64 | tf_op jit(solution)/shard_map/ppermute | solution.py:30
  175.9 2.6 %collective-permute-start.33 = (f32[4,2]{1,0:T(4,128)S(1)}, f32[4,2]{1,0:T(4,128)S(1)}, u32[]{:S(2)}, u32[]{:S(2)}) collective-permute-start(f32[4,2]{1,0:T(4,128)S(1)} %add.48), channel_id=1, source_target_pairs={{0,16},{2,18},{4,20},{6,22},{8,24},{10,26},{12,28},{14,30},{16,0},... | collective-permute-start | bytes 104 | tf_op jit(solution)/shard_map/ppermute | solution.py:30
  181.4 2.9 %update.3 = (f32[3,128,768]{2,1,0:T(8,128)}, f32[3,128,768]{2,1,0:T(8,128)}, f32[3,128,768]{2,1,0:T(8,128)}, f32[3,128,768]{2,1,0:T(8,128)}) custom-call(f32[4,2]{1,0:T(4,128)S(1)} %add.49.gram_ref, bf16[16,192,128]{2,1,0:T(8,128)(2,1)S(1)} %all-to-all-done.2.got_ref, ...), custom_call_target="tpu_custom_call", output_to_operand_aliasing={{0}: (6, {}), {1}: (7, {}), {2}: (8, {}), {3}: (9, {})} | custom-call | tf_op jit(solution)/shard_map/update/pallas_call | solution.py:321
  (123 shorter events, 58.5 us)
Async XLA Ops:
  4.6 26.8 %all-to-all-start = ((bf16[8,288,128]{2,1,0:T(8,128)(2,1)}), bf16[8,288,128]{2,1,0:T(8,128)(2,1)S(1)}, u32[]{:S(2)}, u32[]{:S(2)}) async-start(bf16[8,288,128]{2,1,0:T(8,128)(2,1)} %get-tuple-element.38), calls=%async_computation | async-start | bytes 1179648 | tf_op jit(solution)/shard_map/all_to_all | solution.py:381
  9.8 15.2 %collective-permute-start.2 = (bf16[128,2176]{1,0:T(8,128)(2,1)}, bf16[128,2176]{1,0:T(8,128)(2,1)S(1)}, u32[]{:S(2)}, u32[]{:S(2)}) collective-permute-start(bf16[128,2176]{1,0:T(8,128)(2,1)} %get-tuple-element.43.refs_0_), channel_id=1, source_target_pairs={{0,1},{1,0},{2,3},{3,2},{4,5},{5,4},{6,7},{7,6},{8,9},{9,8},{10,11... | collective-permute-start | bytes 1671176 | tf_op jit(solution)/shard_map/ppermute | solution.py:30
  11.3 20.0 %collective-permute-start.1 = (bf16[128,2176]{1,0:T(8,128)(2,1)}, bf16[128,2176]{1,0:T(8,128)(2,1)S(1)}, u32[]{:S(2)}, u32[]{:S(2)}) collective-permute-start(bf16[128,2176]{1,0:T(8,128)(2,1)} %get-tuple-element.43.refs_0_), channel_id=1, source_target_pairs={{0,4},{2,6},{4,0},{6,2},{8,12},{10,14},{12,8},{14,10},{16,20},{18,... | collective-permute-start | bytes 1671176 | tf_op jit(solution)/shard_map/ppermute | solution.py:30
  13.4 18.1 %collective-permute-start = (bf16[128,2176]{1,0:T(8,128)(2,1)}, bf16[128,2176]{1,0:T(8,128)(2,1)}, u32[]{:S(2)}, u32[]{:S(2)}) collective-permute-start(bf16[128,2176]{1,0:T(8,128)(2,1)} %get-tuple-element.43.refs_0_), channel_id=1, source_target_pairs={{0,8},{2,10},{4,12},{6,14},{8,0},{10,2},{12,4},{14,6},{16,24},{18,... | collective-permute-start | bytes 1671176 | tf_op jit(solution)/shard_map/ppermute | solution.py:30
  31.4 20.2 %collective-permute-start.4 = (bf16[128,2176]{1,0:T(8,128)(2,1)}, bf16[128,2176]{1,0:T(8,128)(2,1)S(1)}, u32[]{:S(2)}, u32[]{:S(2)}) collective-permute-start(bf16[128,2176]{1,0:T(8,128)(2,1)} %collective-permute-done.refs_1_), channel_id=1, source_target_pairs={{0,1},{1,0},{2,3},{3,2},{4,5},{5,4},{6,7},{7,6},{8,9},{9,8},{10,11... | collective-permute-start | bytes 1671176 | tf_op jit(solution)/shard_map/ppermute | solution.py:30
  32.9 20.5 %collective-permute-start.3 = (bf16[128,2176]{1,0:T(8,128)(2,1)}, bf16[128,2176]{1,0:T(8,128)(2,1)S(1)}, u32[]{:S(2)}, u32[]{:S(2)}) collective-permute-start(bf16[128,2176]{1,0:T(8,128)(2,1)} %collective-permute-done.refs_1_), channel_id=1, source_target_pairs={{0,4},{2,6},{4,0},{6,2},{8,12},{10,14},{12,8},{14,10},{16,20},{18,... | collective-permute-start | bytes 1671176 | tf_op jit(solution)/shard_map/ppermute | solution.py:30
  34.4 27.9 %collective-permute-start.19 = (bf16[1,8,288,128]{3,2,1,0:T(8,128)(2,1)S(1)}, bf16[1,8,288,128]{3,2,1,0:T(8,128)(2,1)S(1)}, u32[]{:S(2)}, u32[]{:S(2)}) collective-permute-start(bf16[1,8,288,128]{3,2,1,0:T(8,128)(2,1)S(1)} %bitcast.31), channel_id=1, source_target_pairs={{0,16},{2,18},{4,20},{6,22},{8,24},{10,26},{12,28},{14,30},{16,0},... | collective-permute-start | bytes 1769480 | tf_op jit(solution)/shard_map/ppermute | solution.py:30
  37.0 14.6 %collective-permute-start.6 = (bf16[48,2176]{1,0:T(8,128)(2,1)S(1)}, bf16[48,2176]{1,0:T(8,128)(2,1)}, u32[]{:S(2)}, u32[]{:S(2)}) collective-permute-start(bf16[48,2176]{1,0:T(8,128)(2,1)S(1)} %slice.13), channel_id=1, source_target_pairs={{0,4},{2,6},{4,0},{6,2},{8,12},{10,14},{12,8},{14,10},{16,20},{18,... | collective-permute-start | bytes 626696 | tf_op jit(solution)/shard_map/ppermute | solution.py:30
  38.4 15.0 %collective-permute-start.5 = (bf16[80,2176]{1,0:T(8,128)(2,1)}, bf16[80,2176]{1,0:T(8,128)(2,1)}, u32[]{:S(2)}, u32[]{:S(2)}) collective-permute-start(bf16[80,2176]{1,0:T(8,128)(2,1)} %slice.12), channel_id=1, source_target_pairs={{0,1},{1,0},{2,3},{3,2},{4,5},{5,4},{6,7},{7,6},{8,9},{9,8},{10,11... | collective-permute-start | bytes 1044488 | tf_op jit(solution)/shard_map/ppermute | solution.py:30
  51.6 14.2 %collective-permute-start.14 = (bf16[128,2176]{1,0:T(8,128)(2,1)S(1)}, bf16[128,2176]{1,0:T(8,128)(2,1)}, u32[]{:S(2)}, u32[]{:S(2)}) collective-permute-start(bf16[128,2176]{1,0:T(8,128)(2,1)S(1)} %collective-permute-done.4.refs_5_), channel_id=1, source_target_pairs={{0,2},{2,0},{4,6},{6,4},{8,10},{10,8},{12,14},{14,12},{16,18},{18,... | collective-permute-start | bytes 1671176 | tf_op jit(solution)/shard_map/ppermute | solution.py:30
  53.4 9.4 %collective-permute-start.15 = (bf16[80,2176]{1,0:T(8,128)(2,1)}, bf16[80,2176]{1,0:T(8,128)(2,1)S(1)}, u32[]{:S(2)}, u32[]{:S(2)}) collective-permute-start(bf16[80,2176]{1,0:T(8,128)(2,1)} %collective-permute-done.5.refs_6_), channel_id=1, source_target_pairs={{0,2},{2,0},{4,6},{6,4},{8,10},{10,8},{12,14},{14,12},{16,18},{18,... | collective-permute-start | bytes 1044488 | tf_op jit(solution)/shard_map/ppermute | solution.py:30
  53.4 8.8 %collective-permute-start.8 = (bf16[48,2176]{1,0:T(8,128)(2,1)S(1)}, bf16[48,2176]{1,0:T(8,128)(2,1)S(1)}, u32[]{:S(2)}, u32[]{:S(2)}) collective-permute-start(bf16[48,2176]{1,0:T(8,128)(2,1)S(1)} %slice.17), channel_id=1, source_target_pairs={{0,4},{2,6},{4,0},{6,2},{8,12},{10,14},{12,8},{14,10},{16,20},{18,... | collective-permute-start | bytes 626696 | tf_op jit(solution)/shard_map/ppermute | solution.py:30
  55.0 10.3 %collective-permute-start.7 = (bf16[80,2176]{1,0:T(8,128)(2,1)S(1)}, bf16[80,2176]{1,0:T(8,128)(2,1)S(1)}, u32[]{:S(2)}, u32[]{:S(2)}) collective-permute-start(bf16[80,2176]{1,0:T(8,128)(2,1)S(1)} %slice.16), channel_id=1, source_target_pairs={{0,1},{1,0},{2,3},{3,2},{4,5},{5,4},{6,7},{7,6},{8,9},{9,8},{10,11... | collective-permute-start | bytes 1044488 | tf_op jit(solution)/shard_map/ppermute | solution.py:30
  96.3 24.9 %all-to-all-start.1 = ((bf16[16,96,128]{2,1,0:T(8,128)(2,1)}), bf16[16,96,128]{2,1,0:T(8,128)(2,1)S(1)}, u32[]{:S(2)}, u32[]{:S(2)}) async-start(bf16[16,96,128]{2,1,0:T(8,128)(2,1)} %local_tree.3), calls=%async_computation.1 | async-start | bytes 786432 | tf_op jit(solution)/shard_map/all_to_all | solution.py:465
  101.1 13.7 %collective-permute-start.23 = (bf16[96,1024]{1,0:T(8,128)(2,1)S(1)}, bf16[96,1024]{1,0:T(8,128)(2,1)S(1)}, u32[]{:S(2)}, u32[]{:S(2)}) collective-permute-start(bf16[96,1024]{1,0:T(8,128)(2,1)S(1)} %copy-done.8), channel_id=1, source_target_pairs={{0,8},{2,10},{4,12},{6,14},{8,0},{10,2},{12,4},{14,6},{16,24},{18,... | collective-permute-start | bytes 589832 | tf_op jit(solution)/shard_map/ppermute | solution.py:30
  103.1 13.1 %collective-permute-start.24 = (bf16[96,1024]{1,0:T(8,128)(2,1)S(1)}, bf16[96,1024]{1,0:T(8,128)(2,1)S(1)}, u32[]{:S(2)}, u32[]{:S(2)}) collective-permute-start(bf16[96,1024]{1,0:T(8,128)(2,1)S(1)} %copy-done.8), channel_id=1, source_target_pairs={{0,4},{2,6},{4,0},{6,2},{8,12},{10,14},{12,8},{14,10},{16,20},{18,... | collective-permute-start | bytes 589832 | tf_op jit(solution)/shard_map/ppermute | solution.py:30
  121.9 29.6 %all-to-all-start.2 = ((bf16[16,192,128]{2,1,0:T(8,128)(2,1)}), bf16[16,192,128]{2,1,0:T(8,128)(2,1)S(1)}, u32[]{:S(2)}, u32[]{:S(2)}) async-start(bf16[16,192,128]{2,1,0:T(8,128)(2,1)} %local_tree.2), calls=%async_computation.2 | async-start | bytes 1572864 | tf_op jit(solution)/shard_map/all_to_all | solution.py:465
  126.7 33.4 %collective-permute-start.34 = (bf16[96,1024]{1,0:T(8,128)(2,1)}, bf16[96,1024]{1,0:T(8,128)(2,1)}, u32[]{:S(2)}, u32[]{:S(2)}) collective-permute-start(bf16[96,1024]{1,0:T(8,128)(2,1)} %copy-done.7), channel_id=1, source_target_pairs={{0,2},{2,0},{4,6},{6,4},{8,10},{10,8},{12,14},{14,12},{16,18},{18,... | collective-permute-start | bytes 589832 | tf_op jit(solution)/shard_map/ppermute | solution.py:30
  127.1 32.9 %collective-permute-start.36 = (bf16[96,1024]{1,0:T(8,128)(2,1)}, bf16[96,1024]{1,0:T(8,128)(2,1)}, u32[]{:S(2)}, u32[]{:S(2)}) collective-permute-start(bf16[96,1024]{1,0:T(8,128)(2,1)} %copy-done.12), channel_id=1, source_target_pairs={{0,2},{2,0},{4,6},{6,4},{8,10},{10,8},{12,14},{14,12},{16,18},{18,... | collective-permute-start | bytes 589832 | tf_op jit(solution)/shard_map/ppermute | solution.py:30
  127.3 32.8 %collective-permute-start.35 = (bf16[96,1024]{1,0:T(8,128)(2,1)}, bf16[96,1024]{1,0:T(8,128)(2,1)}, u32[]{:S(2)}, u32[]{:S(2)}) collective-permute-start(bf16[96,1024]{1,0:T(8,128)(2,1)} %copy-done.10), channel_id=1, source_target_pairs={{0,2},{2,0},{4,6},{6,4},{8,10},{10,8},{12,14},{14,12},{16,18},{18,... | collective-permute-start | bytes 589832 | tf_op jit(solution)/shard_map/ppermute | solution.py:30
  140.5 7.1 %collective-permute-start.29 = (f32[2,2]{1,0:T(2,128)S(1)}, f32[2,2]{1,0:T(2,128)S(1)}, u32[]{:S(2)}, u32[]{:S(2)}) collective-permute-start(f32[2,2]{1,0:T(2,128)S(1)} %add.44), channel_id=1, source_target_pairs={{0,16},{2,18},{4,20},{6,22},{8,24},{10,26},{12,28},{14,30},{16,0},... | collective-permute-start | bytes 56 | tf_op jit(solution)/shard_map/ppermute | solution.py:30
  149.7 10.4 %collective-permute-start.38 = (bf16[1,128,768]{2,1,0:T(8,128)(2,1)}, bf16[1,128,768]{2,1,0:T(8,128)(2,1)}, u32[]{:S(2)}, u32[]{:S(2)}) collective-permute-start(bf16[1,128,768]{2,1,0:T(8,128)(2,1)} %bitcast.20.refs_8_), channel_id=1, source_target_pairs={{0,16},{2,18},{4,20},{6,22},{8,24},{10,26},{12,28},{14,30},{16,0},... | collective-permute-start | bytes 589832 | tf_op jit(solution)/shard_map/ppermute | solution.py:30
  163.0 21.3 %all-to-all-start.3 = ((bf16[16,64,256]{2,1,0:T(8,128)(2,1)}), bf16[16,64,256]{2,1,0:T(8,128)(2,1)}, u32[]{:S(2)}, u32[]{:S(2)}) async-start(bf16[16,64,256]{2,1,0:T(8,128)(2,1)} %bitcast.33), calls=%async_computation.3 | async-start | bytes 1048576 | tf_op jit(solution)/shard_map/all_to_all | solution.py:494
  167.2 8.7 %collective-permute-start.32 = (f32[4,2]{1,0:T(4,128)S(1)}, f32[4,2]{1,0:T(4,128)S(1)}, u32[]{:S(2)}, u32[]{:S(2)}) collective-permute-start(f32[4,2]{1,0:T(4,128)S(1)} %add.47), channel_id=1, source_target_pairs={{0,8},{2,10},{4,12},{6,14},{8,0},{10,2},{12,4},{14,6},{16,24},{18,... | collective-permute-start | bytes 104 | tf_op jit(solution)/shard_map/ppermute | solution.py:30
  (35 other events, 215.5 us)

commit v3 on v2

--- a/solution.py
+++ b/solution.py
@@ -71,8 +71,8 @@
     return pieces, weights, ids
 
 
-def tree_sum(value, bits, first=0):
-    for bit in range(first, bits):
+def tree_sum(value, bits):
+    for bit in bits:
         value = value + swapped(value, "dp", bit)
     return value
 
@@ -213,16 +213,14 @@
     gram_ref[...] = gram
 
 
-def vector_kernel(group, mats, idx_ref, gram_ref, in_ref, *refs):
-    factors, out_ref = refs[:-1], refs[-1]
-    part, total = factors[0].shape
+def vector_kernel(group, idx_ref, gram_ref, x_ref, y_ref, dgate_ref, dup_ref, hid_ref, out_ref):
+    part, total = hid_ref.shape
     rows = total // group
     count, _, block_rows = out_ref.shape
     width = count * block_rows
     slot = idx_ref[0]
-    scaled = []
-    for m, ref in zip(mats, factors):
-
+
+    def scaled(m, ref):
         def entry(i, j):
             a, b = slot ^ i, slot ^ j
             value = gram_ref[m * group + a, b]
@@ -231,36 +229,41 @@
             return jnp.full((1, rows), value, f32)
 
         weights = tree_weights(entry, group)
-        scaled.append(
-            jnp.concatenate(
-                [
-                    (ref[:, d * rows : (d + 1) * rows].astype(f32) * weights[d]).astype(bf16)
-                    for d in range(group)
-                ],
-                axis=1,
-            )
+        return jnp.concatenate(
+            [
+                (ref[:, d * rows : (d + 1) * rows].astype(f32) * weights[d]).astype(bf16)
+                for d in range(group)
+            ],
+            axis=1,
         )
-    left = jnp.concatenate(scaled, axis=0)
-    vector = jnp.dot(left, in_ref[:, :width], preferred_element_type=f32).astype(bf16)
+
+    pair = jnp.concatenate([scaled(0, dgate_ref), scaled(1, dup_ref)], axis=0)
+    vectors = (
+        jnp.dot(pair, x_ref[:, :width], preferred_element_type=f32).astype(bf16),
+        jnp.dot(scaled(2, hid_ref), y_ref[:, :width], preferred_element_type=f32).astype(bf16),
+    )
     for i in range(count):
-        out_ref[i] = vector[:, i * block_rows : (i + 1) * block_rows]
-
-
-def update_kernel(group, mats, gram_ref, got_ref, *refs):
+        lanes = slice(i * block_rows, (i + 1) * block_rows)
+        out_ref[i, : 2 * part, :] = vectors[0][:, lanes]
+        out_ref[i, 2 * part :, :] = vectors[1][:, lanes]
+
+
+def update_kernel(group, mats, start, gram_ref, got_ref, *refs):
     masters = refs[:mats]
     first_ref, second_ref = refs[mats : mats + 2]
     outs = refs[-5:] if mats == 1 else refs[-4:]
     sum_ref, new_ref, new_first_ref, new_second_ref = outs[:4]
     outer = got_ref.shape[0] // group
     block_rows = got_ref.shape[2]
-    part = got_ref.shape[1] // mats
+    part = got_ref.shape[1] // 3
     for m in range(mats):
-        entry = lambda i, j: jnp.full((1, block_rows), gram_ref[m * outer + i, j], f32)
+        n = start + m
+        entry = lambda i, j: jnp.full((1, block_rows), gram_ref[n * outer + i, j], f32)
         weights = tree_weights(entry, outer)
         total = 0.0
         for o in range(outer):
             held = [
-                got_ref[o * group + s, m * part : (m + 1) * part, :].astype(f32)
+                got_ref[o * group + s, n * part : (n + 1) * part, :].astype(f32)
                 for s in range(group)
             ]
             total = total + weights[o] * jnp.concatenate(held, axis=0)
@@ -419,31 +422,37 @@
         name="forward_and_gram",
         vmem=5 * rows_bytes // 2 + 3 * weight_bytes + 4 * total * total * (outer // 4),
     )
-    gram = tree_sum(gram, inner_bits)
-
-    def local_vector(left, mats, factors):
-        return call(
-            functools.partial(vector_kernel, group, mats),
-            sds((dp, len(mats) * part, block_rows), bf16),
-            (my_ids, gram, left, *factors),
-            [smem_space] * 2 + [vmem_space] * (1 + len(factors)),
-            vmem=rows_bytes + 3 * len(mats) * 4 * part * width + 4 * mebi,
-            name="local_tree",
-        )
-
-    def last_gram(got, mats):
-        wide = got.reshape(outer, group, mats, part, block_rows).transpose(2, 0, 1, 3, 4)
-        wide = wide.reshape(mats, outer, hidden_width, block_rows).astype(f32)
-        if outer > 2:
-            products = jnp.einsum("miab,mjab->mij", wide, wide, precision=lax.Precision.HIGHEST)
-        else:
-            products = (wide[:, :, None] * wide[:, None]).sum((3, 4))
-        return tree_sum(products.reshape(mats * outer, outer), half)
-
-    def update(got, products, mats, start, olds, previous):
-        block = pl.BlockSpec((mats, block_rows, hidden_width), lambda i: (start, 0, 0))
+    gram = tree_sum(gram, range(inner_bits - 1))
+    hidden_parts = [hidden_own]
+    for bit in reversed(range(1, inner_bits)):
+        hidden_parts += [swapped(piece, "dp", bit) for piece in hidden_parts]
+        gram = after(gram, hidden_parts[1]) if bit == inner_bits - 1 else gram
+    gram = tree_sum(gram, range(inner_bits - 1, inner_bits))
+
+    vector = call(
+        functools.partial(vector_kernel, group),
+        sds((dp, 3 * part, block_rows), bf16),
+        (my_ids, gram, token_all, grad_all, d_gate, d_up, hidden),
+        [smem_space] * 2 + [vmem_space] * 5,
+        name="local_tree",
+        vmem=5 * rows_bytes // 4 + 2 * weight_bytes + 8 * mebi,
+    )
+    got = lax.all_to_all(vector, "dp", 0, 0, tiled=True)
+    hidden_parts = [after(piece, got) for piece in hidden_parts]
+    hidden_parts += [swapped(piece, "dp", 0) for piece in hidden_parts]
+    leaves = got.reshape(outer, group, 3, part, block_rows).transpose(2, 0, 1, 3, 4)
+    leaves = leaves.reshape(3, outer, hidden_width, block_rows).astype(f32)
+    if outer > 2:
+        products = jnp.einsum("miab,mjab->mij", leaves, leaves, precision=lax.Precision.HIGHEST)
+    else:
+        products = (leaves[:, :, None] * leaves[:, None]).sum((3, 4))
+    products = tree_sum(products.reshape(3 * outer, outer), range(dp_bits))
+
+    def update(mats, start, olds, previous):
+        place = lambda i: (start // mats, 0, 0)
+        block = pl.BlockSpec((mats, block_rows, hidden_width), place)
         whole = sds((3, block_rows, hidden_width), f32)
-        kernel = functools.partial(update_kernel, group, mats)
+        kernel = functools.partial(update_kernel, group, mats, start)
         outs, out_specs = (whole,) * 4, (block,) * 4
         if mats == 1:
             outs += (sds((block_rows, hidden_width), bf16),)
@@ -460,24 +469,11 @@
             vmem=4 * got.shape[0] * got.shape[1] * 256 + 10 * mebi,
         )
 
-    down_vector = local_vector(grad_all, (2,), [hidden])
-    pair_vector = local_vector(token_all, (0, 1), [d_gate, d_up])
-    exchange_rows = lambda vector: lax.all_to_all(vector, "dp", 0, 0, tiled=True)
-    down_got = exchange_rows(after(down_vector, pair_vector))
-    hidden_parts = [after(hidden_own, pair_vector)]
-    for bit in reversed(range(inner_bits)):
-        hidden_parts += [swapped(piece, "dp", bit) for piece in hidden_parts]
-    half = inner_bits - 1
-    down_gram = tree_sum(last_gram(down_got, 1), dp_bits, half)
-    pair_got = exchange_rows(after(pair_vector, down_got, *hidden_parts[: group // 2]))
-    *partial_out, new_down = update(down_got, down_gram, 1, 2, masters[2:], ())
-    pair_gram = last_gram(after(pair_got, new_down), 2)
+    *partial_out, new_down = update(1, 2, masters[2:], ())
     downs = [new_down[None]]
     for bit in range(outer_bits):
         downs = [jnp.concatenate(downs)] if len(downs) > 1 else downs
         downs = [downs[0], swapped(downs[0], "dp", inner_bits + bit)]
-    downs[-1] = after(downs[-1], pair_gram)
-    pair_gram = tree_sum(pair_gram, dp_bits, half)
     slot_outputs = call(
         functools.partial(project_kernel, group),
         sds((group, experts, pool, outer * block_rows), bf16),
@@ -494,7 +490,7 @@
     columns = lax.all_to_all(
         slot_outputs, ("dp", "expert"), 0, 0, axis_index_groups=cubes, tiled=True
     )
-    outs = update(pair_got, pair_gram, 2, 0, masters[:2], partial_out)
+    outs = update(2, 0, masters[:2], partial_out)
     forward = call(
         functools.partial(finish_kernel, experts, block_rows),
         sds((pool, width), bf16),

time: 187 us -> 175 us (0.936)
  starting transfers between devices: 58.1 us -> 50.1 us
  waiting for transfers between devices: 91.8 us -> 88.8 us
    ppermute x39 -> x35, waiting for transfers between devices: 91.8 us -> 76.8 us  [swapped(): lax.ppermute(array, axis, [(i, i ^ 1 << bit) for i in range(lax.axis_size...]
    all_to_all x2 -> x1, waiting for transfers between devices: 0.01 us -> 7.73 us  [shards(): got = lax.all_to_all(vector, 'dp', 0, 0, tiled=True)]
    all_to_all x2 -> x1, starting transfers between devices: 9.52 us -> 4.78 us  [shards(): got = lax.all_to_all(vector, 'dp', 0, 0, tiled=True)]
    all_to_all x1, waiting for transfers between devices: 0.01 us -> 4.23 us  [shards(): lax.all_to_all(slot_outputs, ('dp', 'expert'), 0, 0, axis_index_groups=cu...]
    ppermute x39 -> x35, starting transfers between devices: 39 us -> 35.7 us  [swapped(): lax.ppermute(array, axis, [(i, i ^ 1 << bit) for i in range(lax.axis_size...]
    pallas_call x8 -> x7, Pallas kernels: 28.7 us -> 27.6 us  [call(): pl.pallas_call(kernel, out_shape=outs, grid=grid, in_specs=in_specs, out_...]
    unnamed x32 -> x16, local copies, waits for them, and re-layouts: 3.56 us -> 3.81 us
  transfers between devices with their start and end apart: 43 -> 38, of which waited for: 25 -> 23; matrix products, arithmetic and copies ran while one was open for 1% -> 1% of each run, Pallas kernels for 3% -> 3%
where the time goes in v3:
time: 175 us; the launch traced here: 174 us
  waiting for transfers between devices  88.8 us (51%)
  starting transfers between devices  50.1 us (29%)
  Pallas kernels  27.6 us (16%)
  local copies, waits for them, and re-layouts  6.21 us (4%)
    ppermute x35, waiting for transfers between devices, swapped(): lax.ppermute(array, axis, [(i, i ^ 1 << bit) for i in range(lax.axis_size...  76.8 us
    ppermute x35, starting transfers between devices, swapped(): lax.ppermute(array, axis, [(i, i ^ 1 << bit) for i in range(lax.axis_size...  35.7 us
    pallas_call x7, Pallas kernels, call(): pl.pallas_call(kernel, out_shape=outs, grid=grid, in_specs=in_specs, out_...  27.6 us
    all_to_all x1, waiting for transfers between devices, shards(): got = lax.all_to_all(vector, 'dp', 0, 0, tiled=True)  7.73 us
    all_to_all x1, starting transfers between devices, shards(): lax.all_to_all(sent, 'dp', 0, 0, axis_index_groups=groups, tiled=True)  5.39 us
    all_to_all x1, starting transfers between devices, shards(): got = lax.all_to_all(vector, 'dp', 0, 0, tiled=True)  4.78 us
    all_to_all x1, starting transfers between devices, shards(): lax.all_to_all(slot_outputs, ('dp', 'expert'), 0, 0, axis_index_groups=cu...  4.25 us
    all_to_all x1, waiting for transfers between devices, shards(): lax.all_to_all(slot_outputs, ('dp', 'expert'), 0, 0, axis_index_groups=cu...  4.23 us
  transfers between devices with their start and end apart: 38, of which 23 were waited for; matrix products, arithmetic and copies ran while one was open for 1% of the time, Pallas kernels for 3%

profile of v3, /device:TPU:0, one launch (start us, length us, event | category | flops | bytes accessed | tf_op | source)
XLA Modules:
  0.0 174.2 jit_solution(2437496062407738941)
XLA Ops:
  1.9 2.7 %prepare.1 = (bf16[128,2176]{1,0:T(8,128)(2,1)}, bf16[8,288,128]{2,1,0:T(8,128)(2,1)}) custom-call(s32[2,64]{1,0:T(2,128)} %reshape.35.route_ref, s32[1,2]{1,0:T(1,128)} %counts_ref.1, bf16[64,2048]{1,0:T(8,128)(2,1)} %tok_ref.1, bf16[64,2048]{1,0:T(8,128)(2,1)} %cot_ref.1, f32[128,768]{1,0:T(8,128)} %bitcast.28, f32[128,768]{1,0:T(8,128)} %bitcast.30, ...), custom_call_target="tpu_custom_call" | custom-call | tf_op jit(solution)/shard_map/prepare/pallas_call | solution.py:324
  4.6 5.4 %all-to-all-start = ((bf16[8,288,128]{2,1,0:T(8,128)(2,1)}), bf16[8,288,128]{2,1,0:T(8,128)(2,1)S(1)}, u32[]{:S(2)}, u32[]{:S(2)}) async-start(bf16[8,288,128]{2,1,0:T(8,128)(2,1)} %get-tuple-element.38), calls=%async_computation | async-start | bytes 1179648 | tf_op jit(solution)/shard_map/all_to_all | solution.py:384
  15.0 10.1 %collective-permute-done.2.refs_3_ = bf16[128,2176]{1,0:T(8,128)(2,1)S(1)} collective-permute-done((bf16[128,2176]{1,0:T(8,128)(2,1)S(1)}, bf16[128,2176]{1,0:T(8,128)(2,1)S(1)}, u32[]{:S(2)}, u32[]{:S(2)}) %collective-permute-start.2) | collective-permute-done | bytes 557088 | tf_op jit(solution)/shard_map/ppermute | solution.py:30
  25.0 6.4 %collective-permute-done.1.refs_2_ = bf16[128,2176]{1,0:T(8,128)(2,1)S(1)} collective-permute-done((bf16[128,2176]{1,0:T(8,128)(2,1)S(1)}, bf16[128,2176]{1,0:T(8,128)(2,1)S(1)}, u32[]{:S(2)}, u32[]{:S(2)}) %collective-permute-start.1) | collective-permute-done | bytes 557088 | tf_op jit(solution)/shard_map/ppermute | solution.py:30
  34.5 2.6 %collective-permute-start.19 = (bf16[1,8,288,128]{3,2,1,0:T(8,128)(2,1)S(1)}, bf16[1,8,288,128]{3,2,1,0:T(8,128)(2,1)S(1)}, u32[]{:S(2)}, u32[]{:S(2)}) collective-permute-start(bf16[1,8,288,128]{3,2,1,0:T(8,128)(2,1)S(1)} %bitcast.25), channel_id=1, source_target_pairs={{0,16},{2,18},{4,20},{6,22},{8,24},{10,26},{12,28},{14,30},{16,0},... | collective-permute-start | bytes 1769480 | tf_op jit(solution)/shard_map/ppermute | solution.py:30
  39.1 12.7 %collective-permute-done.6.refs_7_ = bf16[48,2176]{1,0:T(8,128)(2,1)} collective-permute-done((bf16[48,2176]{1,0:T(8,128)(2,1)S(1)}, bf16[48,2176]{1,0:T(8,128)(2,1)}, u32[]{:S(2)}, u32[]{:S(2)}) %collective-permute-start.6) | collective-permute-done | bytes 208928 | tf_op jit(solution)/shard_map/ppermute | solution.py:30
  56.7 5.6 %collective-permute-done.19.refs_21_ = bf16[1,8,288,128]{3,2,1,0:T(8,128)(2,1)S(1)} collective-permute-done((bf16[1,8,288,128]{3,2,1,0:T(8,128)(2,1)S(1)}, bf16[1,8,288,128]{3,2,1,0:T(8,128)(2,1)S(1)}, u32[]{:S(2)}, u32[]{:S(2)}) %collective-permute-start.19) | collective-permute-done | bytes 589856 | tf_op jit(solution)/shard_map/ppermute | solution.py:30
  63.0 2.5 %collective-permute-done.7.refs_8_ = bf16[80,2176]{1,0:T(8,128)(2,1)S(1)} collective-permute-done((bf16[80,2176]{1,0:T(8,128)(2,1)S(1)}, bf16[80,2176]{1,0:T(8,128)(2,1)S(1)}, u32[]{:S(2)}, u32[]{:S(2)}) %collective-permute-start.7) | collective-permute-done | bytes 348192 | tf_op jit(solution)/shard_map/ppermute | solution.py:30
  69.5 12.3 %forward_and_gram.1 = (bf16[96,1024]{1,0:T(8,128)(2,1)S(1)}, bf16[96,1024]{1,0:T(8,128)(2,1)}, bf16[96,1024]{1,0:T(8,128)(2,1)S(1)}, bf16[96,1024]{1,0:T(8,128)(...) custom-call(s32[3]{0:T(128)S(1)} %pad_add_fusion.idx_ref, ...), custom_call_target="tpu_custom_call" | custom-call | tf_op jit(solution)/shard_map/forward_and_gram/pallas_call | solution.py:324
  84.9 2.5 %collective-permute-done.21 = f32[24,128]{1,0:T(8,128)S(1)} collective-permute-done((f32[24,128]{1,0:T(8,128)S(1)}, f32[24,128]{1,0:T(8,128)S(1)}, u32[]{:S(2)}, u32[]{:S(2)}) %collective-permute-start.21) | collective-permute-done | bytes 12320 | tf_op jit(solution)/shard_map/ppermute | solution.py:30
  89.9 2.9 %collective-permute-done.23 = f32[24,128]{1,0:T(8,128)S(1)} collective-permute-done((f32[24,128]{1,0:T(8,128)S(1)}, f32[24,128]{1,0:T(8,128)S(1)}, u32[]{:S(2)}, u32[]{:S(2)}) %collective-permute-start.23) | collective-permute-done | bytes 12320 | tf_op jit(solution)/shard_map/ppermute | solution.py:30
  92.8 3.6 %local_tree.1 = bf16[16,288,128]{2,1,0:T(8,128)(2,1)} custom-call(s32[3]{0:T(128)S(1)} %pad_add_fusion.idx_ref, f32[24,128]{1,0:T(8,128)S(1)} %add.29.gram_ref, bf16[1024,2048]{1,0:T(8,128)(2,1)S(1)} %get-tuple-element.51.x_ref, bf16[1024,2176]{1,0:T(8,128)(2,1)S(1)} %get-tuple-element.52.y_ref, bf16[96,1024]{1,0:T(8,128)(2,1)S(1)} %get-tuple-element.53.dgate_ref, ...), custom_call_target="tpu_custom_call" | custom-call | tf_op jit(solution)/shard_map/local_tree/pallas_call | solution.py:324
  96.4 4.8 %all-to-all-start.1 = ((bf16[16,288,128]{2,1,0:T(8,128)(2,1)}), bf16[16,288,128]{2,1,0:T(8,128)(2,1)S(1)}, u32[]{:S(2)}, u32[]{:S(2)}) async-start(bf16[16,288,128]{2,1,0:T(8,128)(2,1)} %local_tree.1), calls=%async_computation.1 | async-start | bytes 2359296 | tf_op jit(solution)/shard_map/all_to_all | solution.py:440
  103.3 15.3 %collective-permute-done.28.refs_2_ = bf16[96,1024]{1,0:T(8,128)(2,1)} collective-permute-done((bf16[96,1024]{1,0:T(8,128)(2,1)}, bf16[96,1024]{1,0:T(8,128)(2,1)}, u32[]{:S(2)}, u32[]{:S(2)}) %collective-permute-start.28) | collective-permute-done | bytes 196640 | tf_op jit(solution)/shard_map/ppermute | solution.py:30
  118.6 7.7 %all-to-all-done.1.got_ref = bf16[16,288,128]{2,1,0:T(8,128)(2,1)S(1)} async-done(((bf16[16,288,128]{2,1,0:T(8,128)(2,1)}), bf16[16,288,128]{2,1,0:T(8,128)(2,1)S(1)}, u32[]{:S(2)}, u32[]{:S(2)}) %all-to-all-start.1) | async-done | bytes 1179680 | tf_op jit(solution)/shard_map/all_to_all | solution.py:440
  129.8 2.1 %collective-permute-start.25 = (f32[6,2]{1,0:T(8,128)S(1)}, f32[6,2]{1,0:T(8,128)S(1)}, u32[]{:S(2)}, u32[]{:S(2)}) collective-permute-start(f32[6,2]{1,0:T(8,128)S(1)} %add.30), channel_id=1, source_target_pairs={{0,4},{2,6},{4,0},{6,2},{8,12},{10,14},{12,8},{14,10},{16,20},{18,... | collective-permute-start | bytes 152 | tf_op jit(solution)/shard_map/ppermute | solution.py:30
  133.5 3.6 %collective-permute-start.26 = (f32[6,2]{1,0:T(8,128)S(1)}, f32[6,2]{1,0:T(8,128)S(1)}, u32[]{:S(2)}, u32[]{:S(2)}) collective-permute-start(f32[6,2]{1,0:T(8,128)S(1)} %add.31), channel_id=1, source_target_pairs={{0,8},{2,10},{4,12},{6,14},{8,0},{10,2},{12,4},{14,6},{16,24},{18,... | collective-permute-start | bytes 152 | tf_op jit(solution)/shard_map/ppermute | solution.py:30
  138.7 3.6 %collective-permute-start.27 = (f32[6,2]{1,0:T(8,128)S(1)}, f32[6,2]{1,0:T(8,128)S(1)}, u32[]{:S(2)}, u32[]{:S(2)}) collective-permute-start(f32[6,2]{1,0:T(8,128)S(1)} %add.32), channel_id=1, source_target_pairs={{0,16},{2,18},{4,20},{6,22},{8,24},{10,26},{12,28},{14,30},{16,0},... | collective-permute-start | bytes 152 | tf_op jit(solution)/shard_map/ppermute | solution.py:30
  146.9 2.9 %collective-permute-start.34 = (bf16[1,128,768]{2,1,0:T(8,128)(2,1)S(1)}, bf16[1,128,768]{2,1,0:T(8,128)(2,1)S(1)}, u32[]{:S(2)}, u32[]{:S(2)}) collective-permute-start(bf16[1,128,768]{2,1,0:T(8,128)(2,1)S(1)} %bitcast.34), channel_id=1, source_target_pairs={{0,16},{2,18},{4,20},{6,22},{8,24},{10,26},{12,28},{14,30},{16,0},... | collective-permute-start | bytes 589832 | tf_op jit(solution)/shard_map/ppermute | solution.py:30
  149.9 6.0 %collective-permute-done.34.refs_9_ = bf16[1,128,768]{2,1,0:T(8,128)(2,1)S(1)} collective-permute-done((bf16[1,128,768]{2,1,0:T(8,128)(2,1)S(1)}, bf16[1,128,768]{2,1,0:T(8,128)(2,1)S(1)}, u32[]{:S(2)}, u32[]{:S(2)}) %collective-permute-start.34) | collective-permute-done | bytes 196640 | tf_op jit(solution)/shard_map/ppermute | solution.py:30
  155.8 2.2 %project.1 = bf16[8,2,64,256]{3,2,1,0:T(8,128)(2,1)S(1)} custom-call(s32[3]{0:T(128)S(1)} %pad_add_fusion.idx_ref, bf16[96,1024]{1,0:T(8,128)(2,1)} %get-tuple-element.64.refs_0_, bf16[96,1024]{1,0:T(8,128)(2,1)} %collective-permute-done.22.refs_1_, bf16[96,1024]{1,0:T(8,128)(2,1)} %collective-permute-done.28.refs_2_, ...), custom_call_target="tpu_custom_call" | custom-call | tf_op jit(solution)/shard_map/project/pallas_call | solution.py:324
  158.9 4.2 %all-to-all-start.2 = ((bf16[16,64,256]{2,1,0:T(8,128)(2,1)}), bf16[16,64,256]{2,1,0:T(8,128)(2,1)}, u32[]{:S(2)}, u32[]{:S(2)}) async-start(bf16[16,64,256]{2,1,0:T(8,128)(2,1)} %bitcast.27), calls=%async_computation.2 | async-start | bytes 1048576 | tf_op jit(solution)/shard_map/all_to_all | solution.py:490
  165.2 2.9 %update.3 = (f32[3,128,768]{2,1,0:T(8,128)}, f32[3,128,768]{2,1,0:T(8,128)}, f32[3,128,768]{2,1,0:T(8,128)}, f32[3,128,768]{2,1,0:T(8,128)}) custom-call(f32[6,2]{1,0:T(8,128)S(1)} %add.33.gram_ref, bf16[16,288,128]{2,1,0:T(8,128)(2,1)S(1)} %all-to-all-done.1.got_ref, ...), custom_call_target="tpu_custom_call", output_to_operand_aliasing={{0}: (6, {}), {1}: (7, {}), {2}: (8, {}), {3}: (9, {})} | custom-call | tf_op jit(solution)/shard_map/update/pallas_call | solution.py:324
  168.1 4.2 %all-to-all-done.2.got_ref = bf16[16,64,256]{2,1,0:T(8,128)(2,1)} async-done(((bf16[16,64,256]{2,1,0:T(8,128)(2,1)}), bf16[16,64,256]{2,1,0:T(8,128)(2,1)}, u32[]{:S(2)}, u32[]{:S(2)}) %all-to-all-start.2) | async-done | bytes 524320 | tf_op jit(solution)/shard_map/all_to_all | solution.py:490
  (91 shorter events, 44.3 us)
Async XLA Ops:
  4.6 27.0 %all-to-all-start = ((bf16[8,288,128]{2,1,0:T(8,128)(2,1)}), bf16[8,288,128]{2,1,0:T(8,128)(2,1)S(1)}, u32[]{:S(2)}, u32[]{:S(2)}) async-start(bf16[8,288,128]{2,1,0:T(8,128)(2,1)} %get-tuple-element.38), calls=%async_computation | async-start | bytes 1179648 | tf_op jit(solution)/shard_map/all_to_all | solution.py:384
  10.0 15.0 %collective-permute-start.2 = (bf16[128,2176]{1,0:T(8,128)(2,1)S(1)}, bf16[128,2176]{1,0:T(8,128)(2,1)S(1)}, u32[]{:S(2)}, u32[]{:S(2)}) collective-permute-start(bf16[128,2176]{1,0:T(8,128)(2,1)S(1)} %copy-done.6), channel_id=1, source_target_pairs={{0,1},{1,0},{2,3},{3,2},{4,5},{5,4},{6,7},{7,6},{8,9},{9,8},{10,11... | collective-permute-start | bytes 1671176 | tf_op jit(solution)/shard_map/ppermute | solution.py:30
  11.5 19.9 %collective-permute-start.1 = (bf16[128,2176]{1,0:T(8,128)(2,1)S(1)}, bf16[128,2176]{1,0:T(8,128)(2,1)S(1)}, u32[]{:S(2)}, u32[]{:S(2)}) collective-permute-start(bf16[128,2176]{1,0:T(8,128)(2,1)S(1)} %copy-done.6), channel_id=1, source_target_pairs={{0,4},{2,6},{4,0},{6,2},{8,12},{10,14},{12,8},{14,10},{16,20},{18,... | collective-permute-start | bytes 1671176 | tf_op jit(solution)/shard_map/ppermute | solution.py:30
  13.5 18.1 %collective-permute-start = (bf16[128,2176]{1,0:T(8,128)(2,1)S(1)}, bf16[128,2176]{1,0:T(8,128)(2,1)}, u32[]{:S(2)}, u32[]{:S(2)}) collective-permute-start(bf16[128,2176]{1,0:T(8,128)(2,1)S(1)} %copy-done.6), channel_id=1, source_target_pairs={{0,8},{2,10},{4,12},{6,14},{8,0},{10,2},{12,4},{14,6},{16,24},{18,... | collective-permute-start | bytes 1671176 | tf_op jit(solution)/shard_map/ppermute | solution.py:30
  31.6 20.2 %collective-permute-start.4 = (bf16[128,2176]{1,0:T(8,128)(2,1)}, bf16[128,2176]{1,0:T(8,128)(2,1)S(1)}, u32[]{:S(2)}, u32[]{:S(2)}) collective-permute-start(bf16[128,2176]{1,0:T(8,128)(2,1)} %collective-permute-done.refs_1_), channel_id=1, source_target_pairs={{0,1},{1,0},{2,3},{3,2},{4,5},{5,4},{6,7},{7,6},{8,9},{9,8},{10,11... | collective-permute-start | bytes 1671176 | tf_op jit(solution)/shard_map/ppermute | solution.py:30
  33.1 20.5 %collective-permute-start.3 = (bf16[128,2176]{1,0:T(8,128)(2,1)}, bf16[128,2176]{1,0:T(8,128)(2,1)S(1)}, u32[]{:S(2)}, u32[]{:S(2)}) collective-permute-start(bf16[128,2176]{1,0:T(8,128)(2,1)} %collective-permute-done.refs_1_), channel_id=1, source_target_pairs={{0,4},{2,6},{4,0},{6,2},{8,12},{10,14},{12,8},{14,10},{16,20},{18,... | collective-permute-start | bytes 1671176 | tf_op jit(solution)/shard_map/ppermute | solution.py:30
  34.5 27.9 %collective-permute-start.19 = (bf16[1,8,288,128]{3,2,1,0:T(8,128)(2,1)S(1)}, bf16[1,8,288,128]{3,2,1,0:T(8,128)(2,1)S(1)}, u32[]{:S(2)}, u32[]{:S(2)}) collective-permute-start(bf16[1,8,288,128]{3,2,1,0:T(8,128)(2,1)S(1)} %bitcast.25), channel_id=1, source_target_pairs={{0,16},{2,18},{4,20},{6,22},{8,24},{10,26},{12,28},{14,30},{16,0},... | collective-permute-start | bytes 1769480 | tf_op jit(solution)/shard_map/ppermute | solution.py:30
  37.1 14.6 %collective-permute-start.6 = (bf16[48,2176]{1,0:T(8,128)(2,1)S(1)}, bf16[48,2176]{1,0:T(8,128)(2,1)}, u32[]{:S(2)}, u32[]{:S(2)}) collective-permute-start(bf16[48,2176]{1,0:T(8,128)(2,1)S(1)} %slice.13), channel_id=1, source_target_pairs={{0,4},{2,6},{4,0},{6,2},{8,12},{10,14},{12,8},{14,10},{16,20},{18,... | collective-permute-start | bytes 626696 | tf_op jit(solution)/shard_map/ppermute | solution.py:30
  38.5 15.0 %collective-permute-start.5 = (bf16[80,2176]{1,0:T(8,128)(2,1)}, bf16[80,2176]{1,0:T(8,128)(2,1)}, u32[]{:S(2)}, u32[]{:S(2)}) collective-permute-start(bf16[80,2176]{1,0:T(8,128)(2,1)} %slice.12), channel_id=1, source_target_pairs={{0,1},{1,0},{2,3},{3,2},{4,5},{5,4},{6,7},{7,6},{8,9},{9,8},{10,11... | collective-permute-start | bytes 1044488 | tf_op jit(solution)/shard_map/ppermute | solution.py:30
  51.8 14.2 %collective-permute-start.14 = (bf16[128,2176]{1,0:T(8,128)(2,1)S(1)}, bf16[128,2176]{1,0:T(8,128)(2,1)}, u32[]{:S(2)}, u32[]{:S(2)}) collective-permute-start(bf16[128,2176]{1,0:T(8,128)(2,1)S(1)} %collective-permute-done.4.refs_5_), channel_id=1, source_target_pairs={{0,2},{2,0},{4,6},{6,4},{8,10},{10,8},{12,14},{14,12},{16,18},{18,... | collective-permute-start | bytes 1671176 | tf_op jit(solution)/shard_map/ppermute | solution.py:30
  53.5 9.4 %collective-permute-start.15 = (bf16[80,2176]{1,0:T(8,128)(2,1)}, bf16[80,2176]{1,0:T(8,128)(2,1)S(1)}, u32[]{:S(2)}, u32[]{:S(2)}) collective-permute-start(bf16[80,2176]{1,0:T(8,128)(2,1)} %collective-permute-done.5.refs_6_), channel_id=1, source_target_pairs={{0,2},{2,0},{4,6},{6,4},{8,10},{10,8},{12,14},{14,12},{16,18},{18,... | collective-permute-start | bytes 1044488 | tf_op jit(solution)/shard_map/ppermute | solution.py:30
  53.6 8.8 %collective-permute-start.8 = (bf16[48,2176]{1,0:T(8,128)(2,1)S(1)}, bf16[48,2176]{1,0:T(8,128)(2,1)S(1)}, u32[]{:S(2)}, u32[]{:S(2)}) collective-permute-start(bf16[48,2176]{1,0:T(8,128)(2,1)S(1)} %slice.17), channel_id=1, source_target_pairs={{0,4},{2,6},{4,0},{6,2},{8,12},{10,14},{12,8},{14,10},{16,20},{18,... | collective-permute-start | bytes 626696 | tf_op jit(solution)/shard_map/ppermute | solution.py:30
  55.1 10.3 %collective-permute-start.7 = (bf16[80,2176]{1,0:T(8,128)(2,1)S(1)}, bf16[80,2176]{1,0:T(8,128)(2,1)S(1)}, u32[]{:S(2)}, u32[]{:S(2)}) collective-permute-start(bf16[80,2176]{1,0:T(8,128)(2,1)S(1)} %slice.16), channel_id=1, source_target_pairs={{0,1},{1,0},{2,3},{3,2},{4,5},{5,4},{6,7},{7,6},{8,9},{9,8},{10,11... | collective-permute-start | bytes 1044488 | tf_op jit(solution)/shard_map/ppermute | solution.py:30
  81.8 7.3 %collective-permute-start.22 = (bf16[96,1024]{1,0:T(8,128)(2,1)}, bf16[96,1024]{1,0:T(8,128)(2,1)}, u32[]{:S(2)}, u32[]{:S(2)}) collective-permute-start(bf16[96,1024]{1,0:T(8,128)(2,1)} %get-tuple-element.64.refs_0_), channel_id=1, source_target_pairs={{0,8},{2,10},{4,12},{6,14},{8,0},{10,2},{12,4},{14,6},{16,24},{18,... | collective-permute-start | bytes 589832 | tf_op jit(solution)/shard_map/ppermute | solution.py:30
  96.4 29.9 %all-to-all-start.1 = ((bf16[16,288,128]{2,1,0:T(8,128)(2,1)}), bf16[16,288,128]{2,1,0:T(8,128)(2,1)S(1)}, u32[]{:S(2)}, u32[]{:S(2)}) async-start(bf16[16,288,128]{2,1,0:T(8,128)(2,1)} %local_tree.1), calls=%async_computation.1 | async-start | bytes 2359296 | tf_op jit(solution)/shard_map/all_to_all | solution.py:440
  101.2 17.4 %collective-permute-start.28 = (bf16[96,1024]{1,0:T(8,128)(2,1)}, bf16[96,1024]{1,0:T(8,128)(2,1)}, u32[]{:S(2)}, u32[]{:S(2)}) collective-permute-start(bf16[96,1024]{1,0:T(8,128)(2,1)} %get-tuple-element.64.refs_0_), channel_id=1, source_target_pairs={{0,4},{2,6},{4,0},{6,2},{8,12},{10,14},{12,8},{14,10},{16,20},{18,... | collective-permute-start | bytes 589832 | tf_op jit(solution)/shard_map/ppermute | solution.py:30
  103.1 24.5 %collective-permute-start.29 = (bf16[96,1024]{1,0:T(8,128)(2,1)}, bf16[96,1024]{1,0:T(8,128)(2,1)}, u32[]{:S(2)}, u32[]{:S(2)}) collective-permute-start(bf16[96,1024]{1,0:T(8,128)(2,1)} %collective-permute-done.22.refs_1_), channel_id=1, source_target_pairs={{0,4},{2,6},{4,0},{6,2},{8,12},{10,14},{12,8},{14,10},{16,20},{18,... | collective-permute-start | bytes 589832 | tf_op jit(solution)/shard_map/ppermute | solution.py:30
  126.3 23.5 %collective-permute-start.30 = (bf16[96,1024]{1,0:T(8,128)(2,1)}, bf16[96,1024]{1,0:T(8,128)(2,1)}, u32[]{:S(2)}, u32[]{:S(2)}) collective-permute-start(bf16[96,1024]{1,0:T(8,128)(2,1)} %get-tuple-element.64.refs_0_), channel_id=1, source_target_pairs={{0,2},{2,0},{4,6},{6,4},{8,10},{10,8},{12,14},{14,12},{16,18},{18,... | collective-permute-start | bytes 589832 | tf_op jit(solution)/shard_map/ppermute | solution.py:30
  127.1 22.7 %collective-permute-start.31 = (bf16[96,1024]{1,0:T(8,128)(2,1)}, bf16[96,1024]{1,0:T(8,128)(2,1)}, u32[]{:S(2)}, u32[]{:S(2)}) collective-permute-start(bf16[96,1024]{1,0:T(8,128)(2,1)} %collective-permute-done.22.refs_1_), channel_id=1, source_target_pairs={{0,2},{2,0},{4,6},{6,4},{8,10},{10,8},{12,14},{14,12},{16,18},{18,... | collective-permute-start | bytes 589832 | tf_op jit(solution)/shard_map/ppermute | solution.py:30
  127.1 22.7 %collective-permute-start.32 = (bf16[96,1024]{1,0:T(8,128)(2,1)}, bf16[96,1024]{1,0:T(8,128)(2,1)}, u32[]{:S(2)}, u32[]{:S(2)}) collective-permute-start(bf16[96,1024]{1,0:T(8,128)(2,1)} %collective-permute-done.28.refs_2_), channel_id=1, source_target_pairs={{0,2},{2,0},{4,6},{6,4},{8,10},{10,8},{12,14},{14,12},{16,18},{18,... | collective-permute-start | bytes 589832 | tf_op jit(solution)/shard_map/ppermute | solution.py:30
  127.6 22.2 %collective-permute-start.33 = (bf16[96,1024]{1,0:T(8,128)(2,1)}, bf16[96,1024]{1,0:T(8,128)(2,1)}, u32[]{:S(2)}, u32[]{:S(2)}) collective-permute-start(bf16[96,1024]{1,0:T(8,128)(2,1)} %collective-permute-done.29.refs_3_), channel_id=1, source_target_pairs={{0,2},{2,0},{4,6},{6,4},{8,10},{10,8},{12,14},{14,12},{16,18},{18,... | collective-permute-start | bytes 589832 | tf_op jit(solution)/shard_map/ppermute | solution.py:30
  133.5 5.2 %collective-permute-start.26 = (f32[6,2]{1,0:T(8,128)S(1)}, f32[6,2]{1,0:T(8,128)S(1)}, u32[]{:S(2)}, u32[]{:S(2)}) collective-permute-start(f32[6,2]{1,0:T(8,128)S(1)} %add.31), channel_id=1, source_target_pairs={{0,8},{2,10},{4,12},{6,14},{8,0},{10,2},{12,4},{14,6},{16,24},{18,... | collective-permute-start | bytes 152 | tf_op jit(solution)/shard_map/ppermute | solution.py:30
  146.9 8.9 %collective-permute-start.34 = (bf16[1,128,768]{2,1,0:T(8,128)(2,1)S(1)}, bf16[1,128,768]{2,1,0:T(8,128)(2,1)S(1)}, u32[]{:S(2)}, u32[]{:S(2)}) collective-permute-start(bf16[1,128,768]{2,1,0:T(8,128)(2,1)S(1)} %bitcast.34), channel_id=1, source_target_pairs={{0,16},{2,18},{4,20},{6,22},{8,24},{10,26},{12,28},{14,30},{16,0},... | collective-permute-start | bytes 589832 | tf_op jit(solution)/shard_map/ppermute | solution.py:30
  158.9 13.4 %all-to-all-start.2 = ((bf16[16,64,256]{2,1,0:T(8,128)(2,1)}), bf16[16,64,256]{2,1,0:T(8,128)(2,1)}, u32[]{:S(2)}, u32[]{:S(2)}) async-start(bf16[16,64,256]{2,1,0:T(8,128)(2,1)} %bitcast.27), calls=%async_computation.2 | async-start | bytes 1048576 | tf_op jit(solution)/shard_map/all_to_all | solution.py:490
  (22 other events, 102.1 us)

commit v4 on v3

--- a/solution.py
+++ b/solution.py
@@ -51,8 +51,9 @@
     weights = exchange(sent)
     from_z, from_y, from_x, weights = lax.optimization_barrier((from_z, from_y, from_x, weights))
     from_zy, from_zx = y(from_z), x(from_z)
+    from_zyx = [x(from_zy[:x_rows]), y(from_zx[x_rows:])]
+    from_y, from_x, from_zy, from_zx = lax.optimization_barrier((from_y, from_x, from_zy, from_zx))
     from_yx = [x(from_y[:x_rows]), y(from_x[x_rows:])]
-    from_zyx = [x(from_zy[:x_rows]), y(from_zx[x_rows:])]
     from_z, from_y, from_x, mine, ids, *_ = lax.optimization_barrier(
         (from_z, from_y, from_x, mine, ids, from_zy, from_zx)
     )
@@ -386,7 +387,7 @@
     )
     if inner_bits == 3 and experts == 2:
         pieces, own_group, my_ids = waved_gather(
-            mine, -(-5 * pool // 64) * 16, sent, exchange, my_ids
+            mine, -(-4 * pool // 64) * 16, sent, exchange, my_ids
         )
     else:
         steps = [("expert", b) for b in range(bits_of(experts))]

time: 175 us -> 173 us (0.989)
  no operation moved by 1% of the time
where the time goes in v4:
time: 173 us; the launch traced here: 172 us
  waiting for transfers between devices  87.2 us (50%)
  starting transfers between devices  50.7 us (29%)
  Pallas kernels  27.3 us (16%)
  local copies, waits for them, and re-layouts  5.48 us (3%)
    ppermute x35, waiting for transfers between devices, swapped(): lax.ppermute(array, axis, [(i, i ^ 1 << bit) for i in range(lax.axis_size...  75.3 us
    ppermute x35, starting transfers between devices, swapped(): lax.ppermute(array, axis, [(i, i ^ 1 << bit) for i in range(lax.axis_size...  36.7 us
    pallas_call x7, Pallas kernels, call(): pl.pallas_call(kernel, out_shape=outs, grid=grid, in_specs=in_specs, out_...  27.3 us
    all_to_all x1, waiting for transfers between devices, shards(): got = lax.all_to_all(vector, 'dp', 0, 0, tiled=True)  7.73 us
    all_to_all x1, starting transfers between devices, shards(): lax.all_to_all(sent, 'dp', 0, 0, axis_index_groups=groups, tiled=True)  5.39 us
    all_to_all x1, starting transfers between devices, shards(): got = lax.all_to_all(vector, 'dp', 0, 0, tiled=True)  4.43 us
    all_to_all x1, starting transfers between devices, shards(): lax.all_to_all(slot_outputs, ('dp', 'expert'), 0, 0, axis_index_groups=cu...  4.25 us
    all_to_all x1, waiting for transfers between devices, shards(): lax.all_to_all(slot_outputs, ('dp', 'expert'), 0, 0, axis_index_groups=cu...  4.23 us
  transfers between devices with their start and end apart: 38, of which 23 were waited for; matrix products, arithmetic and copies ran while one was open for 1% of the time, Pallas kernels for 3%

profile of v4, /device:TPU:0, one launch (start us, length us, event | category | flops | bytes accessed | tf_op | source)
XLA Modules:
  0.0 172.2 jit_solution(664399695180547756)
XLA Ops:
  1.9 2.7 %prepare.1 = (bf16[128,2176]{1,0:T(8,128)(2,1)}, bf16[8,288,128]{2,1,0:T(8,128)(2,1)}) custom-call(s32[2,64]{1,0:T(2,128)} %reshape.35.route_ref, s32[1,2]{1,0:T(1,128)} %counts_ref.1, bf16[64,2048]{1,0:T(8,128)(2,1)} %tok_ref.1, bf16[64,2048]{1,0:T(8,128)(2,1)} %cot_ref.1, f32[128,768]{1,0:T(8,128)} %bitcast.28, f32[128,768]{1,0:T(8,128)} %bitcast.30, ...), custom_call_target="tpu_custom_call" | custom-call | tf_op jit(solution)/shard_map/prepare/pallas_call | solution.py:325
  4.6 5.4 %all-to-all-start = ((bf16[8,288,128]{2,1,0:T(8,128)(2,1)}), bf16[8,288,128]{2,1,0:T(8,128)(2,1)S(1)}, u32[]{:S(2)}, u32[]{:S(2)}) async-start(bf16[8,288,128]{2,1,0:T(8,128)(2,1)} %get-tuple-element.42), calls=%async_computation | async-start | bytes 1179648 | tf_op jit(solution)/shard_map/all_to_all | solution.py:385
  15.0 10.1 %collective-permute-done.2.refs_3_ = bf16[128,2176]{1,0:T(8,128)(2,1)S(1)} collective-permute-done((bf16[128,2176]{1,0:T(8,128)(2,1)S(1)}, bf16[128,2176]{1,0:T(8,128)(2,1)S(1)}, u32[]{:S(2)}, u32[]{:S(2)}) %collective-permute-start.2) | collective-permute-done | bytes 557088 | tf_op jit(solution)/shard_map/ppermute | solution.py:30
  25.0 6.4 %collective-permute-done.1.refs_2_ = bf16[128,2176]{1,0:T(8,128)(2,1)S(1)} collective-permute-done((bf16[128,2176]{1,0:T(8,128)(2,1)S(1)}, bf16[128,2176]{1,0:T(8,128)(2,1)S(1)}, u32[]{:S(2)}, u32[]{:S(2)}) %collective-permute-start.1) | collective-permute-done | bytes 557088 | tf_op jit(solution)/shard_map/ppermute | solution.py:30
  31.6 2.6 %collective-permute-start.19 = (bf16[1,8,288,128]{3,2,1,0:T(8,128)(2,1)S(1)}, bf16[1,8,288,128]{3,2,1,0:T(8,128)(2,1)S(1)}, u32[]{:S(2)}, u32[]{:S(2)}) collective-permute-start(bf16[1,8,288,128]{3,2,1,0:T(8,128)(2,1)S(1)} %bitcast.25), channel_id=1, source_target_pairs={{0,16},{2,18},{4,20},{6,22},{8,24},{10,26},{12,28},{14,30},{16,0},... | collective-permute-start | bytes 1769480 | tf_op jit(solution)/shard_map/ppermute | solution.py:30
  37.2 11.1 %collective-permute-done.4.refs_5_ = bf16[128,2176]{1,0:T(8,128)(2,1)S(1)} collective-permute-done((bf16[128,2176]{1,0:T(8,128)(2,1)}, bf16[128,2176]{1,0:T(8,128)(2,1)S(1)}, u32[]{:S(2)}, u32[]{:S(2)}) %collective-permute-start.4) | collective-permute-done | bytes 557088 | tf_op jit(solution)/shard_map/ppermute | solution.py:30
  53.2 6.8 %collective-permute-done.19.refs_21_ = bf16[1,8,288,128]{3,2,1,0:T(8,128)(2,1)S(1)} collective-permute-done((bf16[1,8,288,128]{3,2,1,0:T(8,128)(2,1)S(1)}, bf16[1,8,288,128]{3,2,1,0:T(8,128)(2,1)S(1)}, u32[]{:S(2)}, u32[]{:S(2)}) %collective-permute-start.19) | collective-permute-done | bytes 589856 | tf_op jit(solution)/shard_map/ppermute | solution.py:30
  64.7 2.1 %collective-permute-done.10.refs_11_ = bf16[128,2176]{1,0:T(8,128)(2,1)S(1)} collective-permute-done((bf16[128,2176]{1,0:T(8,128)(2,1)}, bf16[128,2176]{1,0:T(8,128)(2,1)S(1)}, u32[]{:S(2)}, u32[]{:S(2)}) %collective-permute-start.10) | collective-permute-done | bytes 557088 | tf_op jit(solution)/shard_map/ppermute | solution.py:30
  68.2 12.0 %forward_and_gram.1 = (bf16[96,1024]{1,0:T(8,128)(2,1)S(1)}, bf16[96,1024]{1,0:T(8,128)(2,1)}, bf16[96,1024]{1,0:T(8,128)(2,1)S(1)}, bf16[96,1024]{1,0:T(8,128)(...) custom-call(s32[3]{0:T(128)S(1)} %pad_add_fusion.idx_ref, ...), custom_call_target="tpu_custom_call" | custom-call | tf_op jit(solution)/shard_map/forward_and_gram/pallas_call | solution.py:325
  83.4 2.6 %collective-permute-done.21 = f32[24,128]{1,0:T(8,128)S(1)} collective-permute-done((f32[24,128]{1,0:T(8,128)S(1)}, f32[24,128]{1,0:T(8,128)S(1)}, u32[]{:S(2)}, u32[]{:S(2)}) %collective-permute-start.21) | collective-permute-done | bytes 12320 | tf_op jit(solution)/shard_map/ppermute | solution.py:30
  88.5 2.7 %collective-permute-done.23 = f32[24,128]{1,0:T(8,128)S(1)} collective-permute-done((f32[24,128]{1,0:T(8,128)S(1)}, f32[24,128]{1,0:T(8,128)S(1)}, u32[]{:S(2)}, u32[]{:S(2)}) %collective-permute-start.23) | collective-permute-done | bytes 12320 | tf_op jit(solution)/shard_map/ppermute | solution.py:30
  91.2 3.6 %local_tree.1 = bf16[16,288,128]{2,1,0:T(8,128)(2,1)} custom-call(s32[3]{0:T(128)S(1)} %pad_add_fusion.idx_ref, f32[24,128]{1,0:T(8,128)S(1)} %add.29.gram_ref, bf16[1024,2048]{1,0:T(8,128)(2,1)S(1)} %get-tuple-element.59.x_ref, bf16[1024,2176]{1,0:T(8,128)(2,1)S(1)} %get-tuple-element.60.y_ref, bf16[96,1024]{1,0:T(8,128)(2,1)S(1)} %get-tuple-element.61.dgate_ref, ...), custom_call_target="tpu_custom_call" | custom-call | tf_op jit(solution)/shard_map/local_tree/pallas_call | solution.py:325
  94.8 4.4 %all-to-all-start.1 = ((bf16[16,288,128]{2,1,0:T(8,128)(2,1)}), bf16[16,288,128]{2,1,0:T(8,128)(2,1)S(1)}, u32[]{:S(2)}, u32[]{:S(2)}) async-start(bf16[16,288,128]{2,1,0:T(8,128)(2,1)} %local_tree.1), calls=%async_computation.1 | async-start | bytes 2359296 | tf_op jit(solution)/shard_map/all_to_all | solution.py:441
  101.3 15.3 %collective-permute-done.28.refs_2_ = bf16[96,1024]{1,0:T(8,128)(2,1)} collective-permute-done((bf16[96,1024]{1,0:T(8,128)(2,1)}, bf16[96,1024]{1,0:T(8,128)(2,1)}, u32[]{:S(2)}, u32[]{:S(2)}) %collective-permute-start.28) | collective-permute-done | bytes 196640 | tf_op jit(solution)/shard_map/ppermute | solution.py:30
  116.6 7.7 %all-to-all-done.1.got_ref = bf16[16,288,128]{2,1,0:T(8,128)(2,1)S(1)} async-done(((bf16[16,288,128]{2,1,0:T(8,128)(2,1)}), bf16[16,288,128]{2,1,0:T(8,128)(2,1)S(1)}, u32[]{:S(2)}, u32[]{:S(2)}) %all-to-all-start.1) | async-done | bytes 1179680 | tf_op jit(solution)/shard_map/all_to_all | solution.py:441
  127.8 2.1 %collective-permute-start.25 = (f32[6,2]{1,0:T(8,128)S(1)}, f32[6,2]{1,0:T(8,128)S(1)}, u32[]{:S(2)}, u32[]{:S(2)}) collective-permute-start(f32[6,2]{1,0:T(8,128)S(1)} %add.30), channel_id=1, source_target_pairs={{0,4},{2,6},{4,0},{6,2},{8,12},{10,14},{12,8},{14,10},{16,20},{18,... | collective-permute-start | bytes 152 | tf_op jit(solution)/shard_map/ppermute | solution.py:30
  131.5 3.6 %collective-permute-start.26 = (f32[6,2]{1,0:T(8,128)S(1)}, f32[6,2]{1,0:T(8,128)S(1)}, u32[]{:S(2)}, u32[]{:S(2)}) collective-permute-start(f32[6,2]{1,0:T(8,128)S(1)} %add.31), channel_id=1, source_target_pairs={{0,8},{2,10},{4,12},{6,14},{8,0},{10,2},{12,4},{14,6},{16,24},{18,... | collective-permute-start | bytes 152 | tf_op jit(solution)/shard_map/ppermute | solution.py:30
  136.7 3.6 %collective-permute-start.27 = (f32[6,2]{1,0:T(8,128)S(1)}, f32[6,2]{1,0:T(8,128)S(1)}, u32[]{:S(2)}, u32[]{:S(2)}) collective-permute-start(f32[6,2]{1,0:T(8,128)S(1)} %add.32), channel_id=1, source_target_pairs={{0,16},{2,18},{4,20},{6,22},{8,24},{10,26},{12,28},{14,30},{16,0},... | collective-permute-start | bytes 152 | tf_op jit(solution)/shard_map/ppermute | solution.py:30
  144.9 2.9 %collective-permute-start.34 = (bf16[1,128,768]{2,1,0:T(8,128)(2,1)S(1)}, bf16[1,128,768]{2,1,0:T(8,128)(2,1)S(1)}, u32[]{:S(2)}, u32[]{:S(2)}) collective-permute-start(bf16[1,128,768]{2,1,0:T(8,128)(2,1)S(1)} %bitcast.34), channel_id=1, source_target_pairs={{0,16},{2,18},{4,20},{6,22},{8,24},{10,26},{12,28},{14,30},{16,0},... | collective-permute-start | bytes 589832 | tf_op jit(solution)/shard_map/ppermute | solution.py:30
  147.9 6.0 %collective-permute-done.34.refs_9_ = bf16[1,128,768]{2,1,0:T(8,128)(2,1)S(1)} collective-permute-done((bf16[1,128,768]{2,1,0:T(8,128)(2,1)S(1)}, bf16[1,128,768]{2,1,0:T(8,128)(2,1)S(1)}, u32[]{:S(2)}, u32[]{:S(2)}) %collective-permute-start.34) | collective-permute-done | bytes 196640 | tf_op jit(solution)/shard_map/ppermute | solution.py:30
  153.9 2.2 %project.1 = bf16[8,2,64,256]{3,2,1,0:T(8,128)(2,1)S(1)} custom-call(s32[3]{0:T(128)S(1)} %pad_add_fusion.idx_ref, bf16[96,1024]{1,0:T(8,128)(2,1)} %get-tuple-element.72.refs_0_, bf16[96,1024]{1,0:T(8,128)(2,1)} %collective-permute-done.22.refs_1_, bf16[96,1024]{1,0:T(8,128)(2,1)} %collective-permute-done.28.refs_2_, ...), custom_call_target="tpu_custom_call" | custom-call | tf_op jit(solution)/shard_map/project/pallas_call | solution.py:325
  156.9 4.2 %all-to-all-start.2 = ((bf16[16,64,256]{2,1,0:T(8,128)(2,1)}), bf16[16,64,256]{2,1,0:T(8,128)(2,1)}, u32[]{:S(2)}, u32[]{:S(2)}) async-start(bf16[16,64,256]{2,1,0:T(8,128)(2,1)} %bitcast.27), calls=%async_computation.2 | async-start | bytes 1048576 | tf_op jit(solution)/shard_map/all_to_all | solution.py:491
  163.2 2.9 %update.3 = (f32[3,128,768]{2,1,0:T(8,128)}, f32[3,128,768]{2,1,0:T(8,128)}, f32[3,128,768]{2,1,0:T(8,128)}, f32[3,128,768]{2,1,0:T(8,128)}) custom-call(f32[6,2]{1,0:T(8,128)S(1)} %add.33.gram_ref, bf16[16,288,128]{2,1,0:T(8,128)(2,1)S(1)} %all-to-all-done.1.got_ref, ...), custom_call_target="tpu_custom_call", output_to_operand_aliasing={{0}: (6, {}), {1}: (7, {}), {2}: (8, {}), {3}: (9, {})} | custom-call | tf_op jit(solution)/shard_map/update/pallas_call | solution.py:325
  166.1 4.2 %all-to-all-done.2.got_ref = bf16[16,64,256]{2,1,0:T(8,128)(2,1)} async-done(((bf16[16,64,256]{2,1,0:T(8,128)(2,1)}), bf16[16,64,256]{2,1,0:T(8,128)(2,1)}, u32[]{:S(2)}, u32[]{:S(2)}) %all-to-all-start.2) | async-done | bytes 524320 | tf_op jit(solution)/shard_map/all_to_all | solution.py:491
  (91 shorter events, 44.0 us)
Async XLA Ops:
  4.6 27.0 %all-to-all-start = ((bf16[8,288,128]{2,1,0:T(8,128)(2,1)}), bf16[8,288,128]{2,1,0:T(8,128)(2,1)S(1)}, u32[]{:S(2)}, u32[]{:S(2)}) async-start(bf16[8,288,128]{2,1,0:T(8,128)(2,1)} %get-tuple-element.42), calls=%async_computation | async-start | bytes 1179648 | tf_op jit(solution)/shard_map/all_to_all | solution.py:385
  10.0 15.0 %collective-permute-start.2 = (bf16[128,2176]{1,0:T(8,128)(2,1)S(1)}, bf16[128,2176]{1,0:T(8,128)(2,1)S(1)}, u32[]{:S(2)}, u32[]{:S(2)}) collective-permute-start(bf16[128,2176]{1,0:T(8,128)(2,1)S(1)} %copy-done.6), channel_id=1, source_target_pairs={{0,1},{1,0},{2,3},{3,2},{4,5},{5,4},{6,7},{7,6},{8,9},{9,8},{10,11... | collective-permute-start | bytes 1671176 | tf_op jit(solution)/shard_map/ppermute | solution.py:30
  11.5 19.9 %collective-permute-start.1 = (bf16[128,2176]{1,0:T(8,128)(2,1)S(1)}, bf16[128,2176]{1,0:T(8,128)(2,1)S(1)}, u32[]{:S(2)}, u32[]{:S(2)}) collective-permute-start(bf16[128,2176]{1,0:T(8,128)(2,1)S(1)} %copy-done.6), channel_id=1, source_target_pairs={{0,4},{2,6},{4,0},{6,2},{8,12},{10,14},{12,8},{14,10},{16,20},{18,... | collective-permute-start | bytes 1671176 | tf_op jit(solution)/shard_map/ppermute | solution.py:30
  13.5 18.1 %collective-permute-start = (bf16[128,2176]{1,0:T(8,128)(2,1)S(1)}, bf16[128,2176]{1,0:T(8,128)(2,1)}, u32[]{:S(2)}, u32[]{:S(2)}) collective-permute-start(bf16[128,2176]{1,0:T(8,128)(2,1)S(1)} %copy-done.6), channel_id=1, source_target_pairs={{0,8},{2,10},{4,12},{6,14},{8,0},{10,2},{12,4},{14,6},{16,24},{18,... | collective-permute-start | bytes 1671176 | tf_op jit(solution)/shard_map/ppermute | solution.py:30
  31.6 28.4 %collective-permute-start.19 = (bf16[1,8,288,128]{3,2,1,0:T(8,128)(2,1)S(1)}, bf16[1,8,288,128]{3,2,1,0:T(8,128)(2,1)S(1)}, u32[]{:S(2)}, u32[]{:S(2)}) collective-permute-start(bf16[1,8,288,128]{3,2,1,0:T(8,128)(2,1)S(1)} %bitcast.25), channel_id=1, source_target_pairs={{0,16},{2,18},{4,20},{6,22},{8,24},{10,26},{12,28},{14,30},{16,0},... | collective-permute-start | bytes 1769480 | tf_op jit(solution)/shard_map/ppermute | solution.py:30
  34.2 14.1 %collective-permute-start.4 = (bf16[128,2176]{1,0:T(8,128)(2,1)}, bf16[128,2176]{1,0:T(8,128)(2,1)S(1)}, u32[]{:S(2)}, u32[]{:S(2)}) collective-permute-start(bf16[128,2176]{1,0:T(8,128)(2,1)} %collective-permute-done.refs_1_), channel_id=1, source_target_pairs={{0,1},{1,0},{2,3},{3,2},{4,5},{5,4},{6,7},{7,6},{8,9},{9,8},{10,11... | collective-permute-start | bytes 1671176 | tf_op jit(solution)/shard_map/ppermute | solution.py:30
  35.6 14.2 %collective-permute-start.3 = (bf16[128,2176]{1,0:T(8,128)(2,1)}, bf16[128,2176]{1,0:T(8,128)(2,1)S(1)}, u32[]{:S(2)}, u32[]{:S(2)}) collective-permute-start(bf16[128,2176]{1,0:T(8,128)(2,1)} %collective-permute-done.refs_1_), channel_id=1, source_target_pairs={{0,4},{2,6},{4,0},{6,2},{8,12},{10,14},{12,8},{14,10},{16,20},{18,... | collective-permute-start | bytes 1671176 | tf_op jit(solution)/shard_map/ppermute | solution.py:30
  48.3 11.7 %collective-permute-start.8 = (bf16[64,2176]{1,0:T(8,128)(2,1)S(1)}, bf16[64,2176]{1,0:T(8,128)(2,1)S(1)}, u32[]{:S(2)}, u32[]{:S(2)}) collective-permute-start(bf16[64,2176]{1,0:T(8,128)(2,1)S(1)} %slice.17), channel_id=1, source_target_pairs={{0,4},{2,6},{4,0},{6,2},{8,12},{10,14},{12,8},{14,10},{16,20},{18,... | collective-permute-start | bytes 835592 | tf_op jit(solution)/shard_map/ppermute | solution.py:30
  49.9 10.6 %collective-permute-start.7 = (bf16[64,2176]{1,0:T(8,128)(2,1)S(1)}, bf16[64,2176]{1,0:T(8,128)(2,1)S(1)}, u32[]{:S(2)}, u32[]{:S(2)}) collective-permute-start(bf16[64,2176]{1,0:T(8,128)(2,1)S(1)} %slice.16), channel_id=1, source_target_pairs={{0,1},{1,0},{2,3},{3,2},{4,5},{5,4},{6,7},{7,6},{8,9},{9,8},{10,11... | collective-permute-start | bytes 835592 | tf_op jit(solution)/shard_map/ppermute | solution.py:30
  51.4 10.0 %collective-permute-start.6 = (bf16[64,2176]{1,0:T(8,128)(2,1)S(1)}, bf16[64,2176]{1,0:T(8,128)(2,1)S(1)}, u32[]{:S(2)}, u32[]{:S(2)}) collective-permute-start(bf16[64,2176]{1,0:T(8,128)(2,1)S(1)} %slice.13), channel_id=1, source_target_pairs={{0,4},{2,6},{4,0},{6,2},{8,12},{10,14},{12,8},{14,10},{16,20},{18,... | collective-permute-start | bytes 835592 | tf_op jit(solution)/shard_map/ppermute | solution.py:30
  52.1 10.5 %collective-permute-start.5 = (bf16[64,2176]{1,0:T(8,128)(2,1)S(1)}, bf16[64,2176]{1,0:T(8,128)(2,1)S(1)}, u32[]{:S(2)}, u32[]{:S(2)}) collective-permute-start(bf16[64,2176]{1,0:T(8,128)(2,1)S(1)} %slice.12), channel_id=1, source_target_pairs={{0,1},{1,0},{2,3},{3,2},{4,5},{5,4},{6,7},{7,6},{8,9},{9,8},{10,11... | collective-permute-start | bytes 835592 | tf_op jit(solution)/shard_map/ppermute | solution.py:30
  62.6 4.7 %collective-permute-start.13 = (bf16[128,2176]{1,0:T(8,128)(2,1)S(1)}, bf16[128,2176]{1,0:T(8,128)(2,1)S(1)}, u32[]{:S(2)}, u32[]{:S(2)}) collective-permute-start(bf16[128,2176]{1,0:T(8,128)(2,1)S(1)} %collective-permute-done.3.refs_4_), channel_id=1, source_target_pairs={{0,2},{2,0},{4,6},{6,4},{8,10},{10,8},{12,14},{14,12},{16,18},{18,... | collective-permute-start | bytes 1671176 | tf_op jit(solution)/shard_map/ppermute | solution.py:30
  80.2 7.3 %collective-permute-start.22 = (bf16[96,1024]{1,0:T(8,128)(2,1)}, bf16[96,1024]{1,0:T(8,128)(2,1)}, u32[]{:S(2)}, u32[]{:S(2)}) collective-permute-start(bf16[96,1024]{1,0:T(8,128)(2,1)} %get-tuple-element.72.refs_0_), channel_id=1, source_target_pairs={{0,8},{2,10},{4,12},{6,14},{8,0},{10,2},{12,4},{14,6},{16,24},{18,... | collective-permute-start | bytes 589832 | tf_op jit(solution)/shard_map/ppermute | solution.py:30
  94.8 29.6 %all-to-all-start.1 = ((bf16[16,288,128]{2,1,0:T(8,128)(2,1)}), bf16[16,288,128]{2,1,0:T(8,128)(2,1)S(1)}, u32[]{:S(2)}, u32[]{:S(2)}) async-start(bf16[16,288,128]{2,1,0:T(8,128)(2,1)} %local_tree.1), calls=%async_computation.1 | async-start | bytes 2359296 | tf_op jit(solution)/shard_map/all_to_all | solution.py:441
  99.2 17.4 %collective-permute-start.28 = (bf16[96,1024]{1,0:T(8,128)(2,1)}, bf16[96,1024]{1,0:T(8,128)(2,1)}, u32[]{:S(2)}, u32[]{:S(2)}) collective-permute-start(bf16[96,1024]{1,0:T(8,128)(2,1)} %get-tuple-element.72.refs_0_), channel_id=1, source_target_pairs={{0,4},{2,6},{4,0},{6,2},{8,12},{10,14},{12,8},{14,10},{16,20},{18,... | collective-permute-start | bytes 589832 | tf_op jit(solution)/shard_map/ppermute | solution.py:30
  101.1 24.5 %collective-permute-start.29 = (bf16[96,1024]{1,0:T(8,128)(2,1)}, bf16[96,1024]{1,0:T(8,128)(2,1)}, u32[]{:S(2)}, u32[]{:S(2)}) collective-permute-start(bf16[96,1024]{1,0:T(8,128)(2,1)} %collective-permute-done.22.refs_1_), channel_id=1, source_target_pairs={{0,4},{2,6},{4,0},{6,2},{8,12},{10,14},{12,8},{14,10},{16,20},{18,... | collective-permute-start | bytes 589832 | tf_op jit(solution)/shard_map/ppermute | solution.py:30
  124.3 23.5 %collective-permute-start.30 = (bf16[96,1024]{1,0:T(8,128)(2,1)}, bf16[96,1024]{1,0:T(8,128)(2,1)}, u32[]{:S(2)}, u32[]{:S(2)}) collective-permute-start(bf16[96,1024]{1,0:T(8,128)(2,1)} %get-tuple-element.72.refs_0_), channel_id=1, source_target_pairs={{0,2},{2,0},{4,6},{6,4},{8,10},{10,8},{12,14},{14,12},{16,18},{18,... | collective-permute-start | bytes 589832 | tf_op jit(solution)/shard_map/ppermute | solution.py:30
  125.1 22.8 %collective-permute-start.31 = (bf16[96,1024]{1,0:T(8,128)(2,1)}, bf16[96,1024]{1,0:T(8,128)(2,1)}, u32[]{:S(2)}, u32[]{:S(2)}) collective-permute-start(bf16[96,1024]{1,0:T(8,128)(2,1)} %collective-permute-done.22.refs_1_), channel_id=1, source_target_pairs={{0,2},{2,0},{4,6},{6,4},{8,10},{10,8},{12,14},{14,12},{16,18},{18,... | collective-permute-start | bytes 589832 | tf_op jit(solution)/shard_map/ppermute | solution.py:30
  125.1 22.8 %collective-permute-start.32 = (bf16[96,1024]{1,0:T(8,128)(2,1)}, bf16[96,1024]{1,0:T(8,128)(2,1)}, u32[]{:S(2)}, u32[]{:S(2)}) collective-permute-start(bf16[96,1024]{1,0:T(8,128)(2,1)} %collective-permute-done.28.refs_2_), channel_id=1, source_target_pairs={{0,2},{2,0},{4,6},{6,4},{8,10},{10,8},{12,14},{14,12},{16,18},{18,... | collective-permute-start | bytes 589832 | tf_op jit(solution)/shard_map/ppermute | solution.py:30
  125.6 22.3 %collective-permute-start.33 = (bf16[96,1024]{1,0:T(8,128)(2,1)}, bf16[96,1024]{1,0:T(8,128)(2,1)}, u32[]{:S(2)}, u32[]{:S(2)}) collective-permute-start(bf16[96,1024]{1,0:T(8,128)(2,1)} %collective-permute-done.29.refs_3_), channel_id=1, source_target_pairs={{0,2},{2,0},{4,6},{6,4},{8,10},{10,8},{12,14},{14,12},{16,18},{18,... | collective-permute-start | bytes 589832 | tf_op jit(solution)/shard_map/ppermute | solution.py:30
  131.5 5.2 %collective-permute-start.26 = (f32[6,2]{1,0:T(8,128)S(1)}, f32[6,2]{1,0:T(8,128)S(1)}, u32[]{:S(2)}, u32[]{:S(2)}) collective-permute-start(f32[6,2]{1,0:T(8,128)S(1)} %add.31), channel_id=1, source_target_pairs={{0,8},{2,10},{4,12},{6,14},{8,0},{10,2},{12,4},{14,6},{16,24},{18,... | collective-permute-start | bytes 152 | tf_op jit(solution)/shard_map/ppermute | solution.py:30
  136.7 5.1 %collective-permute-start.27 = (f32[6,2]{1,0:T(8,128)S(1)}, f32[6,2]{1,0:T(8,128)S(1)}, u32[]{:S(2)}, u32[]{:S(2)}) collective-permute-start(f32[6,2]{1,0:T(8,128)S(1)} %add.32), channel_id=1, source_target_pairs={{0,16},{2,18},{4,20},{6,22},{8,24},{10,26},{12,28},{14,30},{16,0},... | collective-permute-start | bytes 152 | tf_op jit(solution)/shard_map/ppermute | solution.py:30
  144.9 8.9 %collective-permute-start.34 = (bf16[1,128,768]{2,1,0:T(8,128)(2,1)S(1)}, bf16[1,128,768]{2,1,0:T(8,128)(2,1)S(1)}, u32[]{:S(2)}, u32[]{:S(2)}) collective-permute-start(bf16[1,128,768]{2,1,0:T(8,128)(2,1)S(1)} %bitcast.34), channel_id=1, source_target_pairs={{0,16},{2,18},{4,20},{6,22},{8,24},{10,26},{12,28},{14,30},{16,0},... | collective-permute-start | bytes 589832 | tf_op jit(solution)/shard_map/ppermute | solution.py:30
  156.9 13.4 %all-to-all-start.2 = ((bf16[16,64,256]{2,1,0:T(8,128)(2,1)}), bf16[16,64,256]{2,1,0:T(8,128)(2,1)}, u32[]{:S(2)}, u32[]{:S(2)}) async-start(bf16[16,64,256]{2,1,0:T(8,128)(2,1)} %bitcast.27), calls=%async_computation.2 | async-start | bytes 1048576 | tf_op jit(solution)/shard_map/all_to_all | solution.py:491
  (22 other events, 104.9 us)

commit v5 on v4

--- a/solution.py
+++ b/solution.py
@@ -439,7 +439,6 @@
         vmem=5 * rows_bytes // 4 + 2 * weight_bytes + 8 * mebi,
     )
     got = lax.all_to_all(vector, "dp", 0, 0, tiled=True)
-    hidden_parts = [after(piece, got) for piece in hidden_parts]
     hidden_parts += [swapped(piece, "dp", 0) for piece in hidden_parts]
     leaves = got.reshape(outer, group, 3, part, block_rows).transpose(2, 0, 1, 3, 4)
     leaves = leaves.reshape(3, outer, hidden_width, block_rows).astype(f32)

time: 173 us -> 172 us (level)
    all_to_all x1, waiting for transfers between devices: 7.73 us -> 3.99 us  [shards(): got = lax.all_to_all(vector, 'dp', 0, 0, tiled=True)]
    ppermute x35, waiting for transfers between devices: 75.3 us -> 78.5 us  [swapped(): lax.ppermute(array, axis, [(i, i ^ 1 << bit) for i in range(lax.axis_size...]
  transfers between devices with their start and end apart: 38 -> 38, of which waited for: 23 -> 24; matrix products, arithmetic and copies ran while one was open for 1% -> 1% of each run, Pallas kernels for 3% -> 3%
where the time goes in v5:
time: 172 us; the launch traced here: 171 us
  waiting for transfers between devices  86.7 us (50%)
  starting transfers between devices  50.2 us (29%)
  Pallas kernels  27.3 us (16%)
  local copies, waits for them, and re-layouts  5.48 us (3%)
    ppermute x35, waiting for transfers between devices, swapped(): lax.ppermute(array, axis, [(i, i ^ 1 << bit) for i in range(lax.axis_size...  78.5 us
    ppermute x35, starting transfers between devices, swapped(): lax.ppermute(array, axis, [(i, i ^ 1 << bit) for i in range(lax.axis_size...  36.2 us
    pallas_call x7, Pallas kernels, call(): pl.pallas_call(kernel, out_shape=outs, grid=grid, in_specs=in_specs, out_...  27.3 us
    all_to_all x1, starting transfers between devices, shards(): lax.all_to_all(sent, 'dp', 0, 0, axis_index_groups=groups, tiled=True)  5.39 us
    all_to_all x1, starting transfers between devices, shards(): got = lax.all_to_all(vector, 'dp', 0, 0, tiled=True)  4.43 us
    all_to_all x1, starting transfers between devices, shards(): lax.all_to_all(slot_outputs, ('dp', 'expert'), 0, 0, axis_index_groups=cu...  4.25 us
    all_to_all x1, waiting for transfers between devices, shards(): lax.all_to_all(slot_outputs, ('dp', 'expert'), 0, 0, axis_index_groups=cu...  4.23 us
    all_to_all x1, waiting for transfers between devices, shards(): got = lax.all_to_all(vector, 'dp', 0, 0, tiled=True)  3.99 us
  transfers between devices with their start and end apart: 38, of which 24 were waited for; matrix products, arithmetic and copies ran while one was open for 1% of the time, Pallas kernels for 3%

profile of v5, /device:TPU:0, one launch (start us, length us, event | category | flops | bytes accessed | tf_op | source)
XLA Modules:
  0.0 171.1 jit_solution(9612291579962173651)
XLA Ops:
  1.9 2.7 %prepare.1 = (bf16[128,2176]{1,0:T(8,128)(2,1)}, bf16[8,288,128]{2,1,0:T(8,128)(2,1)}) custom-call(s32[2,64]{1,0:T(2,128)} %reshape.35.route_ref, s32[1,2]{1,0:T(1,128)} %counts_ref.1, bf16[64,2048]{1,0:T(8,128)(2,1)} %tok_ref.1, bf16[64,2048]{1,0:T(8,128)(2,1)} %cot_ref.1, f32[128,768]{1,0:T(8,128)} %bitcast.28, f32[128,768]{1,0:T(8,128)} %bitcast.30, ...), custom_call_target="tpu_custom_call" | custom-call | tf_op jit(solution)/shard_map/prepare/pallas_call | solution.py:325
  4.6 5.4 %all-to-all-start = ((bf16[8,288,128]{2,1,0:T(8,128)(2,1)}), bf16[8,288,128]{2,1,0:T(8,128)(2,1)S(1)}, u32[]{:S(2)}, u32[]{:S(2)}) async-start(bf16[8,288,128]{2,1,0:T(8,128)(2,1)} %get-tuple-element.38), calls=%async_computation | async-start | bytes 1179648 | tf_op jit(solution)/shard_map/all_to_all | solution.py:385
  15.0 10.1 %collective-permute-done.2.refs_3_ = bf16[128,2176]{1,0:T(8,128)(2,1)S(1)} collective-permute-done((bf16[128,2176]{1,0:T(8,128)(2,1)S(1)}, bf16[128,2176]{1,0:T(8,128)(2,1)S(1)}, u32[]{:S(2)}, u32[]{:S(2)}) %collective-permute-start.2) | collective-permute-done | bytes 557088 | tf_op jit(solution)/shard_map/ppermute | solution.py:30
  25.0 6.4 %collective-permute-done.1.refs_2_ = bf16[128,2176]{1,0:T(8,128)(2,1)S(1)} collective-permute-done((bf16[128,2176]{1,0:T(8,128)(2,1)S(1)}, bf16[128,2176]{1,0:T(8,128)(2,1)S(1)}, u32[]{:S(2)}, u32[]{:S(2)}) %collective-permute-start.1) | collective-permute-done | bytes 557088 | tf_op jit(solution)/shard_map/ppermute | solution.py:30
  31.6 2.6 %collective-permute-start.19 = (bf16[1,8,288,128]{3,2,1,0:T(8,128)(2,1)S(1)}, bf16[1,8,288,128]{3,2,1,0:T(8,128)(2,1)S(1)}, u32[]{:S(2)}, u32[]{:S(2)}) collective-permute-start(bf16[1,8,288,128]{3,2,1,0:T(8,128)(2,1)S(1)} %bitcast.25), channel_id=1, source_target_pairs={{0,16},{2,18},{4,20},{6,22},{8,24},{10,26},{12,28},{14,30},{16,0},... | collective-permute-start | bytes 1769480 | tf_op jit(solution)/shard_map/ppermute | solution.py:30
  37.2 11.1 %collective-permute-done.4.refs_5_ = bf16[128,2176]{1,0:T(8,128)(2,1)S(1)} collective-permute-done((bf16[128,2176]{1,0:T(8,128)(2,1)}, bf16[128,2176]{1,0:T(8,128)(2,1)S(1)}, u32[]{:S(2)}, u32[]{:S(2)}) %collective-permute-start.4) | collective-permute-done | bytes 557088 | tf_op jit(solution)/shard_map/ppermute | solution.py:30
  53.2 6.8 %collective-permute-done.19.refs_21_ = bf16[1,8,288,128]{3,2,1,0:T(8,128)(2,1)S(1)} collective-permute-done((bf16[1,8,288,128]{3,2,1,0:T(8,128)(2,1)S(1)}, bf16[1,8,288,128]{3,2,1,0:T(8,128)(2,1)S(1)}, u32[]{:S(2)}, u32[]{:S(2)}) %collective-permute-start.19) | collective-permute-done | bytes 589856 | tf_op jit(solution)/shard_map/ppermute | solution.py:30
  68.2 12.0 %forward_and_gram.1 = (bf16[96,1024]{1,0:T(8,128)(2,1)S(1)}, bf16[96,1024]{1,0:T(8,128)(2,1)}, bf16[96,1024]{1,0:T(8,128)(2,1)S(1)}, bf16[96,1024]{1,0:T(8,128)(...) custom-call(s32[3]{0:T(128)S(1)} %pad_add_fusion.idx_ref, ...), custom_call_target="tpu_custom_call" | custom-call | tf_op jit(solution)/shard_map/forward_and_gram/pallas_call | solution.py:325
  83.4 2.6 %collective-permute-done.21 = f32[24,128]{1,0:T(8,128)S(1)} collective-permute-done((f32[24,128]{1,0:T(8,128)S(1)}, f32[24,128]{1,0:T(8,128)S(1)}, u32[]{:S(2)}, u32[]{:S(2)}) %collective-permute-start.21) | collective-permute-done | bytes 12320 | tf_op jit(solution)/shard_map/ppermute | solution.py:30
  88.5 2.7 %collective-permute-done.23 = f32[24,128]{1,0:T(8,128)S(1)} collective-permute-done((f32[24,128]{1,0:T(8,128)S(1)}, f32[24,128]{1,0:T(8,128)S(1)}, u32[]{:S(2)}, u32[]{:S(2)}) %collective-permute-start.23) | collective-permute-done | bytes 12320 | tf_op jit(solution)/shard_map/ppermute | solution.py:30
  91.2 3.6 %local_tree.1 = bf16[16,288,128]{2,1,0:T(8,128)(2,1)} custom-call(s32[3]{0:T(128)S(1)} %pad_add_fusion.idx_ref, f32[24,128]{1,0:T(8,128)S(1)} %add.29.gram_ref, bf16[1024,2048]{1,0:T(8,128)(2,1)S(1)} %get-tuple-element.55.x_ref, bf16[1024,2176]{1,0:T(8,128)(2,1)S(1)} %get-tuple-element.56.y_ref, bf16[96,1024]{1,0:T(8,128)(2,1)S(1)} %get-tuple-element.57.dgate_ref, ...), custom_call_target="tpu_custom_call" | custom-call | tf_op jit(solution)/shard_map/local_tree/pallas_call | solution.py:325
  94.8 4.4 %all-to-all-start.1 = ((bf16[16,288,128]{2,1,0:T(8,128)(2,1)}), bf16[16,288,128]{2,1,0:T(8,128)(2,1)S(1)}, u32[]{:S(2)}, u32[]{:S(2)}) async-start(bf16[16,288,128]{2,1,0:T(8,128)(2,1)} %local_tree.1), calls=%async_computation.1 | async-start | bytes 2359296 | tf_op jit(solution)/shard_map/all_to_all | solution.py:441
  101.8 14.8 %collective-permute-done.28.refs_2_ = bf16[96,1024]{1,0:T(8,128)(2,1)} collective-permute-done((bf16[96,1024]{1,0:T(8,128)(2,1)}, bf16[96,1024]{1,0:T(8,128)(2,1)}, u32[]{:S(2)}, u32[]{:S(2)}) %collective-permute-start.28) | collective-permute-done | bytes 196640 | tf_op jit(solution)/shard_map/ppermute | solution.py:30
  116.6 3.7 %collective-permute-done.29.refs_3_ = bf16[96,1024]{1,0:T(8,128)(2,1)} collective-permute-done((bf16[96,1024]{1,0:T(8,128)(2,1)}, bf16[96,1024]{1,0:T(8,128)(2,1)}, u32[]{:S(2)}, u32[]{:S(2)}) %collective-permute-start.29) | collective-permute-done | bytes 196640 | tf_op jit(solution)/shard_map/ppermute | solution.py:30
  120.3 4.0 %all-to-all-done.1.got_ref = bf16[16,288,128]{2,1,0:T(8,128)(2,1)S(1)} async-done(((bf16[16,288,128]{2,1,0:T(8,128)(2,1)}), bf16[16,288,128]{2,1,0:T(8,128)(2,1)S(1)}, u32[]{:S(2)}, u32[]{:S(2)}) %all-to-all-start.1) | async-done | bytes 1179680 | tf_op jit(solution)/shard_map/all_to_all | solution.py:441
  126.8 2.1 %collective-permute-start.25 = (f32[6,2]{1,0:T(8,128)S(1)}, f32[6,2]{1,0:T(8,128)S(1)}, u32[]{:S(2)}, u32[]{:S(2)}) collective-permute-start(f32[6,2]{1,0:T(8,128)S(1)} %add.30), channel_id=1, source_target_pairs={{0,4},{2,6},{4,0},{6,2},{8,12},{10,14},{12,8},{14,10},{16,20},{18,... | collective-permute-start | bytes 152 | tf_op jit(solution)/shard_map/ppermute | solution.py:30
  130.5 3.6 %collective-permute-start.26 = (f32[6,2]{1,0:T(8,128)S(1)}, f32[6,2]{1,0:T(8,128)S(1)}, u32[]{:S(2)}, u32[]{:S(2)}) collective-permute-start(f32[6,2]{1,0:T(8,128)S(1)} %add.31), channel_id=1, source_target_pairs={{0,8},{2,10},{4,12},{6,14},{8,0},{10,2},{12,4},{14,6},{16,24},{18,... | collective-permute-start | bytes 152 | tf_op jit(solution)/shard_map/ppermute | solution.py:30
  135.7 3.6 %collective-permute-start.27 = (f32[6,2]{1,0:T(8,128)S(1)}, f32[6,2]{1,0:T(8,128)S(1)}, u32[]{:S(2)}, u32[]{:S(2)}) collective-permute-start(f32[6,2]{1,0:T(8,128)S(1)} %add.32), channel_id=1, source_target_pairs={{0,16},{2,18},{4,20},{6,22},{8,24},{10,26},{12,28},{14,30},{16,0},... | collective-permute-start | bytes 152 | tf_op jit(solution)/shard_map/ppermute | solution.py:30
  143.9 2.9 %collective-permute-start.34 = (bf16[1,128,768]{2,1,0:T(8,128)(2,1)S(1)}, bf16[1,128,768]{2,1,0:T(8,128)(2,1)S(1)}, u32[]{:S(2)}, u32[]{:S(2)}) collective-permute-start(bf16[1,128,768]{2,1,0:T(8,128)(2,1)S(1)} %bitcast.34), channel_id=1, source_target_pairs={{0,16},{2,18},{4,20},{6,22},{8,24},{10,26},{12,28},{14,30},{16,0},... | collective-permute-start | bytes 589832 | tf_op jit(solution)/shard_map/ppermute | solution.py:30
  146.9 6.0 %collective-permute-done.34.refs_9_ = bf16[1,128,768]{2,1,0:T(8,128)(2,1)S(1)} collective-permute-done((bf16[1,128,768]{2,1,0:T(8,128)(2,1)S(1)}, bf16[1,128,768]{2,1,0:T(8,128)(2,1)S(1)}, u32[]{:S(2)}, u32[]{:S(2)}) %collective-permute-start.34) | collective-permute-done | bytes 196640 | tf_op jit(solution)/shard_map/ppermute | solution.py:30
  152.8 2.2 %project.1 = bf16[8,2,64,256]{3,2,1,0:T(8,128)(2,1)S(1)} custom-call(s32[3]{0:T(128)S(1)} %pad_add_fusion.idx_ref, bf16[96,1024]{1,0:T(8,128)(2,1)} %get-tuple-element.53.refs_0_, bf16[96,1024]{1,0:T(8,128)(2,1)} %collective-permute-done.22.refs_1_, bf16[96,1024]{1,0:T(8,128)(2,1)} %collective-permute-done.28.refs_2_, ...), custom_call_target="tpu_custom_call" | custom-call | tf_op jit(solution)/shard_map/project/pallas_call | solution.py:325
  155.9 4.2 %all-to-all-start.2 = ((bf16[16,64,256]{2,1,0:T(8,128)(2,1)}), bf16[16,64,256]{2,1,0:T(8,128)(2,1)}, u32[]{:S(2)}, u32[]{:S(2)}) async-start(bf16[16,64,256]{2,1,0:T(8,128)(2,1)} %bitcast.27), calls=%async_computation.2 | async-start | bytes 1048576 | tf_op jit(solution)/shard_map/all_to_all | solution.py:490
  162.2 2.9 %update.3 = (f32[3,128,768]{2,1,0:T(8,128)}, f32[3,128,768]{2,1,0:T(8,128)}, f32[3,128,768]{2,1,0:T(8,128)}, f32[3,128,768]{2,1,0:T(8,128)}) custom-call(f32[6,2]{1,0:T(8,128)S(1)} %add.33.gram_ref, bf16[16,288,128]{2,1,0:T(8,128)(2,1)S(1)} %all-to-all-done.1.got_ref, ...), custom_call_target="tpu_custom_call", output_to_operand_aliasing={{0}: (6, {}), {1}: (7, {}), {2}: (8, {}), {3}: (9, {})} | custom-call | tf_op jit(solution)/shard_map/update/pallas_call | solution.py:325
  165.1 4.2 %all-to-all-done.2.got_ref = bf16[16,64,256]{2,1,0:T(8,128)(2,1)} async-done(((bf16[16,64,256]{2,1,0:T(8,128)(2,1)}), bf16[16,64,256]{2,1,0:T(8,128)(2,1)}, u32[]{:S(2)}, u32[]{:S(2)}) %all-to-all-start.2) | async-done | bytes 524320 | tf_op jit(solution)/shard_map/all_to_all | solution.py:490
  (91 shorter events, 45.6 us)
Async XLA Ops:
  4.6 27.0 %all-to-all-start = ((bf16[8,288,128]{2,1,0:T(8,128)(2,1)}), bf16[8,288,128]{2,1,0:T(8,128)(2,1)S(1)}, u32[]{:S(2)}, u32[]{:S(2)}) async-start(bf16[8,288,128]{2,1,0:T(8,128)(2,1)} %get-tuple-element.38), calls=%async_computation | async-start | bytes 1179648 | tf_op jit(solution)/shard_map/all_to_all | solution.py:385
  10.0 15.0 %collective-permute-start.2 = (bf16[128,2176]{1,0:T(8,128)(2,1)S(1)}, bf16[128,2176]{1,0:T(8,128)(2,1)S(1)}, u32[]{:S(2)}, u32[]{:S(2)}) collective-permute-start(bf16[128,2176]{1,0:T(8,128)(2,1)S(1)} %copy-done.6), channel_id=1, source_target_pairs={{0,1},{1,0},{2,3},{3,2},{4,5},{5,4},{6,7},{7,6},{8,9},{9,8},{10,11... | collective-permute-start | bytes 1671176 | tf_op jit(solution)/shard_map/ppermute | solution.py:30
  11.5 19.9 %collective-permute-start.1 = (bf16[128,2176]{1,0:T(8,128)(2,1)S(1)}, bf16[128,2176]{1,0:T(8,128)(2,1)S(1)}, u32[]{:S(2)}, u32[]{:S(2)}) collective-permute-start(bf16[128,2176]{1,0:T(8,128)(2,1)S(1)} %copy-done.6), channel_id=1, source_target_pairs={{0,4},{2,6},{4,0},{6,2},{8,12},{10,14},{12,8},{14,10},{16,20},{18,... | collective-permute-start | bytes 1671176 | tf_op jit(solution)/shard_map/ppermute | solution.py:30
  13.5 18.1 %collective-permute-start = (bf16[128,2176]{1,0:T(8,128)(2,1)S(1)}, bf16[128,2176]{1,0:T(8,128)(2,1)}, u32[]{:S(2)}, u32[]{:S(2)}) collective-permute-start(bf16[128,2176]{1,0:T(8,128)(2,1)S(1)} %copy-done.6), channel_id=1, source_target_pairs={{0,8},{2,10},{4,12},{6,14},{8,0},{10,2},{12,4},{14,6},{16,24},{18,... | collective-permute-start | bytes 1671176 | tf_op jit(solution)/shard_map/ppermute | solution.py:30
  31.6 28.4 %collective-permute-start.19 = (bf16[1,8,288,128]{3,2,1,0:T(8,128)(2,1)S(1)}, bf16[1,8,288,128]{3,2,1,0:T(8,128)(2,1)S(1)}, u32[]{:S(2)}, u32[]{:S(2)}) collective-permute-start(bf16[1,8,288,128]{3,2,1,0:T(8,128)(2,1)S(1)} %bitcast.25), channel_id=1, source_target_pairs={{0,16},{2,18},{4,20},{6,22},{8,24},{10,26},{12,28},{14,30},{16,0},... | collective-permute-start | bytes 1769480 | tf_op jit(solution)/shard_map/ppermute | solution.py:30
  34.2 14.1 %collective-permute-start.4 = (bf16[128,2176]{1,0:T(8,128)(2,1)}, bf16[128,2176]{1,0:T(8,128)(2,1)S(1)}, u32[]{:S(2)}, u32[]{:S(2)}) collective-permute-start(bf16[128,2176]{1,0:T(8,128)(2,1)} %collective-permute-done.refs_1_), channel_id=1, source_target_pairs={{0,1},{1,0},{2,3},{3,2},{4,5},{5,4},{6,7},{7,6},{8,9},{9,8},{10,11... | collective-permute-start | bytes 1671176 | tf_op jit(solution)/shard_map/ppermute | solution.py:30
  35.6 14.2 %collective-permute-start.3 = (bf16[128,2176]{1,0:T(8,128)(2,1)}, bf16[128,2176]{1,0:T(8,128)(2,1)S(1)}, u32[]{:S(2)}, u32[]{:S(2)}) collective-permute-start(bf16[128,2176]{1,0:T(8,128)(2,1)} %collective-permute-done.refs_1_), channel_id=1, source_target_pairs={{0,4},{2,6},{4,0},{6,2},{8,12},{10,14},{12,8},{14,10},{16,20},{18,... | collective-permute-start | bytes 1671176 | tf_op jit(solution)/shard_map/ppermute | solution.py:30
  48.3 11.7 %collective-permute-start.8 = (bf16[64,2176]{1,0:T(8,128)(2,1)S(1)}, bf16[64,2176]{1,0:T(8,128)(2,1)S(1)}, u32[]{:S(2)}, u32[]{:S(2)}) collective-permute-start(bf16[64,2176]{1,0:T(8,128)(2,1)S(1)} %slice.17), channel_id=1, source_target_pairs={{0,4},{2,6},{4,0},{6,2},{8,12},{10,14},{12,8},{14,10},{16,20},{18,... | collective-permute-start | bytes 835592 | tf_op jit(solution)/shard_map/ppermute | solution.py:30
  49.9 10.6 %collective-permute-start.7 = (bf16[64,2176]{1,0:T(8,128)(2,1)S(1)}, bf16[64,2176]{1,0:T(8,128)(2,1)S(1)}, u32[]{:S(2)}, u32[]{:S(2)}) collective-permute-start(bf16[64,2176]{1,0:T(8,128)(2,1)S(1)} %slice.16), channel_id=1, source_target_pairs={{0,1},{1,0},{2,3},{3,2},{4,5},{5,4},{6,7},{7,6},{8,9},{9,8},{10,11... | collective-permute-start | bytes 835592 | tf_op jit(solution)/shard_map/ppermute | solution.py:30
  51.4 10.0 %collective-permute-start.6 = (bf16[64,2176]{1,0:T(8,128)(2,1)S(1)}, bf16[64,2176]{1,0:T(8,128)(2,1)S(1)}, u32[]{:S(2)}, u32[]{:S(2)}) collective-permute-start(bf16[64,2176]{1,0:T(8,128)(2,1)S(1)} %slice.13), channel_id=1, source_target_pairs={{0,4},{2,6},{4,0},{6,2},{8,12},{10,14},{12,8},{14,10},{16,20},{18,... | collective-permute-start | bytes 835592 | tf_op jit(solution)/shard_map/ppermute | solution.py:30
  52.1 10.5 %collective-permute-start.5 = (bf16[64,2176]{1,0:T(8,128)(2,1)S(1)}, bf16[64,2176]{1,0:T(8,128)(2,1)S(1)}, u32[]{:S(2)}, u32[]{:S(2)}) collective-permute-start(bf16[64,2176]{1,0:T(8,128)(2,1)S(1)} %slice.12), channel_id=1, source_target_pairs={{0,1},{1,0},{2,3},{3,2},{4,5},{5,4},{6,7},{7,6},{8,9},{9,8},{10,11... | collective-permute-start | bytes 835592 | tf_op jit(solution)/shard_map/ppermute | solution.py:30
  62.6 4.7 %collective-permute-start.13 = (bf16[128,2176]{1,0:T(8,128)(2,1)S(1)}, bf16[128,2176]{1,0:T(8,128)(2,1)S(1)}, u32[]{:S(2)}, u32[]{:S(2)}) collective-permute-start(bf16[128,2176]{1,0:T(8,128)(2,1)S(1)} %collective-permute-done.3.refs_4_), channel_id=1, source_target_pairs={{0,2},{2,0},{4,6},{6,4},{8,10},{10,8},{12,14},{14,12},{16,18},{18,... | collective-permute-start | bytes 1671176 | tf_op jit(solution)/shard_map/ppermute | solution.py:30
  80.2 7.3 %collective-permute-start.22 = (bf16[96,1024]{1,0:T(8,128)(2,1)}, bf16[96,1024]{1,0:T(8,128)(2,1)}, u32[]{:S(2)}, u32[]{:S(2)}) collective-permute-start(bf16[96,1024]{1,0:T(8,128)(2,1)} %get-tuple-element.53.refs_0_), channel_id=1, source_target_pairs={{0,8},{2,10},{4,12},{6,14},{8,0},{10,2},{12,4},{14,6},{16,24},{18,... | collective-permute-start | bytes 589832 | tf_op jit(solution)/shard_map/ppermute | solution.py:30
  94.8 29.6 %all-to-all-start.1 = ((bf16[16,288,128]{2,1,0:T(8,128)(2,1)}), bf16[16,288,128]{2,1,0:T(8,128)(2,1)S(1)}, u32[]{:S(2)}, u32[]{:S(2)}) async-start(bf16[16,288,128]{2,1,0:T(8,128)(2,1)} %local_tree.1), calls=%async_computation.1 | async-start | bytes 2359296 | tf_op jit(solution)/shard_map/all_to_all | solution.py:441
  99.2 17.4 %collective-permute-start.28 = (bf16[96,1024]{1,0:T(8,128)(2,1)}, bf16[96,1024]{1,0:T(8,128)(2,1)}, u32[]{:S(2)}, u32[]{:S(2)}) collective-permute-start(bf16[96,1024]{1,0:T(8,128)(2,1)} %get-tuple-element.53.refs_0_), channel_id=1, source_target_pairs={{0,4},{2,6},{4,0},{6,2},{8,12},{10,14},{12,8},{14,10},{16,20},{18,... | collective-permute-start | bytes 589832 | tf_op jit(solution)/shard_map/ppermute | solution.py:30
  101.1 19.2 %collective-permute-start.29 = (bf16[96,1024]{1,0:T(8,128)(2,1)}, bf16[96,1024]{1,0:T(8,128)(2,1)}, u32[]{:S(2)}, u32[]{:S(2)}) collective-permute-start(bf16[96,1024]{1,0:T(8,128)(2,1)} %collective-permute-done.22.refs_1_), channel_id=1, source_target_pairs={{0,4},{2,6},{4,0},{6,2},{8,12},{10,14},{12,8},{14,10},{16,20},{18,... | collective-permute-start | bytes 589832 | tf_op jit(solution)/shard_map/ppermute | solution.py:30
  101.3 45.6 %collective-permute-start.30 = (bf16[96,1024]{1,0:T(8,128)(2,1)}, bf16[96,1024]{1,0:T(8,128)(2,1)}, u32[]{:S(2)}, u32[]{:S(2)}) collective-permute-start(bf16[96,1024]{1,0:T(8,128)(2,1)} %get-tuple-element.53.refs_0_), channel_id=1, source_target_pairs={{0,2},{2,0},{4,6},{6,4},{8,10},{10,8},{12,14},{14,12},{16,18},{18,... | collective-permute-start | bytes 589832 | tf_op jit(solution)/shard_map/ppermute | solution.py:30
  101.3 45.6 %collective-permute-start.31 = (bf16[96,1024]{1,0:T(8,128)(2,1)}, bf16[96,1024]{1,0:T(8,128)(2,1)}, u32[]{:S(2)}, u32[]{:S(2)}) collective-permute-start(bf16[96,1024]{1,0:T(8,128)(2,1)} %collective-permute-done.22.refs_1_), channel_id=1, source_target_pairs={{0,2},{2,0},{4,6},{6,4},{8,10},{10,8},{12,14},{14,12},{16,18},{18,... | collective-permute-start | bytes 589832 | tf_op jit(solution)/shard_map/ppermute | solution.py:30
  116.6 30.2 %collective-permute-start.32 = (bf16[96,1024]{1,0:T(8,128)(2,1)}, bf16[96,1024]{1,0:T(8,128)(2,1)}, u32[]{:S(2)}, u32[]{:S(2)}) collective-permute-start(bf16[96,1024]{1,0:T(8,128)(2,1)} %collective-permute-done.28.refs_2_), channel_id=1, source_target_pairs={{0,2},{2,0},{4,6},{6,4},{8,10},{10,8},{12,14},{14,12},{16,18},{18,... | collective-permute-start | bytes 589832 | tf_op jit(solution)/shard_map/ppermute | solution.py:30
  120.3 26.5 %collective-permute-start.33 = (bf16[96,1024]{1,0:T(8,128)(2,1)}, bf16[96,1024]{1,0:T(8,128)(2,1)}, u32[]{:S(2)}, u32[]{:S(2)}) collective-permute-start(bf16[96,1024]{1,0:T(8,128)(2,1)} %collective-permute-done.29.refs_3_), channel_id=1, source_target_pairs={{0,2},{2,0},{4,6},{6,4},{8,10},{10,8},{12,14},{14,12},{16,18},{18,... | collective-permute-start | bytes 589832 | tf_op jit(solution)/shard_map/ppermute | solution.py:30
  130.5 5.2 %collective-permute-start.26 = (f32[6,2]{1,0:T(8,128)S(1)}, f32[6,2]{1,0:T(8,128)S(1)}, u32[]{:S(2)}, u32[]{:S(2)}) collective-permute-start(f32[6,2]{1,0:T(8,128)S(1)} %add.31), channel_id=1, source_target_pairs={{0,8},{2,10},{4,12},{6,14},{8,0},{10,2},{12,4},{14,6},{16,24},{18,... | collective-permute-start | bytes 152 | tf_op jit(solution)/shard_map/ppermute | solution.py:30
  135.7 5.1 %collective-permute-start.27 = (f32[6,2]{1,0:T(8,128)S(1)}, f32[6,2]{1,0:T(8,128)S(1)}, u32[]{:S(2)}, u32[]{:S(2)}) collective-permute-start(f32[6,2]{1,0:T(8,128)S(1)} %add.32), channel_id=1, source_target_pairs={{0,16},{2,18},{4,20},{6,22},{8,24},{10,26},{12,28},{14,30},{16,0},... | collective-permute-start | bytes 152 | tf_op jit(solution)/shard_map/ppermute | solution.py:30
  143.9 8.9 %collective-permute-start.34 = (bf16[1,128,768]{2,1,0:T(8,128)(2,1)S(1)}, bf16[1,128,768]{2,1,0:T(8,128)(2,1)S(1)}, u32[]{:S(2)}, u32[]{:S(2)}) collective-permute-start(bf16[1,128,768]{2,1,0:T(8,128)(2,1)S(1)} %bitcast.34), channel_id=1, source_target_pairs={{0,16},{2,18},{4,20},{6,22},{8,24},{10,26},{12,28},{14,30},{16,0},... | collective-permute-start | bytes 589832 | tf_op jit(solution)/shard_map/ppermute | solution.py:30
  155.9 13.4 %all-to-all-start.2 = ((bf16[16,64,256]{2,1,0:T(8,128)(2,1)}), bf16[16,64,256]{2,1,0:T(8,128)(2,1)}, u32[]{:S(2)}, u32[]{:S(2)}) async-start(bf16[16,64,256]{2,1,0:T(8,128)(2,1)} %bitcast.27), calls=%async_computation.2 | async-start | bytes 1048576 | tf_op jit(solution)/shard_map/all_to_all | solution.py:490
  (22 other events, 105.7 us)

commit v6 on v5

--- a/solution.py
+++ b/solution.py
@@ -427,7 +427,6 @@
     hidden_parts = [hidden_own]
     for bit in reversed(range(1, inner_bits)):
         hidden_parts += [swapped(piece, "dp", bit) for piece in hidden_parts]
-        gram = after(gram, hidden_parts[1]) if bit == inner_bits - 1 else gram
     gram = tree_sum(gram, range(inner_bits - 1, inner_bits))
 
     vector = call(
@@ -438,7 +437,7 @@
         name="local_tree",
         vmem=5 * rows_bytes // 4 + 2 * weight_bytes + 8 * mebi,
     )
-    got = lax.all_to_all(vector, "dp", 0, 0, tiled=True)
+    got = lax.all_to_all(after(vector, *hidden_parts[1:2]), "dp", 0, 0, tiled=True)
     hidden_parts += [swapped(piece, "dp", 0) for piece in hidden_parts]
     leaves = got.reshape(outer, group, 3, part, block_rows).transpose(2, 0, 1, 3, 4)
     leaves = leaves.reshape(3, outer, hidden_width, block_rows).astype(f32)

time: 172 us -> 170 us (0.988)
  transfers between devices with their start and end apart: 38 -> 38, of which waited for: 24 -> 23; matrix products, arithmetic and copies ran while one was open for 1% -> 1% of each run, Pallas kernels for 3% -> 5%
where the time goes in v6:
time: 170 us; the launch traced here: 169 us
  waiting for transfers between devices  85.3 us (50%)
  starting transfers between devices  49.8 us (29%)
  Pallas kernels  27.3 us (16%)
  local copies, waits for them, and re-layouts  5.48 us (3%)
    ppermute x35, waiting for transfers between devices, swapped(): lax.ppermute(array, axis, [(i, i ^ 1 << bit) for i in range(lax.axis_size...  77.1 us
    ppermute x35, starting transfers between devices, swapped(): lax.ppermute(array, axis, [(i, i ^ 1 << bit) for i in range(lax.axis_size...  36.2 us
    pallas_call x7, Pallas kernels, call(): pl.pallas_call(kernel, out_shape=outs, grid=grid, in_specs=in_specs, out_...  27.3 us
    all_to_all x1, starting transfers between devices, shards(): lax.all_to_all(sent, 'dp', 0, 0, axis_index_groups=groups, tiled=True)  5.39 us
    all_to_all x1, starting transfers between devices, shards(): lax.all_to_all(slot_outputs, ('dp', 'expert'), 0, 0, axis_index_groups=cu...  4.25 us
    all_to_all x1, waiting for transfers between devices, shards(): lax.all_to_all(slot_outputs, ('dp', 'expert'), 0, 0, axis_index_groups=cu...  4.23 us
    all_to_all x1, waiting for transfers between devices, shards(): lax.all_to_all(after(vector, *hidden_parts[1:2]), 'dp', 0, 0, tiled=True)  3.99 us
    all_to_all x1, starting transfers between devices, shards(): lax.all_to_all(after(vector, *hidden_parts[1:2]), 'dp', 0, 0, tiled=True)  3.98 us
  transfers between devices with their start and end apart: 38, of which 23 were waited for; matrix products, arithmetic and copies ran while one was open for 1% of the time, Pallas kernels for 5%

profile of v6, /device:TPU:0, one launch (start us, length us, event | category | flops | bytes accessed | tf_op | source)
XLA Modules:
  0.0 169.3 jit_solution(8220899988246241117)
XLA Ops:
  1.9 2.7 %prepare.1 = (bf16[128,2176]{1,0:T(8,128)(2,1)}, bf16[8,288,128]{2,1,0:T(8,128)(2,1)}) custom-call(s32[2,64]{1,0:T(2,128)} %reshape.35.route_ref, s32[1,2]{1,0:T(1,128)} %counts_ref.1, bf16[64,2048]{1,0:T(8,128)(2,1)} %tok_ref.1, bf16[64,2048]{1,0:T(8,128)(2,1)} %cot_ref.1, f32[128,768]{1,0:T(8,128)} %bitcast.28, f32[128,768]{1,0:T(8,128)} %bitcast.30, ...), custom_call_target="tpu_custom_call" | custom-call | tf_op jit(solution)/shard_map/prepare/pallas_call | solution.py:325
  4.6 5.4 %all-to-all-start = ((bf16[8,288,128]{2,1,0:T(8,128)(2,1)}), bf16[8,288,128]{2,1,0:T(8,128)(2,1)S(1)}, u32[]{:S(2)}, u32[]{:S(2)}) async-start(bf16[8,288,128]{2,1,0:T(8,128)(2,1)} %get-tuple-element.38), calls=%async_computation | async-start | bytes 1179648 | tf_op jit(solution)/shard_map/all_to_all | solution.py:385
  15.0 10.1 %collective-permute-done.2.refs_3_ = bf16[128,2176]{1,0:T(8,128)(2,1)S(1)} collective-permute-done((bf16[128,2176]{1,0:T(8,128)(2,1)S(1)}, bf16[128,2176]{1,0:T(8,128)(2,1)S(1)}, u32[]{:S(2)}, u32[]{:S(2)}) %collective-permute-start.2) | collective-permute-done | bytes 557088 | tf_op jit(solution)/shard_map/ppermute | solution.py:30
  25.0 6.4 %collective-permute-done.1.refs_2_ = bf16[128,2176]{1,0:T(8,128)(2,1)S(1)} collective-permute-done((bf16[128,2176]{1,0:T(8,128)(2,1)S(1)}, bf16[128,2176]{1,0:T(8,128)(2,1)S(1)}, u32[]{:S(2)}, u32[]{:S(2)}) %collective-permute-start.1) | collective-permute-done | bytes 557088 | tf_op jit(solution)/shard_map/ppermute | solution.py:30
  31.6 2.6 %collective-permute-start.19 = (bf16[1,8,288,128]{3,2,1,0:T(8,128)(2,1)S(1)}, bf16[1,8,288,128]{3,2,1,0:T(8,128)(2,1)S(1)}, u32[]{:S(2)}, u32[]{:S(2)}) collective-permute-start(bf16[1,8,288,128]{3,2,1,0:T(8,128)(2,1)S(1)} %bitcast.25), channel_id=1, source_target_pairs={{0,16},{2,18},{4,20},{6,22},{8,24},{10,26},{12,28},{14,30},{16,0},... | collective-permute-start | bytes 1769480 | tf_op jit(solution)/shard_map/ppermute | solution.py:30
  37.2 11.1 %collective-permute-done.4.refs_5_ = bf16[128,2176]{1,0:T(8,128)(2,1)S(1)} collective-permute-done((bf16[128,2176]{1,0:T(8,128)(2,1)}, bf16[128,2176]{1,0:T(8,128)(2,1)S(1)}, u32[]{:S(2)}, u32[]{:S(2)}) %collective-permute-start.4) | collective-permute-done | bytes 557088 | tf_op jit(solution)/shard_map/ppermute | solution.py:30
  53.2 6.8 %collective-permute-done.19.refs_21_ = bf16[1,8,288,128]{3,2,1,0:T(8,128)(2,1)S(1)} collective-permute-done((bf16[1,8,288,128]{3,2,1,0:T(8,128)(2,1)S(1)}, bf16[1,8,288,128]{3,2,1,0:T(8,128)(2,1)S(1)}, u32[]{:S(2)}, u32[]{:S(2)}) %collective-permute-start.19) | collective-permute-done | bytes 589856 | tf_op jit(solution)/shard_map/ppermute | solution.py:30
  68.2 12.0 %forward_and_gram.1 = (bf16[96,1024]{1,0:T(8,128)(2,1)S(1)}, bf16[96,1024]{1,0:T(8,128)(2,1)}, bf16[96,1024]{1,0:T(8,128)(2,1)S(1)}, bf16[96,1024]{1,0:T(8,128)(...) custom-call(s32[3]{0:T(128)S(1)} %pad_add_fusion.idx_ref, ...), custom_call_target="tpu_custom_call" | custom-call | tf_op jit(solution)/shard_map/forward_and_gram/pallas_call | solution.py:325
  83.4 2.6 %collective-permute-done.21 = f32[24,128]{1,0:T(8,128)S(1)} collective-permute-done((f32[24,128]{1,0:T(8,128)S(1)}, f32[24,128]{1,0:T(8,128)S(1)}, u32[]{:S(2)}, u32[]{:S(2)}) %collective-permute-start.21) | collective-permute-done | bytes 12320 | tf_op jit(solution)/shard_map/ppermute | solution.py:30
  87.1 2.7 %collective-permute-done.22 = f32[24,128]{1,0:T(8,128)S(1)} collective-permute-done((f32[24,128]{1,0:T(8,128)S(1)}, f32[24,128]{1,0:T(8,128)S(1)}, u32[]{:S(2)}, u32[]{:S(2)}) %collective-permute-start.22) | collective-permute-done | bytes 12320 | tf_op jit(solution)/shard_map/ppermute | solution.py:30
  89.8 3.6 %local_tree.1 = bf16[16,288,128]{2,1,0:T(8,128)(2,1)} custom-call(s32[3]{0:T(128)S(1)} %pad_add_fusion.idx_ref, f32[24,128]{1,0:T(8,128)S(1)} %add.29.gram_ref, bf16[1024,2048]{1,0:T(8,128)(2,1)S(1)} %get-tuple-element.53.x_ref, bf16[1024,2176]{1,0:T(8,128)(2,1)S(1)} %get-tuple-element.54.y_ref, bf16[96,1024]{1,0:T(8,128)(2,1)S(1)} %get-tuple-element.55.dgate_ref, ...), custom_call_target="tpu_custom_call" | custom-call | tf_op jit(solution)/shard_map/local_tree/pallas_call | solution.py:325
  93.4 4.0 %all-to-all-start.1 = ((bf16[16,288,128]{2,1,0:T(8,128)(2,1)}), bf16[16,288,128]{2,1,0:T(8,128)(2,1)S(1)}, u32[]{:S(2)}, u32[]{:S(2)}) async-start(bf16[16,288,128]{2,1,0:T(8,128)(2,1)} %local_tree.1), calls=%async_computation.1 | async-start | bytes 2359296 | tf_op jit(solution)/shard_map/all_to_all | solution.py:440
  100.0 14.8 %collective-permute-done.28.refs_2_ = bf16[96,1024]{1,0:T(8,128)(2,1)} collective-permute-done((bf16[96,1024]{1,0:T(8,128)(2,1)}, bf16[96,1024]{1,0:T(8,128)(2,1)}, u32[]{:S(2)}, u32[]{:S(2)}) %collective-permute-start.28) | collective-permute-done | bytes 196640 | tf_op jit(solution)/shard_map/ppermute | solution.py:30
  114.8 3.7 %collective-permute-done.29.refs_3_ = bf16[96,1024]{1,0:T(8,128)(2,1)} collective-permute-done((bf16[96,1024]{1,0:T(8,128)(2,1)}, bf16[96,1024]{1,0:T(8,128)(2,1)}, u32[]{:S(2)}, u32[]{:S(2)}) %collective-permute-start.29) | collective-permute-done | bytes 196640 | tf_op jit(solution)/shard_map/ppermute | solution.py:30
  118.5 4.0 %all-to-all-done.1.got_ref = bf16[16,288,128]{2,1,0:T(8,128)(2,1)S(1)} async-done(((bf16[16,288,128]{2,1,0:T(8,128)(2,1)}), bf16[16,288,128]{2,1,0:T(8,128)(2,1)S(1)}, u32[]{:S(2)}, u32[]{:S(2)}) %all-to-all-start.1) | async-done | bytes 1179680 | tf_op jit(solution)/shard_map/all_to_all | solution.py:440
  125.0 2.1 %collective-permute-start.25 = (f32[6,2]{1,0:T(8,128)S(1)}, f32[6,2]{1,0:T(8,128)S(1)}, u32[]{:S(2)}, u32[]{:S(2)}) collective-permute-start(f32[6,2]{1,0:T(8,128)S(1)} %add.30), channel_id=1, source_target_pairs={{0,4},{2,6},{4,0},{6,2},{8,12},{10,14},{12,8},{14,10},{16,20},{18,... | collective-permute-start | bytes 152 | tf_op jit(solution)/shard_map/ppermute | solution.py:30
  128.7 3.6 %collective-permute-start.26 = (f32[6,2]{1,0:T(8,128)S(1)}, f32[6,2]{1,0:T(8,128)S(1)}, u32[]{:S(2)}, u32[]{:S(2)}) collective-permute-start(f32[6,2]{1,0:T(8,128)S(1)} %add.31), channel_id=1, source_target_pairs={{0,8},{2,10},{4,12},{6,14},{8,0},{10,2},{12,4},{14,6},{16,24},{18,... | collective-permute-start | bytes 152 | tf_op jit(solution)/shard_map/ppermute | solution.py:30
  133.9 3.6 %collective-permute-start.27 = (f32[6,2]{1,0:T(8,128)S(1)}, f32[6,2]{1,0:T(8,128)S(1)}, u32[]{:S(2)}, u32[]{:S(2)}) collective-permute-start(f32[6,2]{1,0:T(8,128)S(1)} %add.32), channel_id=1, source_target_pairs={{0,16},{2,18},{4,20},{6,22},{8,24},{10,26},{12,28},{14,30},{16,0},... | collective-permute-start | bytes 152 | tf_op jit(solution)/shard_map/ppermute | solution.py:30
  142.1 2.9 %collective-permute-start.34 = (bf16[1,128,768]{2,1,0:T(8,128)(2,1)S(1)}, bf16[1,128,768]{2,1,0:T(8,128)(2,1)S(1)}, u32[]{:S(2)}, u32[]{:S(2)}) collective-permute-start(bf16[1,128,768]{2,1,0:T(8,128)(2,1)S(1)} %bitcast.34), channel_id=1, source_target_pairs={{0,16},{2,18},{4,20},{6,22},{8,24},{10,26},{12,28},{14,30},{16,0},... | collective-permute-start | bytes 589832 | tf_op jit(solution)/shard_map/ppermute | solution.py:30
  145.0 6.0 %collective-permute-done.34.refs_9_ = bf16[1,128,768]{2,1,0:T(8,128)(2,1)S(1)} collective-permute-done((bf16[1,128,768]{2,1,0:T(8,128)(2,1)S(1)}, bf16[1,128,768]{2,1,0:T(8,128)(2,1)S(1)}, u32[]{:S(2)}, u32[]{:S(2)}) %collective-permute-start.34) | collective-permute-done | bytes 196640 | tf_op jit(solution)/shard_map/ppermute | solution.py:30
  151.0 2.2 %project.1 = bf16[8,2,64,256]{3,2,1,0:T(8,128)(2,1)S(1)} custom-call(s32[3]{0:T(128)S(1)} %pad_add_fusion.idx_ref, bf16[96,1024]{1,0:T(8,128)(2,1)} %get-tuple-element.58.refs_0_, bf16[96,1024]{1,0:T(8,128)(2,1)} %collective-permute-done.23.refs_1_, bf16[96,1024]{1,0:T(8,128)(2,1)} %collective-permute-done.28.refs_2_, ...), custom_call_target="tpu_custom_call" | custom-call | tf_op jit(solution)/shard_map/project/pallas_call | solution.py:325
  154.1 4.2 %all-to-all-start.2 = ((bf16[16,64,256]{2,1,0:T(8,128)(2,1)}), bf16[16,64,256]{2,1,0:T(8,128)(2,1)}, u32[]{:S(2)}, u32[]{:S(2)}) async-start(bf16[16,64,256]{2,1,0:T(8,128)(2,1)} %bitcast.27), calls=%async_computation.2 | async-start | bytes 1048576 | tf_op jit(solution)/shard_map/all_to_all | solution.py:489
  160.3 2.9 %update.3 = (f32[3,128,768]{2,1,0:T(8,128)}, f32[3,128,768]{2,1,0:T(8,128)}, f32[3,128,768]{2,1,0:T(8,128)}, f32[3,128,768]{2,1,0:T(8,128)}) custom-call(f32[6,2]{1,0:T(8,128)S(1)} %add.33.gram_ref, bf16[16,288,128]{2,1,0:T(8,128)(2,1)S(1)} %all-to-all-done.1.got_ref, ...), custom_call_target="tpu_custom_call", output_to_operand_aliasing={{0}: (6, {}), {1}: (7, {}), {2}: (8, {}), {3}: (9, {})} | custom-call | tf_op jit(solution)/shard_map/update/pallas_call | solution.py:325
  163.3 4.2 %all-to-all-done.2.got_ref = bf16[16,64,256]{2,1,0:T(8,128)(2,1)} async-done(((bf16[16,64,256]{2,1,0:T(8,128)(2,1)}), bf16[16,64,256]{2,1,0:T(8,128)(2,1)}, u32[]{:S(2)}, u32[]{:S(2)}) %all-to-all-start.2) | async-done | bytes 524320 | tf_op jit(solution)/shard_map/all_to_all | solution.py:489
  (91 shorter events, 44.2 us)
Async XLA Ops:
  4.6 27.0 %all-to-all-start = ((bf16[8,288,128]{2,1,0:T(8,128)(2,1)}), bf16[8,288,128]{2,1,0:T(8,128)(2,1)S(1)}, u32[]{:S(2)}, u32[]{:S(2)}) async-start(bf16[8,288,128]{2,1,0:T(8,128)(2,1)} %get-tuple-element.38), calls=%async_computation | async-start | bytes 1179648 | tf_op jit(solution)/shard_map/all_to_all | solution.py:385
  10.0 15.0 %collective-permute-start.2 = (bf16[128,2176]{1,0:T(8,128)(2,1)S(1)}, bf16[128,2176]{1,0:T(8,128)(2,1)S(1)}, u32[]{:S(2)}, u32[]{:S(2)}) collective-permute-start(bf16[128,2176]{1,0:T(8,128)(2,1)S(1)} %copy-done.6), channel_id=1, source_target_pairs={{0,1},{1,0},{2,3},{3,2},{4,5},{5,4},{6,7},{7,6},{8,9},{9,8},{10,11... | collective-permute-start | bytes 1671176 | tf_op jit(solution)/shard_map/ppermute | solution.py:30
  11.5 19.9 %collective-permute-start.1 = (bf16[128,2176]{1,0:T(8,128)(2,1)S(1)}, bf16[128,2176]{1,0:T(8,128)(2,1)S(1)}, u32[]{:S(2)}, u32[]{:S(2)}) collective-permute-start(bf16[128,2176]{1,0:T(8,128)(2,1)S(1)} %copy-done.6), channel_id=1, source_target_pairs={{0,4},{2,6},{4,0},{6,2},{8,12},{10,14},{12,8},{14,10},{16,20},{18,... | collective-permute-start | bytes 1671176 | tf_op jit(solution)/shard_map/ppermute | solution.py:30
  13.5 18.1 %collective-permute-start = (bf16[128,2176]{1,0:T(8,128)(2,1)S(1)}, bf16[128,2176]{1,0:T(8,128)(2,1)}, u32[]{:S(2)}, u32[]{:S(2)}) collective-permute-start(bf16[128,2176]{1,0:T(8,128)(2,1)S(1)} %copy-done.6), channel_id=1, source_target_pairs={{0,8},{2,10},{4,12},{6,14},{8,0},{10,2},{12,4},{14,6},{16,24},{18,... | collective-permute-start | bytes 1671176 | tf_op jit(solution)/shard_map/ppermute | solution.py:30
  31.6 28.4 %collective-permute-start.19 = (bf16[1,8,288,128]{3,2,1,0:T(8,128)(2,1)S(1)}, bf16[1,8,288,128]{3,2,1,0:T(8,128)(2,1)S(1)}, u32[]{:S(2)}, u32[]{:S(2)}) collective-permute-start(bf16[1,8,288,128]{3,2,1,0:T(8,128)(2,1)S(1)} %bitcast.25), channel_id=1, source_target_pairs={{0,16},{2,18},{4,20},{6,22},{8,24},{10,26},{12,28},{14,30},{16,0},... | collective-permute-start | bytes 1769480 | tf_op jit(solution)/shard_map/ppermute | solution.py:30
  34.2 14.1 %collective-permute-start.4 = (bf16[128,2176]{1,0:T(8,128)(2,1)}, bf16[128,2176]{1,0:T(8,128)(2,1)S(1)}, u32[]{:S(2)}, u32[]{:S(2)}) collective-permute-start(bf16[128,2176]{1,0:T(8,128)(2,1)} %collective-permute-done.refs_1_), channel_id=1, source_target_pairs={{0,1},{1,0},{2,3},{3,2},{4,5},{5,4},{6,7},{7,6},{8,9},{9,8},{10,11... | collective-permute-start | bytes 1671176 | tf_op jit(solution)/shard_map/ppermute | solution.py:30
  35.6 14.2 %collective-permute-start.3 = (bf16[128,2176]{1,0:T(8,128)(2,1)}, bf16[128,2176]{1,0:T(8,128)(2,1)S(1)}, u32[]{:S(2)}, u32[]{:S(2)}) collective-permute-start(bf16[128,2176]{1,0:T(8,128)(2,1)} %collective-permute-done.refs_1_), channel_id=1, source_target_pairs={{0,4},{2,6},{4,0},{6,2},{8,12},{10,14},{12,8},{14,10},{16,20},{18,... | collective-permute-start | bytes 1671176 | tf_op jit(solution)/shard_map/ppermute | solution.py:30
  48.3 11.7 %collective-permute-start.8 = (bf16[64,2176]{1,0:T(8,128)(2,1)S(1)}, bf16[64,2176]{1,0:T(8,128)(2,1)S(1)}, u32[]{:S(2)}, u32[]{:S(2)}) collective-permute-start(bf16[64,2176]{1,0:T(8,128)(2,1)S(1)} %slice.17), channel_id=1, source_target_pairs={{0,4},{2,6},{4,0},{6,2},{8,12},{10,14},{12,8},{14,10},{16,20},{18,... | collective-permute-start | bytes 835592 | tf_op jit(solution)/shard_map/ppermute | solution.py:30
  49.9 10.6 %collective-permute-start.7 = (bf16[64,2176]{1,0:T(8,128)(2,1)S(1)}, bf16[64,2176]{1,0:T(8,128)(2,1)S(1)}, u32[]{:S(2)}, u32[]{:S(2)}) collective-permute-start(bf16[64,2176]{1,0:T(8,128)(2,1)S(1)} %slice.16), channel_id=1, source_target_pairs={{0,1},{1,0},{2,3},{3,2},{4,5},{5,4},{6,7},{7,6},{8,9},{9,8},{10,11... | collective-permute-start | bytes 835592 | tf_op jit(solution)/shard_map/ppermute | solution.py:30
  51.4 10.0 %collective-permute-start.6 = (bf16[64,2176]{1,0:T(8,128)(2,1)S(1)}, bf16[64,2176]{1,0:T(8,128)(2,1)S(1)}, u32[]{:S(2)}, u32[]{:S(2)}) collective-permute-start(bf16[64,2176]{1,0:T(8,128)(2,1)S(1)} %slice.13), channel_id=1, source_target_pairs={{0,4},{2,6},{4,0},{6,2},{8,12},{10,14},{12,8},{14,10},{16,20},{18,... | collective-permute-start | bytes 835592 | tf_op jit(solution)/shard_map/ppermute | solution.py:30
  52.1 10.5 %collective-permute-start.5 = (bf16[64,2176]{1,0:T(8,128)(2,1)S(1)}, bf16[64,2176]{1,0:T(8,128)(2,1)S(1)}, u32[]{:S(2)}, u32[]{:S(2)}) collective-permute-start(bf16[64,2176]{1,0:T(8,128)(2,1)S(1)} %slice.12), channel_id=1, source_target_pairs={{0,1},{1,0},{2,3},{3,2},{4,5},{5,4},{6,7},{7,6},{8,9},{9,8},{10,11... | collective-permute-start | bytes 835592 | tf_op jit(solution)/shard_map/ppermute | solution.py:30
  62.6 4.7 %collective-permute-start.13 = (bf16[128,2176]{1,0:T(8,128)(2,1)S(1)}, bf16[128,2176]{1,0:T(8,128)(2,1)S(1)}, u32[]{:S(2)}, u32[]{:S(2)}) collective-permute-start(bf16[128,2176]{1,0:T(8,128)(2,1)S(1)} %collective-permute-done.3.refs_4_), channel_id=1, source_target_pairs={{0,2},{2,0},{4,6},{6,4},{8,10},{10,8},{12,14},{14,12},{16,18},{18,... | collective-permute-start | bytes 1671176 | tf_op jit(solution)/shard_map/ppermute | solution.py:30
  80.2 13.2 %collective-permute-start.23 = (bf16[96,1024]{1,0:T(8,128)(2,1)}, bf16[96,1024]{1,0:T(8,128)(2,1)}, u32[]{:S(2)}, u32[]{:S(2)}) collective-permute-start(bf16[96,1024]{1,0:T(8,128)(2,1)} %get-tuple-element.58.refs_0_), channel_id=1, source_target_pairs={{0,8},{2,10},{4,12},{6,14},{8,0},{10,2},{12,4},{14,6},{16,24},{18,... | collective-permute-start | bytes 589832 | tf_op jit(solution)/shard_map/ppermute | solution.py:30
  93.4 29.1 %all-to-all-start.1 = ((bf16[16,288,128]{2,1,0:T(8,128)(2,1)}), bf16[16,288,128]{2,1,0:T(8,128)(2,1)S(1)}, u32[]{:S(2)}, u32[]{:S(2)}) async-start(bf16[16,288,128]{2,1,0:T(8,128)(2,1)} %local_tree.1), calls=%async_computation.1 | async-start | bytes 2359296 | tf_op jit(solution)/shard_map/all_to_all | solution.py:440
  97.4 17.4 %collective-permute-start.28 = (bf16[96,1024]{1,0:T(8,128)(2,1)}, bf16[96,1024]{1,0:T(8,128)(2,1)}, u32[]{:S(2)}, u32[]{:S(2)}) collective-permute-start(bf16[96,1024]{1,0:T(8,128)(2,1)} %get-tuple-element.58.refs_0_), channel_id=1, source_target_pairs={{0,4},{2,6},{4,0},{6,2},{8,12},{10,14},{12,8},{14,10},{16,20},{18,... | collective-permute-start | bytes 589832 | tf_op jit(solution)/shard_map/ppermute | solution.py:30
  99.3 19.2 %collective-permute-start.29 = (bf16[96,1024]{1,0:T(8,128)(2,1)}, bf16[96,1024]{1,0:T(8,128)(2,1)}, u32[]{:S(2)}, u32[]{:S(2)}) collective-permute-start(bf16[96,1024]{1,0:T(8,128)(2,1)} %collective-permute-done.23.refs_1_), channel_id=1, source_target_pairs={{0,4},{2,6},{4,0},{6,2},{8,12},{10,14},{12,8},{14,10},{16,20},{18,... | collective-permute-start | bytes 589832 | tf_op jit(solution)/shard_map/ppermute | solution.py:30
  99.5 45.6 %collective-permute-start.30 = (bf16[96,1024]{1,0:T(8,128)(2,1)}, bf16[96,1024]{1,0:T(8,128)(2,1)}, u32[]{:S(2)}, u32[]{:S(2)}) collective-permute-start(bf16[96,1024]{1,0:T(8,128)(2,1)} %get-tuple-element.58.refs_0_), channel_id=1, source_target_pairs={{0,2},{2,0},{4,6},{6,4},{8,10},{10,8},{12,14},{14,12},{16,18},{18,... | collective-permute-start | bytes 589832 | tf_op jit(solution)/shard_map/ppermute | solution.py:30
  99.5 45.6 %collective-permute-start.31 = (bf16[96,1024]{1,0:T(8,128)(2,1)}, bf16[96,1024]{1,0:T(8,128)(2,1)}, u32[]{:S(2)}, u32[]{:S(2)}) collective-permute-start(bf16[96,1024]{1,0:T(8,128)(2,1)} %collective-permute-done.23.refs_1_), channel_id=1, source_target_pairs={{0,2},{2,0},{4,6},{6,4},{8,10},{10,8},{12,14},{14,12},{16,18},{18,... | collective-permute-start | bytes 589832 | tf_op jit(solution)/shard_map/ppermute | solution.py:30
  114.8 30.2 %collective-permute-start.32 = (bf16[96,1024]{1,0:T(8,128)(2,1)}, bf16[96,1024]{1,0:T(8,128)(2,1)}, u32[]{:S(2)}, u32[]{:S(2)}) collective-permute-start(bf16[96,1024]{1,0:T(8,128)(2,1)} %collective-permute-done.28.refs_2_), channel_id=1, source_target_pairs={{0,2},{2,0},{4,6},{6,4},{8,10},{10,8},{12,14},{14,12},{16,18},{18,... | collective-permute-start | bytes 589832 | tf_op jit(solution)/shard_map/ppermute | solution.py:30
  118.5 26.5 %collective-permute-start.33 = (bf16[96,1024]{1,0:T(8,128)(2,1)}, bf16[96,1024]{1,0:T(8,128)(2,1)}, u32[]{:S(2)}, u32[]{:S(2)}) collective-permute-start(bf16[96,1024]{1,0:T(8,128)(2,1)} %collective-permute-done.29.refs_3_), channel_id=1, source_target_pairs={{0,2},{2,0},{4,6},{6,4},{8,10},{10,8},{12,14},{14,12},{16,18},{18,... | collective-permute-start | bytes 589832 | tf_op jit(solution)/shard_map/ppermute | solution.py:30
  128.7 5.2 %collective-permute-start.26 = (f32[6,2]{1,0:T(8,128)S(1)}, f32[6,2]{1,0:T(8,128)S(1)}, u32[]{:S(2)}, u32[]{:S(2)}) collective-permute-start(f32[6,2]{1,0:T(8,128)S(1)} %add.31), channel_id=1, source_target_pairs={{0,8},{2,10},{4,12},{6,14},{8,0},{10,2},{12,4},{14,6},{16,24},{18,... | collective-permute-start | bytes 152 | tf_op jit(solution)/shard_map/ppermute | solution.py:30
  133.9 5.1 %collective-permute-start.27 = (f32[6,2]{1,0:T(8,128)S(1)}, f32[6,2]{1,0:T(8,128)S(1)}, u32[]{:S(2)}, u32[]{:S(2)}) collective-permute-start(f32[6,2]{1,0:T(8,128)S(1)} %add.32), channel_id=1, source_target_pairs={{0,16},{2,18},{4,20},{6,22},{8,24},{10,26},{12,28},{14,30},{16,0},... | collective-permute-start | bytes 152 | tf_op jit(solution)/shard_map/ppermute | solution.py:30
  142.1 8.9 %collective-permute-start.34 = (bf16[1,128,768]{2,1,0:T(8,128)(2,1)S(1)}, bf16[1,128,768]{2,1,0:T(8,128)(2,1)S(1)}, u32[]{:S(2)}, u32[]{:S(2)}) collective-permute-start(bf16[1,128,768]{2,1,0:T(8,128)(2,1)S(1)} %bitcast.34), channel_id=1, source_target_pairs={{0,16},{2,18},{4,20},{6,22},{8,24},{10,26},{12,28},{14,30},{16,0},... | collective-permute-start | bytes 589832 | tf_op jit(solution)/shard_map/ppermute | solution.py:30
  154.1 13.4 %all-to-all-start.2 = ((bf16[16,64,256]{2,1,0:T(8,128)(2,1)}), bf16[16,64,256]{2,1,0:T(8,128)(2,1)}, u32[]{:S(2)}, u32[]{:S(2)}) async-start(bf16[16,64,256]{2,1,0:T(8,128)(2,1)} %bitcast.27), calls=%async_computation.2 | async-start | bytes 1048576 | tf_op jit(solution)/shard_map/all_to_all | solution.py:489
  (22 other events, 105.7 us)
